TPU v7x, 32 devices: a whole 2x2x4 slice. The times are simulated.
32 devices in a mesh: seq: 8 (over z, x), wt: 4 (over y, core).
Axes of the slice: x: 2, y: 2, z: 4, core: 2. Of those that a mesh axis runs over, the one named last changes fastest.
Arguments:
- tokens: bfloat16 [4, 4096, 1536], P('wt', 'seq'), may hold values from -6 to 6
- teacher: bfloat16 [4, 4096, 1536], P('wt', 'seq'), may hold values from -6 to 6
- seq_lengths: int32 [4, 1], P('wt'), may hold values from 1024 to 4096, as said below
- w_attn: bfloat16 [1536, 1792], P('wt'), may hold values from -0.15625 to 0.15625
- w_out: bfloat16 [1536, 1536], P('wt'), may hold values from -1.25 to 1.25
- w_in: bfloat16 [1536, 2, 4608], P(None, None, 'wt'), may hold values from -0.15625 to 0.15625
- w_down: bfloat16 [4608, 1536], P('wt'), may hold values from -0.09375 to 0.09375
- gain_attn: float32 [1536], replicated, may hold values from 0.25 to 1.75
- gain_ffn: float32 [1536], replicated, may hold values from 0.25 to 1.75
Outputs:
- block_out: bfloat16 [4, 4096, 1536], P('wt', 'seq')
- loss: float32 [], replicated
- input_grad: float32 [4, 4096, 1536], P('wt', 'seq')
- grad_queries: float32 [1536, 1536], P('wt', 'seq')
- grad_keyvals: float32 [1536, 2, 128], P('wt', None, 'seq')
- grad_out: float32 [1536, 1536], P('wt', 'seq')
- grad_in: float32 [1536, 2, 4608], P('seq', None, 'wt')
- grad_down: float32 [4608, 1536], P('wt', 'seq')
- grad_gain_attn: float32 [1536], replicated
- grad_gain_ffn: float32 [1536], replicated
Inputs may be any that keep to these rules, and one draw needn't show every extreme that they name: `seq_lengths`: each stream packs its sequences from position 0 on; the positions after their sum are padding, fewer than 512 of them.
All inputs are finite; a program needn't handle non-finite values.
Results may differ from a plain program's by a relative error of at most 0.012.
Values may be sent and summed in bfloat16 or wider, within the bound.
A program may use at most 320 MiB of HBM per device.

v0:
```python
import math

import jax
import jax.numpy as jnp
from jax import lax
from jax.sharding import PartitionSpec as P

HEADS = 12
HD = 128
WINDOW = 1024
QBLK = 512


EPSILON = 1e-06
NEGATIVE = -1e30


def passed_along(block, axis, distance):
    devices = range(lax.axis_size(axis))
    route = [(i - distance, i) for i in devices if i - distance in devices]
    return lax.ppermute(block, axis, route)


def rms_scale(values, gain):
    return values * lax.rsqrt(jnp.mean(values * values, axis=-1, keepdims=True) + EPSILON) * gain


def stream_ids(positions, lengths, stream_len):
    seq_ends = jnp.cumsum(lengths)
    seq_starts = seq_ends - lengths
    inside = (positions >= 0) & (positions < seq_ends[-1])
    number = jnp.sum((positions[:, None] >= seq_starts[None, :]).astype(jnp.int32), axis=1) - 1
    return jnp.where(inside, number, -(positions + 2 * stream_len))


def window_mask(query_ids, key_ids):
    query_pos = lax.broadcasted_iota(jnp.int32, (QBLK, WINDOW + QBLK), 0)
    key_pos = lax.broadcasted_iota(jnp.int32, (QBLK, WINDOW + QBLK), 1)
    offset = key_pos - WINDOW - query_pos
    return (offset <= 0) & (offset > -WINDOW) & (query_ids[:, None] == key_ids[None, :])


def gated_act(gate_up):
    return jax.nn.gelu(gate_up[:, 0, :]) * gate_up[:, 1, :]


def per_device(tokens, teacher, seq_lengths, w_attn, w_out, w_in, w_down, gain_attn, gain_ffn):
    tok_rows = tokens.shape[1]
    model_width = tokens.shape[2]
    seq_devices = lax.axis_size("seq")
    seq_place = lax.axis_index("seq")
    stream_len = tok_rows * seq_devices
    all_slots = stream_len * lax.axis_size("wt")
    reach_count = (WINDOW + tok_rows - 1) // tok_rows
    edge_rows = reach_count * tok_rows
    scale = 1.0 / math.sqrt(HD)
    inputs = tokens[0].astype(jnp.float32)
    target = teacher[0].astype(jnp.float32)
    positions = seq_place * tok_rows - edge_rows + jnp.arange(edge_rows + tok_rows, dtype=jnp.int32)
    seq_ids = stream_ids(positions, seq_lengths[0], stream_len)
    valid = (seq_ids[edge_rows:] >= 0).astype(jnp.float32)
    valid_total = lax.psum(jnp.sum(valid), ("seq", "wt"))
    attn_full, out_full = (
        lax.all_gather(w_attn, "wt", axis=0, tiled=True),
        lax.all_gather(w_out, "wt", axis=0, tiled=True),
    )
    normed_f, norm_one_pull = jax.vjp(rms_scale, inputs, gain_attn)
    normed = normed_f.astype(jnp.bfloat16)
    qkv = jnp.dot(normed, attn_full, preferred_element_type=jnp.float32).astype(jnp.bfloat16)
    queries = qkv[:, :model_width].reshape(tok_rows, HEADS, HD)
    key_value = qkv[:, model_width:]
    earlier = [passed_along(key_value, "seq", back_step) for back_step in range(reach_count, 0, -1)]
    extended = jnp.concatenate(earlier + [key_value], axis=0)
    block_count = tok_rows // QBLK

    def block_scores(block):
        start = block * QBLK
        query_ids = lax.dynamic_slice_in_dim(seq_ids, start + edge_rows, QBLK)
        raw = jnp.einsum(
            "qhe,ke->hqk", queries, extended[:, :HD], preferred_element_type=jnp.float32
        )
        allowed = window_mask(query_ids, seq_ids)
        masked = jnp.where(allowed[None], raw * scale, NEGATIVE)
        return (queries, extended, masked)

    def forward_block(block):
        q_blk, window, masked = block_scores(block)
        top = jnp.max(masked, axis=-1, keepdims=True)
        log_total = top + jnp.log(jnp.sum(jnp.exp(masked - top), axis=-1, keepdims=True))
        weights = jnp.exp(masked - log_total).astype(jnp.bfloat16)
        mixed = jnp.einsum(
            "hqk,ke->qhe", weights, window[:, HD:], preferred_element_type=jnp.float32
        )
        return (mixed, log_total)

    mixed_blocks, log_totals = lax.map(forward_block, jnp.arange(block_count, dtype=jnp.int32))
    mixed_b = mixed_blocks.reshape(tok_rows, model_width).astype(jnp.bfloat16)
    middle = inputs + jnp.dot(mixed_b, out_full, preferred_element_type=jnp.float32)
    normed_two_f, norm_two_pull = jax.vjp(rms_scale, middle, gain_ffn)
    normed_two = normed_two_f.astype(jnp.bfloat16)
    in_full, down_full = (
        lax.all_gather(w_in, "wt", axis=2, tiled=True),
        lax.all_gather(w_down, "wt", axis=0, tiled=True),
    )
    gate_up = jnp.einsum("td,dgf->tgf", normed_two, in_full, preferred_element_type=jnp.float32)
    hidden_f, act_pull = jax.vjp(gated_act, gate_up)
    hidden = hidden_f.astype(jnp.bfloat16)
    ffn_part = jnp.dot(hidden, down_full, preferred_element_type=jnp.float32)
    output = middle + ffn_part
    diff = output - target
    masked_diff = valid[:, None] * diff
    squares = jnp.sum(masked_diff * diff)
    cotangent = masked_diff * (all_slots / valid_total)
    cot_low = cotangent.astype(jnp.bfloat16)
    grad_down = jnp.einsum("tf,td->fd", hidden, cot_low, preferred_element_type=jnp.float32)
    grad_hidden = jnp.einsum("td,fd->tf", cot_low, down_full, preferred_element_type=jnp.float32)
    grad_gu = act_pull(grad_hidden)[0].astype(jnp.bfloat16)
    grad_in = jnp.einsum("td,tgf->dgf", normed_two, grad_gu, preferred_element_type=jnp.float32)
    grad_norm_two = jnp.einsum("tgf,dgf->td", grad_gu, in_full, preferred_element_type=jnp.float32)
    grad_middle_norm, grad_gain_ffn = norm_two_pull(grad_norm_two)
    grad_middle = cotangent + grad_middle_norm
    grad_mid_low = grad_middle.astype(jnp.bfloat16)
    grad_out = jnp.einsum("td,te->de", mixed_b, grad_mid_low, preferred_element_type=jnp.float32)
    grad_mixed = jnp.einsum("te,de->td", grad_mid_low, out_full, preferred_element_type=jnp.float32)
    grad_mixed = grad_mixed.astype(jnp.bfloat16).reshape(tok_rows, HEADS, HD)

    def backward_block(grad_ext, block):
        q_blk, window, masked = block_scores(block)
        log_total = lax.dynamic_index_in_dim(log_totals, block, 0, keepdims=False)
        probs = jnp.exp(masked - log_total)
        weights = probs.astype(jnp.bfloat16)
        grad_weights = jnp.einsum(
            "qhe,ke->hqk", grad_mixed, window[:, HD:], preferred_element_type=jnp.float32
        )
        grad_scores = probs * (grad_weights - jnp.sum(probs * grad_weights, axis=-1, keepdims=True))
        grad_scores_low = grad_scores.astype(jnp.bfloat16)
        grad_query = (
            jnp.einsum(
                "hqk,ke->qhe", grad_scores_low, window[:, :HD], preferred_element_type=jnp.float32
            )
            * scale
        )
        grad_key = (
            jnp.einsum("hqk,qhe->ke", grad_scores_low, q_blk, preferred_element_type=jnp.float32)
            * scale
        )
        grad_value = jnp.einsum(
            "hqk,qhe->ke", weights, grad_mixed, preferred_element_type=jnp.float32
        )
        updated = grad_ext + jnp.concatenate([grad_key, grad_value], axis=1)
        return (updated, grad_query)

    grad_ext, grad_query_blocks = lax.scan(
        backward_block,
        jnp.zeros((edge_rows + tok_rows, 2 * HD), jnp.float32),
        jnp.arange(block_count, dtype=jnp.int32),
    )
    grad_kv = grad_ext[edge_rows:]
    for back_step in range(1, reach_count + 1):
        slab_rows = grad_ext[
            edge_rows - back_step * tok_rows : edge_rows - (back_step - 1) * tok_rows
        ]
        grad_kv = grad_kv + passed_along(slab_rows, "seq", -back_step)
    grad_qkv = jnp.concatenate(
        [grad_query_blocks.reshape(tok_rows, model_width), grad_kv], axis=1
    ).astype(jnp.bfloat16)
    grad_attn = jnp.einsum("td,te->de", normed, grad_qkv, preferred_element_type=jnp.float32)
    grad_normed = jnp.einsum("te,de->td", grad_qkv, attn_full, preferred_element_type=jnp.float32)
    grad_input_norm, grad_gain_attn = norm_one_pull(grad_normed)
    grad_inputs = grad_middle + grad_input_norm
    grad_queries = grad_attn[:, :model_width]
    grad_keyvals = grad_attn[:, model_width:].reshape(grad_attn.shape[0], 2, HD)
    grad_queries, grad_keyvals, grad_out, grad_in, grad_down = (
        lax.psum_scatter(grad_queries, "wt", scatter_dimension=0, tiled=True),
        lax.psum_scatter(grad_keyvals, "wt", scatter_dimension=0, tiled=True),
        lax.psum_scatter(grad_out, "wt", scatter_dimension=0, tiled=True),
        lax.psum_scatter(grad_in, "wt", scatter_dimension=2, tiled=True),
        lax.psum_scatter(grad_down, "wt", scatter_dimension=0, tiled=True),
    )
    grad_queries, grad_keyvals, grad_out, grad_in, grad_down = (
        lax.psum_scatter(grad_queries, "seq", scatter_dimension=1, tiled=True),
        lax.psum_scatter(grad_keyvals, "seq", scatter_dimension=2, tiled=True),
        lax.psum_scatter(grad_out, "seq", scatter_dimension=1, tiled=True),
        lax.psum_scatter(grad_in, "seq", scatter_dimension=0, tiled=True),
        lax.psum_scatter(grad_down, "seq", scatter_dimension=1, tiled=True),
    )
    squares_all, gain_attn_all, gain_ffn_all = lax.psum(
        (squares, grad_gain_attn, grad_gain_ffn), ("seq", "wt")
    )
    loss = squares_all / (valid_total * model_width)
    return (
        output.astype(jnp.bfloat16)[None],
        loss,
        grad_inputs[None],
        grad_queries,
        grad_keyvals,
        grad_out,
        grad_in,
        grad_down,
        gain_attn_all,
        gain_ffn_all,
    )


def solution(mesh):
    in_specs = (
        P("wt", "seq", None),
        P("wt", "seq", None),
        P("wt", None),
        P("wt", None),
        P("wt", None),
        P(None, None, "wt"),
        P("wt", None),
        P(),
        P(),
    )
    out_specs = (
        P("wt", "seq", None),
        P(),
        P("wt", "seq", None),
        P("wt", "seq"),
        P("wt", None, "seq"),
        P("wt", "seq"),
        P("seq", None, "wt"),
        P("wt", "seq"),
        P(),
        P(),
    )
    return jax.shard_map(
        per_device, mesh=mesh, in_specs=in_specs, out_specs=out_specs, check_vma=False
    )
```

profile of v0, /device:TPU:11, one launch (start us, length us, event | category | flops | bytes accessed | tf_op | source)
XLA Modules:
  0.0 1789.7 jit_solution(7784154034411583397)
XLA Ops:
  18.4 34.7 %all-gather.5.cloned.1.call-done = bf16[1536,1792]{1,0:T(8,128)(2,1)} async-done(((bf16[384,1792]{1,0:T(8,128)(2,1)}), bf16[1536,1792]{1,0:T(8,128)(2,1)}) %all-gather.5.cloned.1.call-update) | async-done | bytes 5505040 | tf_op jit(solution)/shard_map/all_gather | solution.py:64
  67.0 39.9 %psum.29 = f32[]{:T(128)} all-reduce(f32[]{:T(128)} %fusion.62), channel_id=1, replica_groups=mesh['seq'=8,'wt'=4] {'seq','wt'}, use_global_device_ids=true, to_apply=%region_7.8 | all-reduce | flops 1 | bytes 8 | tf_op jit(solution)/shard_map/psum | solution.py:62
  112.7 16.2 fusion.4
  145.2 17.8 convolution_convert_fusion.2
  169.1 97.4 %all-gather.9.cloned.1.call-done = bf16[1536,2,4608]{2,0,1:T(8,128)(2,1)} async-done(((bf16[1536,2,1152]{2,0,1:T(8,128)(2,1)}), bf16[1536,2,4608]{2,0,1:T(8,128)(2,1)}) %all-gather.9.cloned.1.call-update) | async-done | bytes 28311568 | tf_op jit(solution)/shard_map/all_gather | solution.py:102
  266.5 25.4 %fusion.47 = f32[512,2,4608]{2,0,1:T(8,128)} fusion(bf16[1536,2,4608]{2,0,1:T(8,128)(2,1)} %all-gather.9.cloned.1.call-done, f32[512,1536]{1,0:T(8,128)S(1)} %get-tuple-element.99, f32[1536]{0:T(1024)S(1)} %copy-done.15, f32[512]{0:T(512)S(1)} %fusion.53), kind=kOutput, calls=%fused_computation.88 | convolution fusion | flops 14497873920 | bytes 50339840 | tf_op jit(solution)/shard_map/td,dgf->tgf/dot_general | solution.py:105
  302.2 56.8 %all-gather.11.cloned.1.call-done = bf16[4608,1536]{1,0:T(8,128)(2,1)} async-done(((bf16[1152,1536]{1,0:T(8,128)(2,1)}), bf16[4608,1536]{1,0:T(8,128)(2,1)}) %all-gather.11.cloned.1.call-update) | async-done | bytes 14155792 | tf_op jit(solution)/shard_map/all_gather | solution.py:103
  372.7 24.7 %multiply_bitcast_fusion = (f32[512,1,4608]{2,0,1:T(8,128)}, f32[512,1,4608]{2,0,1:T(8,128)}) fusion(f32[512,2,4608]{2,0,1:T(8,128)} %fusion.47, bf16[512,1536]{1,0:T(8,128)(2,1)S(1)} %get-tuple-element.100, bf16[4608,1536]{1,0:T(8,128)(2,1)} %all-gather.11.cloned.1.call-done), kind=kOutput, calls=%fused_computation.22 | convolution fusion | flops 7299661824 | bytes 53477376 | tf_op jit(solution)/shard_map/td,fd->tf/dot_general | solution.py:116
  397.4 28.6 %fusion.29 = f32[1536,2,4608]{2,0,1:T(8,128)} fusion(f32[512,1,4608]{2,0,1:T(8,128)} %get-tuple-element.90, f32[512,1,4608]{2,0,1:T(8,128)} %get-tuple-element.89, f32[512,1536]{1,0:T(8,128)S(1)} %get-tuple-element.99, f32[1536]{0:T(1024)S(1)} %copy-done.15, f32[512]{0:T(512)S(1)} %fusion.53), kind=kOutput, calls=%fused_computation.71 | convolution fusion | flops 14507311104 | bytes 78651392 | tf_op jit(solution)/shard_map/td,tgf->dgf/dot_general | solution.py:118
  426.1 30.9 %multiply_reduce_fusion = (f32[1536]{0:T(1024)}, f32[512]{0:T(512)S(1)}, f32[512,1536]{1,0:T(8,128)}) fusion(f32[512,1536]{1,0:T(8,128)S(1)} %get-tuple-element.99, f32[512]{0:T(512)S(1)} %fusion.53, f32[1536]{0:T(1024)S(1)} %copy-done.15, bf16[1536,2,4608]{2,0,1:T(8,128)(2,1)} %all-gather.9.cloned.1.call-done, f32[512,1,4608]{2,0,1:T(8,128)} %get-tuple-element.90, ...), kind=kOutput, calls=%fused_computation.47 | convolution fusion | flops 14509668352 | bytes 53493760 | tf_op jit(solution)/shard_map/tgf,dgf->td/dot_general | solution.py:119
  478.0 32.9 %fusion = (f32[12,512]{1,0:T(8,128)S(1)}, f32[1536,512,12]{1,0,2:T(8,128)}) fusion(f32[1536,512,12]{1,0,2:T(8,128)} %get-tuple-element.97, f32[12,512]{1,0:T(8,128)S(1)} %copy-done.14, pred[512,1536]{0,1:T(8,128)(4,1)S(1)} %copy-done.1, bf16[512,12,128]{0,2,1:T(8,128)(2,1)S(1)} %bitcast.137, bf16[1536,256]{1,0:T(8,128)(2,1)S(1)} %copy-done.9), kind=kOutput, calls=%fused_computation.2 | convolution fusion | flops 2463098880 | bytes 78307328 | tf_op jit(solution)/shard_map/while/body/eval_jaxpr/qhe,ke->hqk/dot_general | solution.py:132
  510.9 31.9 %fusion.2 = bf16[12,512,1536]{1,2,0:T(8,128)(2,1)} fusion(f32[1536,512,12]{1,0,2:T(8,128)} %get-tuple-element.104, f32[1536,512,12]{1,0,2:T(8,128)} %get-tuple-element.97, f32[12,512]{1,0:T(8,128)S(1)} %get-tuple-element.103, f32[12,512]{1,0:T(8,128)S(1)} %copy-done.14, pred[512,1536]{0,1:T(8,128)(4,1)S(1)} %copy-done.1), kind=kLoop, calls=%fused_computation.4 | loop fusion | flops 56623104 | bytes 95207424 | tf_op jit(solution)/shard_map/while/body/eval_jaxpr/convert_element_type | solution.py:136
  556.9 17.3 convolution_bitcast_fusion.1
  635.6 174.3 %reduce-scatter.25.cloned.1.call-done = f32[1536,2,1152]{2,0,1:T(8,128)} async-done(((f32[1536,2,4608]{2,0,1:T(8,128)}), f32[1536,2,1152]{2,0,1:T(8,128)}) %reduce-scatter.25.cloned.1.call-update) | async-done | bytes 14155792 | tf_op jit(solution)/shard_map/reduce_scatter | solution.py:177
  810.0 30.7 %reduce-scatter.19.cloned.1.call-done = f32[384,2,128]{0,2,1:T(8,128)} async-done(((f32[1536,2,128]{0,2,1:T(8,128)}), f32[384,2,128]{0,2,1:T(8,128)}) %reduce-scatter.19.cloned.1.call-update) | async-done | bytes 393232 | tf_op jit(solution)/shard_map/reduce_scatter | solution.py:175
  840.7 81.0 %reduce-scatter.23.cloned.1.call-done = f32[384,1536]{1,0:T(8,128)} async-done(((f32[1536,1536]{1,0:T(8,128)}), f32[384,1536]{1,0:T(8,128)}) %reduce-scatter.23.cloned.1.call-update) | async-done | bytes 2359312 | tf_op jit(solution)/shard_map/reduce_scatter | solution.py:176
  924.8 77.9 %reduce-scatter.17.cloned.1.call-done = f32[384,1536]{1,0:T(8,128)} async-done(((f32[1536,1536]{1,0:T(8,128)}), f32[384,1536]{1,0:T(8,128)}) %reduce-scatter.17.cloned.1.call-update) | async-done | bytes 2359312 | tf_op jit(solution)/shard_map/reduce_scatter | solution.py:174
  1005.9 200.5 %reduce-scatter.29.cloned.1.call-done = f32[1152,1536]{1,0:T(8,128)} async-done(((f32[4608,1536]{1,0:T(8,128)}), f32[1152,1536]{1,0:T(8,128)}) %reduce-scatter.29.cloned.1.call-update) | async-done | bytes 7077904 | tf_op jit(solution)/shard_map/reduce_scatter | solution.py:178
  1224.3 45.7 %all-reduce.2 = (f32[]{:T(128)}, f32[1536]{0:T(1024)}, f32[1536]{0:T(1024)}) all-reduce(f32[]{:T(128)} %get-tuple-element.92, f32[1536]{0:T(1024)S(1)} %get-tuple-element.84, f32[1536]{0:T(1024)S(1)} %copy-done.22), channel_id=1, replica_groups=mesh['seq'=8,'wt'=4] {'seq','wt'}, use_global_device_ids=true, to_apply=%region_5.6 | all-reduce | flops 3073 | bytes 24584 | tf_op jit(solution)/shard_map/psum | solution.py:187
  1275.4 163.4 %reduce-scatter.27.cloned.1.call-done = f32[192,2,1152]{2,0,1:T(8,128)} async-done(((f32[1536,2,1152]{2,0,1:T(8,128)}), f32[192,2,1152]{2,0,1:T(8,128)}) %reduce-scatter.27.cloned.1.call-update) | async-done | bytes 1769488 | tf_op jit(solution)/shard_map/reduce_scatter | solution.py:184
  1442.9 60.1 %reduce-scatter.21.cloned.1.call-done = f32[384,2,16]{0,2,1:T(8,128)} async-done(((f32[384,2,128]{0,2,1:T(8,128)}), f32[384,2,16]{0,2,1:T(8,128)}) %reduce-scatter.21.cloned.1.call-update) | async-done | bytes 49168 | tf_op jit(solution)/shard_map/reduce_scatter | solution.py:182
  1503.0 72.1 %reduce-scatter.33.cloned.1.call-done = f32[192,384]{1,0:T(8,128)} async-done(((f32[1536,384]{1,0:T(8,128)}), f32[192,384]{1,0:T(8,128)}) %reduce-scatter.33.cloned.1.call-update) | async-done | bytes 294928
  1575.1 72.6 %reduce-scatter.31.cloned.1.call-done = f32[192,384]{1,0:T(8,128)} async-done(((f32[1536,384]{1,0:T(8,128)}), f32[192,384]{1,0:T(8,128)}) %reduce-scatter.31.cloned.1.call-update) | async-done | bytes 294928
  1647.7 134.1 %reduce-scatter.35.cloned.1.call-done = f32[192,1152]{1,0:T(8,128)} async-done(((f32[1536,1152]{1,0:T(8,128)}), f32[192,1152]{1,0:T(8,128)}) %reduce-scatter.35.cloned.1.call-update) | async-done | bytes 884752
  (130 shorter events, 204.6 us)
Async XLA Ops:
  7.2 45.9 %all-gather.5.cloned.1.call-start = ((), (), s32[]{:S(2)}) async-start(), calls=%async_computation.10 | async-start | bytes 6881280 | tf_op jit(solution)/shard_map/all_gather | solution.py:64
  7.9 155.0 %all-gather.7.cloned.1.call-start = ((), (), s32[]{:S(2)}) async-start(), calls=%async_computation.11 | async-start | bytes 5898240 | tf_op jit(solution)/shard_map/all_gather | solution.py:65
  8.7 257.9 %all-gather.9.cloned.1.call-start = ((), (), s32[]{:S(2)}) async-start(), calls=%async_computation.12 | async-start | bytes 35389440 | tf_op jit(solution)/shard_map/all_gather | solution.py:102
  15.5 37.6 %copy-start.23 = (f32[1536]{0:T(1024)S(1)}, f32[1536]{0:T(1024)}, u32[]{:S(2)}) copy-start(f32[1536]{0:T(1024)} %param.16) | copy-start | bytes 18436
  15.5 343.5 %all-gather.11.cloned.1.call-start = ((), (), s32[]{:S(2)}) async-start(), calls=%async_computation.13 | async-start | bytes 17694720 | tf_op jit(solution)/shard_map/all_gather | solution.py:103
  16.1 793.8 %reduce-scatter.25.cloned.1.call-start = ((), (), s32[]{:S(2)}) async-start(), calls=%async_computation.18 | async-start | bytes 70778880 | tf_op jit(solution)/shard_map/reduce_scatter | solution.py:177
  18.4 40.3 %copy-start.18 = (f32[512]{0:T(512)}, f32[512]{0:T(512)S(1)}, u32[]{:S(2)}) copy-start(f32[512]{0:T(512)S(1)} %fusion.52) | copy-start | bytes 6148
  59.4 51.4 %collective-permute-start.1 = (bf16[512,256]{1,0:T(8,128)(2,1)}, bf16[512,256]{1,0:T(8,128)(2,1)}, u32[]{:S(2)}, u32[]{:S(2)}) collective-permute-start(bf16[512,256]{1,0:T(8,128)(2,1)} %slice.53), channel_id=1, source_target_pairs={{0,4},{4,8},{8,12},{12,16},{16,20},{20,24},{24,28},{1,5},{5,9},{9,... | collective-permute-start | bytes 786440 | tf_op jit(solution)/shard_map/ppermute | solution.py:21
  62.5 48.3 %collective-permute-start = (bf16[512,256]{1,0:T(8,128)(2,1)}, bf16[512,256]{1,0:T(8,128)(2,1)}, u32[]{:S(2)}, u32[]{:S(2)}) collective-permute-start(bf16[512,256]{1,0:T(8,128)(2,1)} %slice.53), channel_id=1, source_target_pairs={{0,8},{4,12},{8,16},{12,20},{16,24},{20,28},{1,9},{5,13},{9,17},{1... | collective-permute-start | bytes 786440 | tf_op jit(solution)/shard_map/ppermute | solution.py:21
  67.0 78.1 %copy-start = (pred[512,1536]{0,1:T(8,128)(4,1)}, pred[512,1536]{0,1:T(8,128)(4,1)S(1)}, u32[]{:S(2)}) copy-start(pred[512,1536]{0,1:T(8,128)(4,1)S(1)} %fusion.25) | copy-start | bytes 2359300
  162.9 103.6 %copy-start.15 = (f32[1536]{0:T(1024)S(1)}, f32[1536]{0:T(1024)}, u32[]{:S(2)}) copy-start(f32[1536]{0:T(1024)} %param.17) | copy-start | bytes 18436
  169.1 122.8 %copy-start.20 = (f32[512]{0:T(512)}, f32[512]{0:T(512)S(1)}, u32[]{:S(2)}) copy-start(f32[512]{0:T(512)S(1)} %get-tuple-element.98) | copy-start | bytes 6148
  426.0 414.6 %reduce-scatter.19.cloned.1.call-start = ((), (), s32[]{:S(2)}) async-start(), calls=%async_computation.15 | async-start | bytes 1966080 | tf_op jit(solution)/shard_map/reduce_scatter | solution.py:175
  575.5 15.8 collective-permute-start.2
  577.6 14.8 collective-permute-start.3
  604.7 317.0 %reduce-scatter.23.cloned.1.call-start = ((), (), s32[]{:S(2)}) async-start(), calls=%async_computation.17 | async-start | bytes 11796480 | tf_op jit(solution)/shard_map/reduce_scatter | solution.py:176
  611.4 391.3 %reduce-scatter.17.cloned.1.call-start = ((), (), s32[]{:S(2)}) async-start(), calls=%async_computation.14 | async-start | bytes 11796480 | tf_op jit(solution)/shard_map/reduce_scatter | solution.py:174
  619.7 586.7 %reduce-scatter.29.cloned.1.call-start = ((), (), s32[]{:S(2)}) async-start(), calls=%async_computation.20 | async-start | bytes 35389440 | tf_op jit(solution)/shard_map/reduce_scatter | solution.py:178
  635.5 803.3 %reduce-scatter.27.cloned.1.call-start = ((), (), s32[]{:S(2)}) async-start(), calls=%async_computation.19 | async-start | bytes 15925248 | tf_op jit(solution)/shard_map/reduce_scatter | solution.py:184
  809.9 693.1 %reduce-scatter.21.cloned.1.call-start = ((), (), s32[]{:S(2)}) async-start(), calls=%async_computation.16 | async-start | bytes 442368 | tf_op jit(solution)/shard_map/reduce_scatter | solution.py:182
  840.7 734.4 %reduce-scatter.33.cloned.1.call-start = ((), (), s32[]{:S(2)}) async-start(), calls=%async_computation.22 | async-start | bytes 2654208
  924.8 722.9 %reduce-scatter.31.cloned.1.call-start = ((), (), s32[]{:S(2)}) async-start(), calls=%async_computation.21 | async-start | bytes 2654208
  1005.8 776.0 %reduce-scatter.35.cloned.1.call-start = ((), (), s32[]{:S(2)}) async-start(), calls=%async_computation.23 | async-start | bytes 7962624
  1215.2 55.4 %copy-start.17 = (f32[512]{0:T(512)S(1)}, f32[512]{0:T(512)}, u32[]{:S(2)}) copy-start(f32[512]{0:T(512)} %copy-done.16) | copy-start | bytes 6148
  (20 other events, 248.7 us)
Sparse Core Ops, SparseCore 0:
  9.6 43.4 all-gather.4
  54.6 38.1 all-gather.6
  94.4 172.0 all-gather.8
  267.9 91.0 all-gather.10
  426.1 383.7 reduce-scatter.24
  812.5 28.1 reduce-scatter.18
  843.2 78.3 reduce-scatter.22
  924.3 78.3 reduce-scatter.16
  1005.3 201.0 reduce-scatter.28
  1210.3 228.4 reduce-scatter.26
  1443.0 59.8 reduce-scatter.20
  1507.3 67.7 reduce-scatter.32
  1579.6 68.0 reduce-scatter.30
  1652.3 129.4 reduce-scatter.34
where the time goes:
time: 1800 us; the launch traced here: 1790 us
  waiting for transfers between devices  1260 us (70%)
  matrix products  285 us (16%)
  blocking collectives  85.6 us (5%)
  other arithmetic  78.3 us (4%)
  local copies, waits for them, and re-layouts  50.7 us (3%)
  between operations  18.4 us (1%)
    unnamed x17, waiting for transfers between devices  281 us
    reduce_scatter x1, waiting for transfers between devices, per_device(): lax.psum_scatter(grad_down, 'wt', scatter_dimension=0, tiled=True)  201 us
    reduce_scatter x1, waiting for transfers between devices, per_device(): lax.psum_scatter(grad_in, 'wt', scatter_dimension=2, tiled=True)  174 us
    reduce_scatter x1, waiting for transfers between devices, per_device(): lax.psum_scatter(grad_in, 'seq', scatter_dimension=0, tiled=True)  163 us
    all_gather x1, waiting for transfers between devices, per_device(): lax.all_gather(w_in, 'wt', axis=2, tiled=True)  97.4 us
    reduce_scatter x1, waiting for transfers between devices, per_device(): lax.psum_scatter(grad_out, 'wt', scatter_dimension=0, tiled=True)  81 us
    reduce_scatter x1, waiting for transfers between devices, per_device(): lax.psum_scatter(grad_queries, 'wt', scatter_dimension=0, tiled=True)  77.9 us
    reduce_scatter x1, waiting for transfers between devices, per_device(): lax.psum_scatter(grad_keyvals, 'seq', scatter_dimension=2, tiled=True)  60.1 us
  transfers between devices with their start and end apart: 18, of which 15 were waited for; matrix products, arithmetic and copies ran while one was open for 19% of the time, Pallas kernels for 0%

commit v1 on v0

--- a/solution.py
+++ b/solution.py
@@ -59,7 +59,7 @@
     positions = seq_place * tok_rows - edge_rows + jnp.arange(edge_rows + tok_rows, dtype=jnp.int32)
     seq_ids = stream_ids(positions, seq_lengths[0], stream_len)
     valid = (seq_ids[edge_rows:] >= 0).astype(jnp.float32)
-    valid_total = lax.psum(jnp.sum(valid), ("seq", "wt"))
+    valid_total = lax.psum(jnp.sum(seq_lengths[0]).astype(jnp.float32), "wt")
     attn_full, out_full = (
         lax.all_gather(w_attn, "wt", axis=0, tiled=True),
         lax.all_gather(w_out, "wt", axis=0, tiled=True),
@@ -98,29 +98,30 @@
     middle = inputs + jnp.dot(mixed_b, out_full, preferred_element_type=jnp.float32)
     normed_two_f, norm_two_pull = jax.vjp(rms_scale, middle, gain_ffn)
     normed_two = normed_two_f.astype(jnp.bfloat16)
-    in_full, down_full = (
-        lax.all_gather(w_in, "wt", axis=2, tiled=True),
-        lax.all_gather(w_down, "wt", axis=0, tiled=True),
-    )
-    gate_up = jnp.einsum("td,dgf->tgf", normed_two, in_full, preferred_element_type=jnp.float32)
+    normed_all = lax.all_gather(normed_two, "wt", axis=0, tiled=True)
+    gate_up = jnp.einsum("td,dgf->tgf", normed_all, w_in, preferred_element_type=jnp.float32)
     hidden_f, act_pull = jax.vjp(gated_act, gate_up)
     hidden = hidden_f.astype(jnp.bfloat16)
-    ffn_part = jnp.dot(hidden, down_full, preferred_element_type=jnp.float32)
-    output = middle + ffn_part
+    ffn_low = jnp.dot(hidden, w_down, preferred_element_type=jnp.float32).astype(jnp.bfloat16)
+    ffn_part = lax.psum_scatter(ffn_low, "wt", scatter_dimension=0, tiled=True)
+    output = middle + ffn_part.astype(jnp.float32)
     diff = output - target
     masked_diff = valid[:, None] * diff
     squares = jnp.sum(masked_diff * diff)
     cotangent = masked_diff * (all_slots / valid_total)
-    cot_low = cotangent.astype(jnp.bfloat16)
-    grad_down = jnp.einsum("tf,td->fd", hidden, cot_low, preferred_element_type=jnp.float32)
-    grad_hidden = jnp.einsum("td,fd->tf", cot_low, down_full, preferred_element_type=jnp.float32)
+    cot_all = lax.all_gather(cotangent.astype(jnp.bfloat16), "wt", axis=0, tiled=True)
+    grad_down = jnp.einsum("td,tf->df", cot_all, hidden, preferred_element_type=jnp.float32)
+    grad_down = lax.psum_scatter(grad_down.astype(jnp.bfloat16), "seq", scatter_dimension=0, tiled=True)
+    grad_hidden = jnp.einsum("td,fd->tf", cot_all, w_down, preferred_element_type=jnp.float32)
     grad_gu = act_pull(grad_hidden)[0].astype(jnp.bfloat16)
-    grad_in = jnp.einsum("td,tgf->dgf", normed_two, grad_gu, preferred_element_type=jnp.float32)
-    grad_norm_two = jnp.einsum("tgf,dgf->td", grad_gu, in_full, preferred_element_type=jnp.float32)
+    norm_two_low = jnp.einsum("tgf,dgf->td", grad_gu, w_in, preferred_element_type=jnp.float32).astype(jnp.bfloat16)
+    grad_norm_two = lax.psum_scatter(norm_two_low, "wt", scatter_dimension=0, tiled=True).astype(jnp.float32)
+    grad_in = jnp.einsum("td,tgf->dgf", normed_all, grad_gu, preferred_element_type=jnp.float32)
+    grad_in = lax.psum_scatter(grad_in.astype(jnp.bfloat16), "seq", scatter_dimension=0, tiled=True)
     grad_middle_norm, grad_gain_ffn = norm_two_pull(grad_norm_two)
     grad_middle = cotangent + grad_middle_norm
     grad_mid_low = grad_middle.astype(jnp.bfloat16)
-    grad_out = jnp.einsum("td,te->de", mixed_b, grad_mid_low, preferred_element_type=jnp.float32)
+    grad_out = jnp.einsum("te,td->ed", grad_mid_low, mixed_b, preferred_element_type=jnp.float32)
     grad_mixed = jnp.einsum("te,de->td", grad_mid_low, out_full, preferred_element_type=jnp.float32)
     grad_mixed = grad_mixed.astype(jnp.bfloat16).reshape(tok_rows, HEADS, HD)
 
@@ -164,26 +165,28 @@
     grad_qkv = jnp.concatenate(
         [grad_query_blocks.reshape(tok_rows, model_width), grad_kv], axis=1
     ).astype(jnp.bfloat16)
-    grad_attn = jnp.einsum("td,te->de", normed, grad_qkv, preferred_element_type=jnp.float32)
+    grad_attn = jnp.einsum("te,td->ed", grad_qkv, normed, preferred_element_type=jnp.float32)
     grad_normed = jnp.einsum("te,de->td", grad_qkv, attn_full, preferred_element_type=jnp.float32)
     grad_input_norm, grad_gain_attn = norm_one_pull(grad_normed)
     grad_inputs = grad_middle + grad_input_norm
-    grad_queries = grad_attn[:, :model_width]
-    grad_keyvals = grad_attn[:, model_width:].reshape(grad_attn.shape[0], 2, HD)
-    grad_queries, grad_keyvals, grad_out, grad_in, grad_down = (
-        lax.psum_scatter(grad_queries, "wt", scatter_dimension=0, tiled=True),
-        lax.psum_scatter(grad_keyvals, "wt", scatter_dimension=0, tiled=True),
-        lax.psum_scatter(grad_out, "wt", scatter_dimension=0, tiled=True),
-        lax.psum_scatter(grad_in, "wt", scatter_dimension=2, tiled=True),
-        lax.psum_scatter(grad_down, "wt", scatter_dimension=0, tiled=True),
-    )
-    grad_queries, grad_keyvals, grad_out, grad_in, grad_down = (
-        lax.psum_scatter(grad_queries, "seq", scatter_dimension=1, tiled=True),
-        lax.psum_scatter(grad_keyvals, "seq", scatter_dimension=2, tiled=True),
-        lax.psum_scatter(grad_out, "seq", scatter_dimension=1, tiled=True),
-        lax.psum_scatter(grad_in, "seq", scatter_dimension=0, tiled=True),
-        lax.psum_scatter(grad_down, "seq", scatter_dimension=1, tiled=True),
-    )
+    grad_keyvals = jnp.swapaxes(grad_attn[model_width:].reshape(2, seq_devices, HD // seq_devices, model_width), 0, 1)
+    slot = model_width // seq_devices
+    packed = jnp.concatenate(
+        [
+            grad_attn[:model_width].reshape(seq_devices, slot, model_width),
+            grad_keyvals.reshape(seq_devices, 2 * HD // seq_devices, model_width),
+            grad_out.reshape(seq_devices, slot, model_width),
+        ],
+        axis=1,
+    ).astype(jnp.bfloat16)
+    packed = packed.reshape(seq_devices, 2 * slot + 2 * HD // seq_devices, lax.axis_size("wt"), -1)
+    packed = lax.psum_scatter(packed, "seq", scatter_dimension=0, tiled=False)
+    packed = lax.psum_scatter(packed, "wt", scatter_dimension=1, tiled=False).astype(jnp.float32)
+    grad_queries = packed[:slot].T
+    grad_keyvals = packed[slot:-slot].T.reshape(-1, 2, HD // seq_devices)
+    grad_out = packed[-slot:].T
+    grad_down = grad_down.astype(jnp.float32).T
+    grad_in = grad_in.astype(jnp.float32)
     squares_all, gain_attn_all, gain_ffn_all = lax.psum(
         (squares, grad_gain_attn, grad_gain_ffn), ("seq", "wt")
     )

time: 1800 us -> 1050 us (0.58)
  waiting for transfers between devices: 1260 us -> 582 us
  matrix products: 285 us -> 245 us
  blocking collectives: 85.6 us -> 48.2 us
    reduce_scatter x7 -> x6, waiting for transfers between devices: 788 us -> 438 us  [the longest x1 146 us: per_device(): packed = lax.psum_scatter(packed, 'seq', scatter_dimension=0, tiled=False)]
    unnamed x17 -> x10, waiting for transfers between devices: 281 us -> 1.51 us
    all_gather x2, waiting for transfers between devices: 154 us -> 94.2 us  [the longest x1 47.3 us: per_device(): normed_all = lax.all_gather(normed_two, 'wt', axis=0, tiled=True)]
    psum x1, blocking collectives: 39.9 us -> 5.77 us  [per_device(): valid_total = lax.psum(jnp.sum(seq_lengths[0]).astype(jnp.float32), 'wt')]
    dot_general x8, matrix products: 149 us -> 122 us  [the longest x1 23.6 us: per_device(): jnp.einsum('td,fd->tf', cot_all, w_down, preferred_element_type=jnp.float32)]
    unnamed x57 -> x75, local copies, waits for them, and re-layouts: 31.6 us -> 12.4 us
  transfers between devices with their start and end apart: 18 -> 14, of which waited for: 15 -> 12; matrix products, arithmetic and copies ran while one was open for 19% -> 13% of each run, Pallas kernels for 0% -> 0%
where the time goes in v1:
time: 1050 us; the launch traced here: 1040 us
  waiting for transfers between devices  582 us (55%)
  matrix products  245 us (23%)
  other arithmetic  91.6 us (9%)
  blocking collectives  48.2 us (5%)
  local copies, waits for them, and re-layouts  42.5 us (4%)
  between operations  18.7 us (2%)
  starting transfers between devices  11.7 us (1%)
    reduce_scatter x1, waiting for transfers between devices, per_device(): packed = lax.psum_scatter(packed, 'seq', scatter_dimension=0, tiled=False)  146 us
    reduce_scatter x1, waiting for transfers between devices, per_device(): lax.psum_scatter(grad_down.astype(jnp.bfloat16), 'seq', scatter_dimension...  83.2 us
    reduce_scatter x1, waiting for transfers between devices, per_device(): lax.psum_scatter(grad_in.astype(jnp.bfloat16), 'seq', scatter_dimension=0...  73.8 us
    reduce_scatter x1, waiting for transfers between devices, per_device(): lax.psum_scatter(norm_two_low, 'wt', scatter_dimension=0, tiled=True)  58 us
    reduce_scatter x1, waiting for transfers between devices, per_device(): ffn_part = lax.psum_scatter(ffn_low, 'wt', scatter_dimension=0, tiled=True)  51 us
    all_gather x1, waiting for transfers between devices, per_device(): normed_all = lax.all_gather(normed_two, 'wt', axis=0, tiled=True)  47.3 us
    all_gather x1, waiting for transfers between devices, per_device(): lax.all_gather(cotangent.astype(jnp.bfloat16), 'wt', axis=0, tiled=True)  46.9 us
    psum x1, blocking collectives, per_device(): lax.psum((squares, grad_gain_attn, grad_gain_ffn), ('seq', 'wt'))  42.5 us
  transfers between devices with their start and end apart: 14, of which 12 were waited for; matrix products, arithmetic and copies ran while one was open for 13% of the time, Pallas kernels for 0%

profile of v1, /device:TPU:11, one launch (start us, length us, event | category | flops | bytes accessed | tf_op | source)
XLA Modules:
  0.0 1040.1 jit_solution(6189398098925557528)
XLA Ops:
  12.9 40.2 %all-gather.5.cloned.1.call-done = bf16[1536,1792]{1,0:T(8,128)(2,1)} async-done(((bf16[384,1792]{1,0:T(8,128)(2,1)}), bf16[1536,1792]{1,0:T(8,128)(2,1)}) %all-gather.5.cloned.1.call-update) | async-done | bytes 5505040 | tf_op jit(solution)/shard_map/all_gather | solution.py:64
  76.6 17.2 %fusion.4 = (f32[12,512]{1,0:T(8,128)S(1)}, f32[1536,512,12]{1,0,2:T(8,128)}) fusion(pred[512,1536]{0,1:T(8,128)(4,1)} %fusion.34, bf16[512,12,128]{0,2,1:T(8,128)(2,1)} %bitcast.168, bf16[1536,256]{1,0:T(8,128)(2,1)S(1)} %pad_maximum_fusion.4), kind=kOutput, calls=%fused_computation.9 | convolution fusion | flops 2444224512 | bytes 40525824 | tf_op jit(solution)/shard_map/while/body/eval_jaxpr/qhe,ke->hqk/dot_general | solution.py:79
  93.8 16.0 %exponential_reduce_fusion = f32[12,512]{1,0:T(8,128)S(1)} fusion(f32[1536,512,12]{1,0,2:T(8,128)} %get-tuple-element.90, f32[12,512]{1,0:T(8,128)S(1)} %get-tuple-element.89, pred[512,1536]{0,1:T(8,128)(4,1)S(1)} %copy-done.5), kind=kLoop, calls=%fused_computation.7 | loop fusion | flops 37742592 | bytes 38584320 | tf_op jit(solution)/shard_map/while/body/eval_jaxpr/reduce_sum | solution.py:89
  110.4 17.8 %convolution_convert_fusion.7 = bf16[128,12,512]{2,0,1:T(8,128)(2,1)} fusion(bf16[1536,256]{1,0:T(8,128)(2,1)} %copy-done.15, f32[1536,512,12]{1,0,2:T(8,128)} %get-tuple-element.90, f32[12,512]{1,0:T(8,128)} %log_add_fusion, pred[512,1536]{0,1:T(8,128)(4,1)} %fusion.34), kind=kOutput, calls=%fused_computation.84 | convolution fusion | flops 2454454272 | bytes 40534016 | tf_op jit(solution)/shard_map/while/body/eval_jaxpr/hqk,ke->qhe/dot_general | solution.py:91
  137.8 47.3 %all-gather.9.cloned.1.call-done = bf16[2048,1536]{1,0:T(8,128)(2,1)} async-done(((bf16[512,1536]{1,0:T(8,128)(2,1)}), bf16[2048,1536]{1,0:T(8,128)(2,1)}) %all-gather.9.cloned.1.call-update) | async-done | bytes 6291472 | tf_op jit(solution)/shard_map/all_gather | solution.py:101
  185.1 19.6 %fusion.13 = f32[2048,2,1152]{2,0,1:T(8,128)S(1)} fusion(bf16[2048,1536]{1,0:T(8,128)(2,1)} %all-gather.9.cloned.1.call-done, bf16[1536,2,1152]{2,1,0:T(2,128)(2,1)} %param.14), kind=kOutput, calls=%fused_computation.32 | convolution fusion | flops 14495514624 | bytes 32243712 | tf_op jit(solution)/shard_map/td,dgf->tgf/dot_general | solution.py:102
  213.2 10.2 convolution_convert_fusion.3
  230.5 51.0 %reduce-scatter.7.cloned.1.call-done = bf16[512,1536]{1,0:T(8,128)(2,1)} async-done(((bf16[2048,1536]{1,0:T(8,128)(2,1)}), bf16[512,1536]{1,0:T(8,128)(2,1)}) %reduce-scatter.7.cloned.1.call-update) | async-done | bytes 1572880 | tf_op jit(solution)/shard_map/reduce_scatter | solution.py:106
  286.3 46.9 %all-gather.11.cloned.1.call-done = bf16[2048,1536]{1,0:T(8,128)(2,1)} async-done(((bf16[512,1536]{1,0:T(8,128)(2,1)}), bf16[2048,1536]{1,0:T(8,128)(2,1)}) %all-gather.11.cloned.1.call-update) | async-done | bytes 6291472 | tf_op jit(solution)/shard_map/all_gather | solution.py:112
  333.2 23.6 %multiply_bitcast_fusion = (f32[2048,1,1152]{2,0,1:T(8,128)}, f32[2048,1,1152]{2,0,1:T(8,128)}) fusion(f32[2048,2,1152]{2,0,1:T(8,128)} %copy-done.7, bf16[2048,1536]{1,0:T(8,128)(2,1)} %all-gather.11.cloned.1.call-done, bf16[1152,1536]{1,0:T(8,128)(2,1)S(1)} %copy-done), kind=kOutput, calls=%fused_computation.25 | convolution fusion | flops 7299661824 | bytes 47579136 | tf_op jit(solution)/shard_map/td,fd->tf/dot_general | solution.py:115
  356.8 21.6 %bitcast_convert_fusion = bf16[2048,1536]{1,0:T(8,128)(2,1)} fusion(bf16[1536,2,1152]{2,1,0:T(2,128)(2,1)} %param.14, f32[2048,1,1152]{2,0,1:T(8,128)} %get-tuple-element.83, f32[2048,1,1152]{2,0,1:T(8,128)} %get-tuple-element.82), kind=kOutput, calls=%fused_computation.13 | convolution fusion | flops 14508097536 | bytes 32243712 | tf_op jit(solution)/shard_map/tgf,dgf->td/dot_general | solution.py:117
  378.5 58.0 %reduce-scatter.9.cloned.1.call-done = bf16[512,1536]{1,0:T(8,128)(2,1)} async-done(((bf16[2048,1536]{1,0:T(8,128)(2,1)}), bf16[512,1536]{1,0:T(8,128)(2,1)}) %reduce-scatter.9.cloned.1.call-update) | async-done | bytes 1572880 | tf_op jit(solution)/shard_map/reduce_scatter | solution.py:118
  452.4 17.2 %convolution_bitcast_fusion = f32[1536,128]{0,1:T(8,128)} fusion(bf16[512,12,128]{0,2,1:T(8,128)(2,1)S(1)} %bitcast.166, f32[1536,512,12]{1,0,2:T(8,128)} %get-tuple-element.90, f32[12,512]{1,0:T(8,128)S(1)} %copy-done.22, pred[512,1536]{0,1:T(8,128)(4,1)S(1)} %copy-done.6), kind=kOutput, calls=%fused_computation.75 | convolution fusion | flops 2453667840 | bytes 40919040 | tf_op jit(solution)/shard_map/while/body/eval_jaxpr/hqk,qhe->ke/dot_general | solution.py:148
  469.7 30.3 %fusion = (f32[12,512]{1,0:T(8,128)S(1)}, f32[1536,512,12]{1,0,2:T(8,128)}) fusion(f32[1536,512,12]{1,0,2:T(8,128)} %get-tuple-element.90, f32[12,512]{1,0:T(8,128)S(1)} %copy-done.22, pred[512,1536]{0,1:T(8,128)(4,1)S(1)} %copy-done.6, bf16[512,12,128]{0,2,1:T(8,128)(2,1)S(1)} %bitcast.167, bf16[1536,256]{1,0:T(8,128)(2,1)S(1)} %copy-done.16), kind=kOutput, calls=%fused_computation.2 | convolution fusion | flops 2463098880 | bytes 78307328 | tf_op jit(solution)/shard_map/while/body/eval_jaxpr/qhe,ke->hqk/dot_general | solution.py:133
  499.9 31.6 %fusion.2 = bf16[12,512,1536]{1,2,0:T(8,128)(2,1)} fusion(f32[1536,512,12]{1,0,2:T(8,128)} %get-tuple-element.94, f32[1536,512,12]{1,0,2:T(8,128)} %get-tuple-element.90, f32[12,512]{1,0:T(8,128)S(1)} %get-tuple-element.93, f32[12,512]{1,0:T(8,128)S(1)} %copy-done.22, pred[512,1536]{0,1:T(8,128)(4,1)S(1)} %copy-done.6), kind=kLoop, calls=%fused_computation.4 | loop fusion | flops 56623104 | bytes 95207424 | tf_op jit(solution)/shard_map/while/body/eval_jaxpr/convert_element_type | solution.py:137
  531.5 13.4 %fusion.36 = f32[1536,128]{0,1:T(8,128)} fusion(bf16[12,512,1536]{1,2,0:T(8,128)(2,1)} %fusion.2, bf16[512,12,128]{0,2,1:T(8,128)(2,1)S(1)} %bitcast.169), kind=kOutput, calls=%fused_computation.77 | convolution fusion | flops 2416115712 | bytes 21233664 | tf_op jit(solution)/shard_map/while/body/eval_jaxpr/hqk,qhe->ke/dot_general | solution.py:145
  574.9 9.1 concatenate.23
  600.8 13.3 %convolution_convert_fusion.1 = bf16[1536,1152]{1,0:T(8,128)(2,1)} fusion(bf16[2048,1536]{1,0:T(8,128)(2,1)} %all-gather.11.cloned.1.call-done, bf16[2048,1152]{1,0:T(8,128)(2,1)} %copy-done.17), kind=kOutput, calls=%fused_computation.28 | convolution fusion | flops 7249526784 | bytes 14548992 | tf_op jit(solution)/shard_map/td,tf->df/dot_general | solution.py:113
  614.2 22.4 %convolution_convert_fusion = bf16[1536,2,1152]{2,0,1:T(8,128)(2,1)} fusion(bf16[2048,1536]{1,0:T(8,128)(2,1)} %all-gather.9.cloned.1.call-done, f32[2048,1,1152]{2,0,1:T(8,128)} %get-tuple-element.83, f32[2048,1,1152]{2,0,1:T(8,128)} %get-tuple-element.82), kind=kOutput, calls=%fused_computation.14 | convolution fusion | flops 14508490752 | bytes 32243712 | tf_op jit(solution)/shard_map/td,tgf->dgf/dot_general | solution.py:119
  637.0 146.1 %reduce-scatter.11.cloned.1.call-done = bf16[1,416,4,384]{3,1,2,0:T(8,128)(2,1)} async-done(((bf16[8,416,4,384]{3,1,2,0:T(8,128)(2,1)}), bf16[1,416,4,384]{3,1,2,0:T(8,128)(2,1)}) %reduce-scatter.11.cloned.1.call-update) | async-done | bytes 1277968 | tf_op jit(solution)/shard_map/reduce_scatter | solution.py:183
  783.7 83.2 %reduce-scatter.17.cloned.1.call-done = bf16[192,1152]{1,0:T(8,128)(2,1)} async-done(((bf16[1536,1152]{1,0:T(8,128)(2,1)}), bf16[192,1152]{1,0:T(8,128)(2,1)}) %reduce-scatter.17.cloned.1.call-update) | async-done | bytes 442384 | tf_op jit(solution)/shard_map/reduce_scatter | solution.py:114
  876.7 42.5 %all-reduce.2 = (f32[]{:T(128)}, f32[1536]{0:T(1024)}, f32[1536]{0:T(1024)}) all-reduce(f32[]{:T(128)} %get-tuple-element.76, f32[1536]{0:T(1024)S(1)} %get-tuple-element.74, f32[1536]{0:T(1024)S(1)} %copy-done.24), channel_id=1, replica_groups=mesh['seq'=8,'wt'=4] {'seq','wt'}, use_global_device_ids=true, to_apply=%region_6.7 | all-reduce | flops 3073 | bytes 24584 | tf_op jit(solution)/shard_map/psum | solution.py:190
  925.8 73.8 %reduce-scatter.15.cloned.1.call-done = bf16[192,2,1152]{2,0,1:T(8,128)(2,1)} async-done(((bf16[1536,2,1152]{2,0,1:T(8,128)(2,1)}), bf16[192,2,1152]{2,0,1:T(8,128)(2,1)}) %reduce-scatter.15.cloned.1.call-update) | async-done | bytes 884752 | tf_op jit(solution)/shard_map/reduce_scatter | solution.py:120
  1002.9 25.7 %reduce-scatter.13.cloned.1.call-done = bf16[416,1,384]{2,0,1:T(8,128)(2,1)} async-done(((bf16[416,4,384]{2,0,1:T(8,128)(2,1)}), bf16[416,1,384]{2,0,1:T(8,128)(2,1)}) %reduce-scatter.13.cloned.1.call-update) | async-done | bytes 319504 | tf_op jit(solution)/shard_map/reduce_scatter | solution.py:184
  (149 shorter events, 143.2 us)
Async XLA Ops:
  7.2 206.0 %copy-start = (bf16[1152,1536]{1,0:T(8,128)(2,1)S(1)}, bf16[1152,1536]{1,0:T(8,128)(2,1)}, u32[]{:S(2)}) copy-start(bf16[1152,1536]{1,0:T(8,128)(2,1)} %param.15) | copy-start | bytes 10616836
  7.2 45.9 %all-gather.5.cloned.1.call-start = ((), (), s32[]{:S(2)}) async-start(), calls=%async_computation.6 | async-start | bytes 6881280 | tf_op jit(solution)/shard_map/all_gather | solution.py:64
  7.9 120.3 %all-gather.7.cloned.1.call-start = ((), (), s32[]{:S(2)}) async-start(), calls=%async_computation.7 | async-start | bytes 5898240 | tf_op jit(solution)/shard_map/all_gather | solution.py:65
  8.7 176.4 %all-gather.9.cloned.1.call-start = ((), (), s32[]{:S(2)}) async-start(), calls=%async_computation.8 | async-start | bytes 7864320 | tf_op jit(solution)/shard_map/all_gather | solution.py:101
  60.0 12.7 %collective-permute-start.1 = (bf16[512,256]{1,0:T(8,128)(2,1)}, bf16[512,256]{1,0:T(8,128)(2,1)}, u32[]{:S(2)}, u32[]{:S(2)}) collective-permute-start(bf16[512,256]{1,0:T(8,128)(2,1)} %slice.79), channel_id=1, source_target_pairs={{0,4},{4,8},{8,12},{12,16},{16,20},{20,24},{24,28},{1,5},{5,9},{9,... | collective-permute-start | bytes 786440 | tf_op jit(solution)/shard_map/ppermute | solution.py:21
  63.1 12.4 %collective-permute-start = (bf16[512,256]{1,0:T(8,128)(2,1)}, bf16[512,256]{1,0:T(8,128)(2,1)}, u32[]{:S(2)}, u32[]{:S(2)}) collective-permute-start(bf16[512,256]{1,0:T(8,128)(2,1)} %slice.79), channel_id=1, source_target_pairs={{0,8},{4,12},{8,16},{12,20},{16,24},{20,28},{1,9},{5,13},{9,17},{1... | collective-permute-start | bytes 786440 | tf_op jit(solution)/shard_map/ppermute | solution.py:21
  137.8 143.8 %reduce-scatter.7.cloned.1.call-start = ((), (), s32[]{:S(2)}) async-start(), calls=%async_computation.9 | async-start | bytes 7864320 | tf_op jit(solution)/shard_map/reduce_scatter | solution.py:106
  223.4 109.8 %all-gather.11.cloned.1.call-start = ((), (), s32[]{:S(2)}) async-start(), calls=%async_computation.10 | async-start | bytes 7864320 | tf_op jit(solution)/shard_map/all_gather | solution.py:112
  286.2 150.4 %reduce-scatter.9.cloned.1.call-start = ((), (), s32[]{:S(2)}) async-start(), calls=%async_computation.11 | async-start | bytes 7864320 | tf_op jit(solution)/shard_map/reduce_scatter | solution.py:118
  378.4 58.1 %copy-start.4 = (f32[512,1536]{1,0:T(8,128)S(1)}, f32[512,1536]{1,0:T(8,128)}, u32[]{:S(2)}) copy-start(f32[512,1536]{1,0:T(8,128)} %copy-done.3) | copy-start | bytes 9437188
  378.4 58.1 %copy-start.26 = (f32[512]{0:T(512)S(1)}, f32[512]{0:T(512)}, u32[]{:S(2)}) copy-start(f32[512]{0:T(512)} %copy-done.25) | copy-start | bytes 6148
  378.4 58.1 %copy-start.27 = (f32[512]{0:T(512)S(1)}, f32[512]{0:T(512)}, u32[]{:S(2)}) copy-start(f32[512]{0:T(512)} %compare_convert_fusion) | copy-start | bytes 6148
  378.5 63.5 %copy-start.33 = (f32[512]{0:T(512)S(1)}, f32[512]{0:T(512)}, u32[]{:S(2)}) copy-start(f32[512]{0:T(512)} %copy-done.32) | copy-start | bytes 6148
  378.5 404.5 %reduce-scatter.11.cloned.1.call-start = ((), (), s32[]{:S(2)}) async-start(), calls=%async_computation.12 | async-start | bytes 11501568 | tf_op jit(solution)/shard_map/reduce_scatter | solution.py:183
  452.4 17.2 %copy-start.16 = (bf16[1536,256]{1,0:T(8,128)(2,1)S(1)}, bf16[1536,256]{1,0:T(8,128)(2,1)}, u32[]{:S(2)}) copy-start(bf16[1536,256]{1,0:T(8,128)(2,1)} %copy-done.15) | copy-start | bytes 2359300
  499.9 31.6 %copy-start.11 = (bf16[512,1536]{0,1:T(8,128)(2,1)S(1)}, bf16[512,1536]{0,1:T(8,128)(2,1)}, u32[]{:S(2)}) copy-start(bf16[512,1536]{0,1:T(8,128)(2,1)} %copy.35) | copy-start | bytes 4718596
  551.4 15.6 %collective-permute-start.2 = (f32[512,256]{0,1:T(8,128)S(1)}, f32[512,256]{0,1:T(8,128)S(1)}, u32[]{:S(2)}, u32[]{:S(2)}) collective-permute-start(f32[512,256]{0,1:T(8,128)S(1)} %get-tuple-element.85), channel_id=1, source_target_pairs={{4,0},{8,4},{12,8},{16,12},{20,16},{24,20},{28,24},{5,1},{9,5},{13... | collective-permute-start | bytes 1572872 | tf_op jit(solution)/shard_map/ppermute | solution.py:21
  553.6 14.4 %collective-permute-start.3 = (f32[512,256]{0,1:T(8,128)S(1)}, f32[512,256]{0,1:T(8,128)S(1)}, u32[]{:S(2)}, u32[]{:S(2)}) collective-permute-start(f32[512,256]{0,1:T(8,128)S(1)} %get-tuple-element.86), channel_id=1, source_target_pairs={{8,0},{12,4},{16,8},{20,12},{24,16},{28,20},{9,1},{13,5},{17,9},{2... | collective-permute-start | bytes 1572872 | tf_op jit(solution)/shard_map/ppermute | solution.py:21
  600.7 266.2 %reduce-scatter.17.cloned.1.call-start = ((), (), s32[]{:S(2)}) async-start(), calls=%async_computation.15 | async-start | bytes 3981312 | tf_op jit(solution)/shard_map/reduce_scatter | solution.py:114
  614.1 385.5 %reduce-scatter.15.cloned.1.call-start = ((), (), s32[]{:S(2)}) async-start(), calls=%async_computation.14 | async-start | bytes 7962624 | tf_op jit(solution)/shard_map/reduce_scatter | solution.py:120
  636.6 232.3 %copy-start.21 = (bf16[128,12,512]{2,0,1:T(8,128)(2,1)S(1)}, bf16[128,12,512]{2,0,1:T(8,128)(2,1)}, u32[]{:S(2)}) copy-start(bf16[128,12,512]{2,0,1:T(8,128)(2,1)} %multiply_convert_fusion.1) | copy-start | bytes 4718596
  636.7 391.9 %reduce-scatter.13.cloned.1.call-start = ((), (), s32[]{:S(2)}) async-start(), calls=%async_computation.13 | async-start | bytes 1597440 | tf_op jit(solution)/shard_map/reduce_scatter | solution.py:184
  868.9 50.9 %copy-start.29 = (f32[512]{0:T(512)S(1)}, f32[512]{0:T(512)}, u32[]{:S(2)}) copy-start(f32[512]{0:T(512)} %copy-done.28) | copy-start | bytes 6148
  919.8 112.0 %copy-start.1 = (bf16[1152,1536]{1,0:T(8,128)(2,1)S(1)}, bf16[1152,1536]{1,0:T(8,128)(2,1)}, u32[]{:S(2)}) copy-start(bf16[1152,1536]{1,0:T(8,128)(2,1)} %param.15) | copy-start | bytes 10616836
  (27 other events, 204.3 us)
Sparse Core Ops, SparseCore 0:
  9.6 43.4 all-gather.4
  54.7 37.4 all-gather.6
  137.9 47.1 all-gather.8
  223.5 57.9 reduce-scatter.6
  286.3 46.8 all-gather.10
  378.6 57.9 reduce-scatter.8
  600.8 182.1 reduce-scatter.10
  787.1 79.8 reduce-scatter.16
  871.1 128.4 reduce-scatter.14
  1002.0 26.5 reduce-scatter.12

commit v2 on v1

--- a/solution.py
+++ b/solution.py
@@ -3,6 +3,8 @@
 import jax
 import jax.numpy as jnp
 from jax import lax
+from jax.experimental import pallas as pl
+from jax.experimental.pallas import tpu as pltpu
 from jax.sharding import PartitionSpec as P
 
 HEADS = 12
@@ -13,6 +15,205 @@
 
 EPSILON = 1e-06
 NEGATIVE = -1e30
+
+MESH = pl.DeviceIdType.MESH
+F32 = jnp.float32
+BF16 = jnp.bfloat16
+
+
+def places():
+    seq, wt = lax.axis_index("seq"), lax.axis_index("wt")
+    return seq // 2, seq % 2, wt // 2, wt % 2
+
+
+def device(z, x, y, c):
+    return (z * 2 + x, y * 2 + c)
+
+
+def remote(src, dst, send, recv, to):
+    copy = pltpu.make_async_remote_copy(
+        src_ref=src, dst_ref=dst, send_sem=send, recv_sem=recv, device_id=to, device_id_type=MESH
+    )
+    copy.start()
+    return copy
+
+
+def greet(devices):
+    barrier = pltpu.get_barrier_semaphore()
+    for one in devices:
+        pl.semaphore_signal(barrier, inc=1, device_id=one, device_id_type=MESH)
+    pl.semaphore_wait(barrier, len(devices))
+
+
+def reduce_kernel(depth, widths, g_refs, p_ref, v_ref, g_outs, p_out, v_out, gx, gt, gz, pc, py, px, pt, pz, vb,
+                  gxs, gxr, gzs, gzr, pcs, pcr, pys, pyr, pxs, pxr, pzs, pzr, vs, vr):
+    z, x, y, c = places()
+    width = gx.shape[-1]
+    cols = pc.shape[-1]
+    sib, ypeer, xpeer = device(z, x, y, 1 - c), device(z, x, 1 - y, c), device(z, 1 - x, y, c)
+    zs = [lax.rem(z + d, depth) for d in range(depth)]
+    zpeers = [device(zs[d], x, y, c) for d in range(depth)]
+    greet([sib, ypeer, xpeer] + zpeers[1:])
+    places_of = [(i, k * width) for i, total in enumerate(widths) for k in range(total // width)]
+    chunks = len(places_of)
+    started = []
+
+    def go(*args):
+        started.append(remote(*args))
+        return started[-1]
+
+    order = list(range(1, depth)) + [0]
+    core = {}
+    for d in order:
+        for h in range(2):
+            at = pl.multiple_of((2 * h + 1 - c) * cols, cols)
+            core[d, h] = go(p_ref.at[zs[d], :, :, pl.ds(at, cols)], pc.at[d, h], pcs.at[d, h], pcr.at[d, h], sib)
+    gxc, gzc, pyc, pxc, pzc, vc = {}, {}, {}, {}, {}, {}
+
+    def g_send(k):
+        if k < chunks:
+            i, at = places_of[k]
+            gxc[k] = go(g_refs[i].at[:, 1 - x, :, pl.ds(at, width)], gx.at[k], gxs.at[k], gxr.at[k], xpeer)
+
+    for k in range(2):
+        g_send(k)
+    vc[0] = go(v_ref, vb.at[0], vs.at[0], vr.at[0], sib)
+
+    def p_y(d):
+        for h in range(2):
+            core[d, h].wait_recv()
+        mine = pl.multiple_of((2 * (1 - y) + c) * cols, cols)
+        pt[d] = (p_ref[zs[d], :, :, pl.ds(mine, cols)].astype(F32) + pc[d, 1 - y].astype(F32)).astype(BF16)
+        pyc[d] = go(pt.at[d], py.at[d], pys.at[d], pyr.at[d], ypeer)
+
+    def g_step(k):
+        gxc[k].wait_recv()
+        g_send(k + 2)
+        i, at = places_of[k]
+        for d in range(depth):
+            own = g_refs[i][zs[d], x, :, at : at + width].astype(F32)
+            gt[k, d] = (own + gx[k, zs[d]].astype(F32)).astype(BF16)
+            if d:
+                gzc[k, d] = go(gt.at[k, d], gz.at[k, d - 1], gzs.at[k, d - 1], gzr.at[k, d - 1], zpeers[d])
+
+    def g_end(k):
+        total = gt[k, 0].astype(F32)
+        for d in range(1, depth):
+            gzc[k, d].wait_recv()
+            total += gz[k, d - 1].astype(F32)
+        i, at = places_of[k]
+        g_outs[i][:, at : at + width] = total
+
+    def p_half(d, side):
+        mine = pl.multiple_of((2 * y + c) * cols, cols)
+        own = p_ref[zs[d], side, :, pl.ds(mine, cols)].astype(F32)
+        return own + pc[d, y, side].astype(F32) + py[d, side].astype(F32)
+
+    def p_x(d):
+        pyc[d].wait_recv()
+        pt[depth + d, 0] = p_half(d, 1 - x).astype(BF16)
+        pxc[d] = go(pt.at[depth + d, 0], px.at[d], pxs.at[d], pxr.at[d], xpeer)
+
+    def p_z(d):
+        pxc[d].wait_recv()
+        pt[depth + d, 1] = (p_half(d, x) + px[d].astype(F32)).astype(BF16)
+        if d:
+            pzc[d] = go(pt.at[depth + d, 1], pz.at[d - 1], pzs.at[d - 1], pzr.at[d - 1], zpeers[d])
+
+    def v_y():
+        vc[0].wait_recv()
+        vb[4] = v_ref[...] + vb[0]
+        vc[1] = go(vb.at[4], vb.at[1], vs.at[1], vr.at[1], ypeer)
+
+    def v_x():
+        vc[1].wait_recv()
+        vb[5] = vb[4] + vb[1]
+        vc[2] = go(vb.at[5], vb.at[2], vs.at[2], vr.at[2], xpeer)
+
+    def v_z():
+        vc[2].wait_recv()
+        vb[6] = vb[5] + vb[2]
+        for d in range(1, depth):
+            vc[2 + d] = go(vb.at[6], vb.at[6 + d], vs.at[2 + d], vr.at[2 + d], zpeers[d])
+
+    def v_end():
+        for d in range(1, depth):
+            vc[2 + d].wait_recv()
+        total = vb[6 + lax.rem(z, depth)]
+        for n in range(1, depth):
+            total += vb[6 + lax.rem(z - n + depth, depth)]
+        v_out[...] = total
+
+    todo = [lambda d=d: p_y(d) for d in order] + [v_y]
+    late = [lambda: p_x(order[0]), v_x, lambda: p_x(order[1]), lambda: p_z(order[0]), v_z]
+    late += [lambda: p_x(order[2]), lambda: p_z(order[1]), lambda: p_x(order[3]), lambda: p_z(order[2]), lambda: p_z(order[3]), v_end]
+    for k in range(chunks):
+        g_step(k)
+        if k >= 2:
+            g_end(k - 2)
+        for _ in range(2):
+            if todo:
+                todo.pop(0)()
+            elif k >= 4 and late:
+                late.pop(0)()
+    for step in todo + late:
+        step()
+    g_end(chunks - 2)
+    g_end(chunks - 1)
+    total = pt[depth, 1].astype(F32)
+    for d in range(1, depth):
+        pzc[d].wait_recv()
+        total += pz[d - 1].astype(F32)
+    p_out[...] = total
+    for copy in started:
+        copy.wait_send()
+
+
+def reduce_all(gs, p, v, width):
+    seq, slot = gs[0].shape[:2]
+    depth = seq // 2
+    rows, model_width = p.shape[1:]
+    cols = model_width // 4
+    widths = tuple(g.shape[2] for g in gs)
+    chunks = sum(widths) // width
+    dma = pltpu.SemaphoreType.DMA
+    n = len(gs)
+
+    def kernel(*refs):
+        reduce_kernel(depth, widths, refs[:n], refs[n], refs[n + 1], refs[n + 2 : 2 * n + 2], *refs[2 * n + 2 :])
+
+    vm = pl.BlockSpec(memory_space=pltpu.VMEM)
+    out = pl.pallas_call(
+        kernel,
+        name="reduce_all",
+        out_shape=[jax.ShapeDtypeStruct((slot, total), F32) for total in widths]
+        + [jax.ShapeDtypeStruct((rows, cols), F32), jax.ShapeDtypeStruct(v.shape, F32)],
+        in_specs=[vm] * (n + 2),
+        out_specs=[vm] * (n + 2),
+        scratch_shapes=[
+            pltpu.VMEM((chunks, depth, slot, width), BF16),
+            pltpu.VMEM((chunks, depth, slot, width), BF16),
+            pltpu.VMEM((chunks, depth - 1, slot, width), BF16),
+            pltpu.VMEM((depth, 2, 2, rows, cols), BF16),
+            pltpu.VMEM((depth, 2, rows, cols), BF16),
+            pltpu.VMEM((depth, rows, cols), BF16),
+            pltpu.VMEM((2 * depth, 2, rows, cols), BF16),
+            pltpu.VMEM((depth - 1, rows, cols), BF16),
+            pltpu.VMEM((6 + depth,) + v.shape, F32),
+            dma((chunks,)), dma((chunks,)), dma((chunks, depth - 1)), dma((chunks, depth - 1)),
+            dma((depth, 2)), dma((depth, 2)), dma((depth,)), dma((depth,)), dma((depth,)), dma((depth,)),
+            dma((depth - 1,)), dma((depth - 1,)), dma((2 + depth,)), dma((2 + depth,)),
+        ],
+        compiler_params=pltpu.CompilerParams(collective_id=1, has_side_effects=True, vmem_limit_bytes=60 << 20),
+    )(*[g.reshape(depth, 2, slot, -1) for g in gs], p.reshape(depth, 2, rows, model_width), v)
+    return out[:n], out[n], out[n + 1]
+
+
+def reduce_plain(gs, p, v, width):
+    gs = [lax.psum_scatter(g, "seq", scatter_dimension=0, tiled=False).astype(F32) for g in gs]
+    p = lax.psum_scatter(p, "seq", scatter_dimension=0, tiled=False)
+    p = lax.psum_scatter(p, "wt", scatter_dimension=1, tiled=True).astype(F32)
+    return gs, p, lax.psum(v, ("seq", "wt"))
 
 
 def passed_along(block, axis, distance):
@@ -111,13 +312,15 @@
     cotangent = masked_diff * (all_slots / valid_total)
     cot_all = lax.all_gather(cotangent.astype(jnp.bfloat16), "wt", axis=0, tiled=True)
     grad_down = jnp.einsum("td,tf->df", cot_all, hidden, preferred_element_type=jnp.float32)
-    grad_down = lax.psum_scatter(grad_down.astype(jnp.bfloat16), "seq", scatter_dimension=0, tiled=True)
+    grad_down = grad_down.astype(jnp.bfloat16)
     grad_hidden = jnp.einsum("td,fd->tf", cot_all, w_down, preferred_element_type=jnp.float32)
     grad_gu = act_pull(grad_hidden)[0].astype(jnp.bfloat16)
     norm_two_low = jnp.einsum("tgf,dgf->td", grad_gu, w_in, preferred_element_type=jnp.float32).astype(jnp.bfloat16)
     grad_norm_two = lax.psum_scatter(norm_two_low, "wt", scatter_dimension=0, tiled=True).astype(jnp.float32)
-    grad_in = jnp.einsum("td,tgf->dgf", normed_all, grad_gu, preferred_element_type=jnp.float32)
-    grad_in = lax.psum_scatter(grad_in.astype(jnp.bfloat16), "seq", scatter_dimension=0, tiled=True)
+    grad_gate, grad_up = (
+        jnp.einsum("td,tf->df", normed_all, grad_gu[:, half], preferred_element_type=jnp.float32).astype(jnp.bfloat16)
+        for half in range(2)
+    )
     grad_middle_norm, grad_gain_ffn = norm_two_pull(grad_norm_two)
     grad_middle = cotangent + grad_middle_norm
     grad_mid_low = grad_middle.astype(jnp.bfloat16)
@@ -169,27 +372,30 @@
     grad_normed = jnp.einsum("te,de->td", grad_qkv, attn_full, preferred_element_type=jnp.float32)
     grad_input_norm, grad_gain_attn = norm_one_pull(grad_normed)
     grad_inputs = grad_middle + grad_input_norm
-    grad_keyvals = jnp.swapaxes(grad_attn[model_width:].reshape(2, seq_devices, HD // seq_devices, model_width), 0, 1)
-    slot = model_width // seq_devices
+    slot, kv_slot = model_width // seq_devices, HD // seq_devices
+    grad_attn = grad_attn.astype(jnp.bfloat16)
+    grad_key, grad_value = (
+        grad_attn[model_width + at : model_width + at + HD].reshape(seq_devices, kv_slot, model_width) for at in (0, HD)
+    )
     packed = jnp.concatenate(
         [
             grad_attn[:model_width].reshape(seq_devices, slot, model_width),
-            grad_keyvals.reshape(seq_devices, 2 * HD // seq_devices, model_width),
-            grad_out.reshape(seq_devices, slot, model_width),
+            grad_key,
+            grad_value,
+            grad_out.astype(jnp.bfloat16).reshape(seq_devices, slot, model_width),
         ],
         axis=1,
-    ).astype(jnp.bfloat16)
-    packed = packed.reshape(seq_devices, 2 * slot + 2 * HD // seq_devices, lax.axis_size("wt"), -1)
-    packed = lax.psum_scatter(packed, "seq", scatter_dimension=0, tiled=False)
-    packed = lax.psum_scatter(packed, "wt", scatter_dimension=1, tiled=False).astype(jnp.float32)
+    )
+    small = jnp.stack([grad_gain_attn, grad_gain_ffn, jnp.full((model_width,), squares)] + [jnp.zeros_like(grad_gain_attn)] * 5)
+    ffn_grads = [part.reshape(seq_devices, slot, -1) for part in (grad_down, grad_gate, grad_up)]
+    reduce = reduce_all if slot % 16 == 0 and kv_slot % 16 == 0 else reduce_plain
+    (grad_down, grad_gate, grad_up), packed, small = reduce(ffn_grads, packed, small, 384)
     grad_queries = packed[:slot].T
-    grad_keyvals = packed[slot:-slot].T.reshape(-1, 2, HD // seq_devices)
+    grad_keyvals = packed[slot:-slot].T.reshape(-1, 2, kv_slot)
     grad_out = packed[-slot:].T
-    grad_down = grad_down.astype(jnp.float32).T
-    grad_in = grad_in.astype(jnp.float32)
-    squares_all, gain_attn_all, gain_ffn_all = lax.psum(
-        (squares, grad_gain_attn, grad_gain_ffn), ("seq", "wt")
-    )
+    grad_down = grad_down.T
+    grad_in = jnp.stack([grad_gate, grad_up], axis=1)
+    gain_attn_all, gain_ffn_all, squares_all = small[0], small[1], small[2, 0]
     loss = squares_all / (valid_total * model_width)
     return (
         output.astype(jnp.bfloat16)[None],

time: 1050 us -> 806 us (0.77)
  waiting for transfers between devices: 582 us -> 218 us
  Pallas kernels: 0 us -> 188 us
  blocking collectives: 48.2 us -> 5.77 us
    reduce_scatter x4 -> x0, waiting for transfers between devices: 329 us -> none  [the longest x1 146 us: per_device(): packed = lax.psum_scatter(packed, 'seq', scatter_dimension=0, tiled=False)]
    pallas_call x0 -> x1, Pallas kernels: none -> 188 us  [reduce_all(): pl.pallas_call(kernel, name='reduce_all', out_shape=[jax.ShapeDtypeStruct...]
    psum x1 -> x0, blocking collectives: 42.5 us -> none  [per_device(): lax.psum((squares, grad_gain_attn, grad_gain_ffn), ('seq', 'wt'))]
    reduce_scatter x1, waiting for transfers between devices: 58 us -> 19.8 us  [per_device(): lax.psum_scatter(norm_two_low, 'wt', scatter_dimension=0, tiled=True)]
    concatenate x4 -> x0, local copies, waits for them, and re-layouts: 16.8 us -> none  [per_device(): jnp.concatenate([grad_attn[:model_width].reshape(seq_devices, slot, model...]
    dot_general x1 -> x2, matrix products: 22.4 us -> 24.2 us  [per_device(): jnp.einsum('td,tf->df', normed_all, grad_gu[:, half], preferred_element_t...]
  transfers between devices with their start and end apart: 14 -> 10, of which waited for: 12 -> 8; matrix products, arithmetic and copies ran while one was open for 13% -> 14% of each run, Pallas kernels for 0% -> 0%
where the time goes in v2:
time: 806 us; the launch traced here: 802 us
  matrix products  239 us (30%)
  waiting for transfers between devices  218 us (27%)
  Pallas kernels  188 us (23%)
  other arithmetic  87.2 us (11%)
  local copies, waits for them, and re-layouts  34.6 us (4%)
  between operations  18.7 us (2%)
  starting transfers between devices  11.2 us (1%)
    pallas_call x1, Pallas kernels, reduce_all(): pl.pallas_call(kernel, name='reduce_all', out_shape=[jax.ShapeDtypeStruct...  188 us
    reduce_scatter x1, waiting for transfers between devices, per_device(): ffn_part = lax.psum_scatter(ffn_low, 'wt', scatter_dimension=0, tiled=True)  51.6 us
    all_gather x1, waiting for transfers between devices, per_device(): normed_all = lax.all_gather(normed_two, 'wt', axis=0, tiled=True)  47.3 us
    all_gather x1, waiting for transfers between devices, per_device(): lax.all_gather(cotangent.astype(jnp.bfloat16), 'wt', axis=0, tiled=True)  46.9 us
    all_gather x1, waiting for transfers between devices, per_device(): lax.all_gather(w_attn, 'wt', axis=0, tiled=True)  40.1 us
    convert_element_type x1, other arithmetic, backward_block(): grad_scores_low = grad_scores.astype(jnp.bfloat16)  31.4 us
    dot_general x1, matrix products, backward_block(): jnp.einsum('qhe,ke->hqk', grad_mixed, window[:, HD:], preferred_element_t...  30.7 us
    dot_general x2, matrix products, per_device(): jnp.einsum('td,tf->df', normed_all, grad_gu[:, half], preferred_element_t...  24.2 us
  transfers between devices with their start and end apart: 10, of which 8 were waited for; matrix products, arithmetic and copies ran while one was open for 14% of the time, Pallas kernels for 0%

profile of v2, /device:TPU:11, one launch (start us, length us, event | category | flops | bytes accessed | tf_op | source)
XLA Modules:
  0.0 802.2 jit_solution(4922486365053119558)
XLA Ops:
  13.0 40.1 %all-gather.5.cloned.1.call-done = bf16[1536,1792]{1,0:T(8,128)(2,1)} async-done(((bf16[384,1792]{1,0:T(8,128)(2,1)}), bf16[1536,1792]{1,0:T(8,128)(2,1)}) %all-gather.5.cloned.1.call-update) | async-done | bytes 5505040 | tf_op jit(solution)/shard_map/all_gather | solution.py:265
  76.6 17.2 %fusion.4 = (f32[12,512]{1,0:T(8,128)S(1)}, f32[1536,512,12]{1,0,2:T(8,128)}) fusion(pred[512,1536]{0,1:T(8,128)(4,1)} %fusion.33, bf16[512,12,128]{0,2,1:T(8,128)(2,1)} %bitcast.156, bf16[1536,256]{1,0:T(8,128)(2,1)S(1)} %pad_maximum_fusion.5), kind=kOutput, calls=%fused_computation.9 | convolution fusion | flops 2444224512 | bytes 40525824 | tf_op jit(solution)/shard_map/while/body/eval_jaxpr/qhe,ke->hqk/dot_general | solution.py:280
  93.8 16.0 %exponential_reduce_fusion = f32[12,512]{1,0:T(8,128)S(1)} fusion(f32[1536,512,12]{1,0,2:T(8,128)} %get-tuple-element.100, f32[12,512]{1,0:T(8,128)S(1)} %get-tuple-element.99, pred[512,1536]{0,1:T(8,128)(4,1)S(1)} %copy-done.5), kind=kLoop, calls=%fused_computation.7 | loop fusion | flops 37742592 | bytes 38584320 | tf_op jit(solution)/shard_map/while/body/eval_jaxpr/reduce_sum | solution.py:290
  110.5 17.8 %convolution_convert_fusion.8 = bf16[128,12,512]{2,0,1:T(8,128)(2,1)} fusion(bf16[1536,256]{1,0:T(8,128)(2,1)} %copy-done.19, f32[1536,512,12]{1,0,2:T(8,128)} %get-tuple-element.100, f32[12,512]{1,0:T(8,128)} %log_add_fusion, pred[512,1536]{0,1:T(8,128)(4,1)} %fusion.33), kind=kOutput, calls=%fused_computation.87 | convolution fusion | flops 2454454272 | bytes 40534016 | tf_op jit(solution)/shard_map/while/body/eval_jaxpr/hqk,ke->qhe/dot_general | solution.py:292
  128.4 6.3 multiply_reduce_fusion
  137.9 47.3 %all-gather.9.cloned.1.call-done = bf16[2048,1536]{1,0:T(8,128)(2,1)} async-done(((bf16[512,1536]{1,0:T(8,128)(2,1)}), bf16[2048,1536]{1,0:T(8,128)(2,1)}) %all-gather.9.cloned.1.call-update) | async-done | bytes 6291472 | tf_op jit(solution)/shard_map/all_gather | solution.py:302
  185.2 19.6 %fusion.12 = f32[2048,2,1152]{2,0,1:T(8,128)S(1)} fusion(bf16[2048,1536]{1,0:T(8,128)(2,1)} %all-gather.9.cloned.1.call-done, bf16[1536,2,1152]{2,1,0:T(2,128)(2,1)} %param.14), kind=kOutput, calls=%fused_computation.33 | convolution fusion | flops 14495514624 | bytes 32243712 | tf_op jit(solution)/shard_map/td,dgf->tgf/dot_general | solution.py:303
  213.2 10.1 %convolution_convert_fusion.5 = bf16[2048,1536]{1,0:T(8,128)(2,1)} fusion(bf16[2048,1152]{1,0:T(8,128)(2,1)S(1)} %multiply_convert_fusion, bf16[1152,1536]{1,0:T(8,128)(2,1)S(1)} %copy-done), kind=kOutput, calls=%fused_computation.32 | convolution fusion | flops 7250903040 | bytes 14548992 | tf_op jit(solution)/shard_map/dot_general | solution.py:306
  229.9 51.6 %reduce-scatter.3.cloned.1.call-done = bf16[512,1536]{1,0:T(8,128)(2,1)} async-done(((bf16[2048,1536]{1,0:T(8,128)(2,1)}), bf16[512,1536]{1,0:T(8,128)(2,1)}) %reduce-scatter.3.cloned.1.call-update) | async-done | bytes 1572880 | tf_op jit(solution)/shard_map/reduce_scatter | solution.py:307
  286.2 46.9 %all-gather.11.cloned.1.call-done = bf16[2048,1536]{1,0:T(8,128)(2,1)} async-done(((bf16[512,1536]{1,0:T(8,128)(2,1)}), bf16[2048,1536]{1,0:T(8,128)(2,1)}) %all-gather.11.cloned.1.call-update) | async-done | bytes 6291472 | tf_op jit(solution)/shard_map/all_gather | solution.py:313
  333.1 23.8 %multiply_bitcast_fusion = (f32[2048,1,1152]{2,0,1:T(8,128)}, f32[2048,1,1152]{2,0,1:T(8,128)}) fusion(f32[2048,2,1152]{2,0,1:T(8,128)} %copy-done.7, bf16[2048,1536]{1,0:T(8,128)(2,1)} %all-gather.11.cloned.1.call-done, bf16[1152,1536]{1,0:T(8,128)(2,1)S(1)} %copy-done), kind=kOutput, calls=%fused_computation.24 | convolution fusion | flops 7299661824 | bytes 47579136 | tf_op jit(solution)/shard_map/td,fd->tf/dot_general | solution.py:316
  357.0 7.3 add_convert_fusion
  367.9 19.0 %bitcast_convert_fusion = bf16[2048,1536]{1,0:T(8,128)(2,1)} fusion(bf16[2048,2,1152]{2,0,1:T(8,128)(2,1)S(1)} %add_convert_fusion, bf16[1536,2,1152]{2,1,0:T(2,128)(2,1)} %param.14), kind=kOutput, calls=%fused_computation.13 | convolution fusion | flops 14498660352 | bytes 22806528 | tf_op jit(solution)/shard_map/tgf,dgf->td/dot_general | solution.py:318
  387.6 13.4 %convolution_convert_fusion.4 = bf16[1536,1152]{1,0:T(8,128)(2,1)} fusion(bf16[2048,1536]{1,0:T(8,128)(2,1)} %all-gather.11.cloned.1.call-done, bf16[2048,1152]{1,0:T(8,128)(2,1)} %copy-done.22), kind=kOutput, calls=%fused_computation.31 | convolution fusion | flops 7249526784 | bytes 14548992 | tf_op jit(solution)/shard_map/td,tf->df/dot_general | solution.py:314
  401.0 11.9 %convolution_convert_fusion.2 = bf16[1536,1152]{1,0:T(8,128)(2,1)} fusion(bf16[2048,1536]{1,0:T(8,128)(2,1)} %all-gather.9.cloned.1.call-done, bf16[2048,2,1152]{2,0,1:T(8,128)(2,1)S(1)} %copy-done.14), kind=kOutput, calls=%fused_computation.29 | convolution fusion | flops 7249526784 | bytes 14548992 | tf_op jit(solution)/shard_map/td,tf->df/dot_general | solution.py:321
  413.0 12.3 %convolution_convert_fusion.3 = bf16[1536,1152]{1,0:T(8,128)(2,1)} fusion(bf16[2048,1536]{1,0:T(8,128)(2,1)} %all-gather.9.cloned.1.call-done, bf16[2048,2,1152]{2,0,1:T(8,128)(2,1)S(1)} %copy-done.14), kind=kOutput, calls=%fused_computation.30 | convolution fusion | flops 7249526784 | bytes 14548992 | tf_op jit(solution)/shard_map/td,tf->df/dot_general | solution.py:321
  425.2 19.8 %reduce-scatter.5.cloned.1.call-done = bf16[512,1536]{1,0:T(8,128)(2,1)} async-done(((bf16[2048,1536]{1,0:T(8,128)(2,1)}), bf16[512,1536]{1,0:T(8,128)(2,1)}) %reduce-scatter.5.cloned.1.call-update) | async-done | bytes 1572880 | tf_op jit(solution)/shard_map/reduce_scatter | solution.py:319
  460.0 17.2 %convolution_bitcast_fusion = f32[1536,128]{0,1:T(8,128)} fusion(bf16[512,12,128]{0,2,1:T(8,128)(2,1)S(1)} %bitcast.154, f32[1536,512,12]{1,0,2:T(8,128)} %get-tuple-element.100, f32[12,512]{1,0:T(8,128)S(1)} %copy-done.25, pred[512,1536]{0,1:T(8,128)(4,1)S(1)} %copy-done.6), kind=kOutput, calls=%fused_computation.77 | convolution fusion | flops 2453667840 | bytes 40919040 | tf_op jit(solution)/shard_map/while/body/eval_jaxpr/hqk,qhe->ke/dot_general | solution.py:351
  477.2 30.7 %fusion = (f32[12,512]{1,0:T(8,128)S(1)}, f32[1536,512,12]{1,0,2:T(8,128)}) fusion(f32[1536,512,12]{1,0,2:T(8,128)} %get-tuple-element.100, f32[12,512]{1,0:T(8,128)S(1)} %copy-done.25, pred[512,1536]{0,1:T(8,128)(4,1)S(1)} %copy-done.6, bf16[512,12,128]{0,2,1:T(8,128)(2,1)S(1)} %bitcast.155, bf16[1536,256]{1,0:T(8,128)(2,1)S(1)} %copy-done.20), kind=kOutput, calls=%fused_computation.2 | convolution fusion | flops 2463098880 | bytes 78307328 | tf_op jit(solution)/shard_map/while/body/eval_jaxpr/qhe,ke->hqk/dot_general | solution.py:336
  507.9 31.4 %fusion.2 = bf16[12,512,1536]{1,2,0:T(8,128)(2,1)} fusion(f32[1536,512,12]{1,0,2:T(8,128)} %get-tuple-element.104, f32[1536,512,12]{1,0,2:T(8,128)} %get-tuple-element.100, f32[12,512]{1,0:T(8,128)S(1)} %get-tuple-element.103, f32[12,512]{1,0:T(8,128)S(1)} %copy-done.25, pred[512,1536]{0,1:T(8,128)(4,1)S(1)} %copy-done.6), kind=kLoop, calls=%fused_computation.4 | loop fusion | flops 56623104 | bytes 95207424 | tf_op jit(solution)/shard_map/while/body/eval_jaxpr/convert_element_type | solution.py:340
  539.3 10.1 %fusion.35 = f32[1536,128]{0,1:T(8,128)S(1)} fusion(bf16[12,512,1536]{1,2,0:T(8,128)(2,1)} %fusion.2, bf16[512,12,128]{0,2,1:T(8,128)(2,1)S(1)} %bitcast.157), kind=kOutput, calls=%fused_computation.79 | convolution fusion | flops 2416115712 | bytes 21233664 | tf_op jit(solution)/shard_map/while/body/eval_jaxpr/hqk,qhe->ke/dot_general | solution.py:348
  563.2 6.5 collective-permute-done.2
  575.6 7.9 fusion.29
  589.7 188.1 %reduce_all.1 = (f32[192,1152]{1,0:T(8,128)}, f32[192,1152]{1,0:T(8,128)}, f32[192,1152]{1,0:T(8,128)}, f32[416,384]{1,0:T(8,128)}, f32[8,1536]{1,0:T(8,128)}) custom-call(bf16[4,2,192,1152]{3,2,1,0:T(8,128)(2,1)} %bitcast.159, bf16[4,2,192,1152]{3,2,1,0:T(8,128)(2,1)} %bitcast.161, bf16[4,2,192,1152]{3,2,1,0:T(8,128)(2,1)} %bitcast.160, ...), custom_call_target="tpu_custom_call" | custom-call | tf_op jit(solution)/shard_map/reduce_all/pallas_call | solution.py:186
  (145 shorter events, 111.1 us)
Async XLA Ops:
  7.2 206.1 %copy-start = (bf16[1152,1536]{1,0:T(8,128)(2,1)S(1)}, bf16[1152,1536]{1,0:T(8,128)(2,1)}, u32[]{:S(2)}) copy-start(bf16[1152,1536]{1,0:T(8,128)(2,1)} %param.15) | copy-start | bytes 10616836
  7.2 45.9 %all-gather.5.cloned.1.call-start = ((), (), s32[]{:S(2)}) async-start(), calls=%async_computation.2 | async-start | bytes 6881280 | tf_op jit(solution)/shard_map/all_gather | solution.py:265
  7.9 120.4 %all-gather.7.cloned.1.call-start = ((), (), s32[]{:S(2)}) async-start(), calls=%async_computation.3 | async-start | bytes 5898240 | tf_op jit(solution)/shard_map/all_gather | solution.py:266
  8.7 176.5 %all-gather.9.cloned.1.call-start = ((), (), s32[]{:S(2)}) async-start(), calls=%async_computation.4 | async-start | bytes 7864320 | tf_op jit(solution)/shard_map/all_gather | solution.py:302
  60.0 12.4 %collective-permute-start.1 = (bf16[512,256]{1,0:T(8,128)(2,1)}, bf16[512,256]{1,0:T(8,128)(2,1)}, u32[]{:S(2)}, u32[]{:S(2)}) collective-permute-start(bf16[512,256]{1,0:T(8,128)(2,1)} %slice.89), channel_id=1, source_target_pairs={{0,4},{4,8},{8,12},{12,16},{16,20},{20,24},{24,28},{1,5},{5,9},{9,... | collective-permute-start | bytes 786440 | tf_op jit(solution)/shard_map/ppermute | solution.py:222
  63.1 12.4 %collective-permute-start = (bf16[512,256]{1,0:T(8,128)(2,1)}, bf16[512,256]{1,0:T(8,128)(2,1)}, u32[]{:S(2)}, u32[]{:S(2)}) collective-permute-start(bf16[512,256]{1,0:T(8,128)(2,1)} %slice.89), channel_id=1, source_target_pairs={{0,8},{4,12},{8,16},{12,20},{16,24},{20,28},{1,9},{5,13},{9,17},{1... | collective-permute-start | bytes 786440 | tf_op jit(solution)/shard_map/ppermute | solution.py:222
  76.6 17.2 %copy-start.19 = (bf16[1536,256]{1,0:T(8,128)(2,1)}, bf16[1536,256]{1,0:T(8,128)(2,1)S(1)}, u32[]{:S(2)}) copy-start(bf16[1536,256]{1,0:T(8,128)(2,1)S(1)} %pad_maximum_fusion.5) | copy-start | bytes 2359300
  76.6 17.2 %copy-start.5 = (pred[512,1536]{0,1:T(8,128)(4,1)S(1)}, pred[512,1536]{0,1:T(8,128)(4,1)}, u32[]{:S(2)}) copy-start(pred[512,1536]{0,1:T(8,128)(4,1)} %fusion.33) | copy-start | bytes 2359300
  137.9 143.7 %reduce-scatter.3.cloned.1.call-start = ((), (), s32[]{:S(2)}) async-start(), calls=%async_computation.5 | async-start | bytes 7864320 | tf_op jit(solution)/shard_map/reduce_scatter | solution.py:307
  223.4 109.7 %all-gather.11.cloned.1.call-start = ((), (), s32[]{:S(2)}) async-start(), calls=%async_computation.6 | async-start | bytes 7864320 | tf_op jit(solution)/shard_map/all_gather | solution.py:313
  286.2 158.9 %reduce-scatter.5.cloned.1.call-start = ((), (), s32[]{:S(2)}) async-start(), calls=%async_computation.7 | async-start | bytes 7864320 | tf_op jit(solution)/shard_map/reduce_scatter | solution.py:319
  387.6 13.4 %copy-start.14 = (bf16[2048,2,1152]{2,0,1:T(8,128)(2,1)S(1)}, bf16[2048,2,1152]{2,0,1:T(8,128)(2,1)}, u32[]{:S(2)}) copy-start(bf16[2048,2,1152]{2,0,1:T(8,128)(2,1)} %copy-done.13) | copy-start | bytes 28311556
  412.9 32.1 %copy-start.4 = (f32[512,1536]{1,0:T(8,128)S(1)}, f32[512,1536]{1,0:T(8,128)}, u32[]{:S(2)}) copy-start(f32[512,1536]{1,0:T(8,128)} %copy-done.3) | copy-start | bytes 9437188
  412.9 32.1 %copy-start.27 = (f32[1536]{0:T(1024)S(1)}, f32[1536]{0:T(1024)}, u32[]{:S(2)}) copy-start(f32[1536]{0:T(1024)} %param.17) | copy-start | bytes 18436
  413.0 32.1 %copy-start.29 = (f32[512]{0:T(512)S(1)}, f32[512]{0:T(512)}, u32[]{:S(2)}) copy-start(f32[512]{0:T(512)} %copy-done.28) | copy-start | bytes 6148
  425.2 24.5 %copy-start.35 = (f32[512]{0:T(512)S(1)}, f32[512]{0:T(512)}, u32[]{:S(2)}) copy-start(f32[512]{0:T(512)} %copy-done.34) | copy-start | bytes 6148
  460.0 17.2 %copy-start.20 = (bf16[1536,256]{1,0:T(8,128)(2,1)S(1)}, bf16[1536,256]{1,0:T(8,128)(2,1)}, u32[]{:S(2)}) copy-start(bf16[1536,256]{1,0:T(8,128)(2,1)} %copy-done.19) | copy-start | bytes 2359300
  507.9 31.4 %copy-start.15 = (bf16[512,1536]{0,1:T(8,128)(2,1)S(1)}, bf16[512,1536]{0,1:T(8,128)(2,1)}, u32[]{:S(2)}) copy-start(bf16[512,1536]{0,1:T(8,128)(2,1)} %copy.32) | copy-start | bytes 4718596
  554.1 15.6 %collective-permute-start.2 = (f32[512,256]{0,1:T(8,128)S(1)}, f32[512,256]{0,1:T(8,128)S(1)}, u32[]{:S(2)}, u32[]{:S(2)}) collective-permute-start(f32[512,256]{0,1:T(8,128)S(1)} %get-tuple-element.95), channel_id=1, source_target_pairs={{4,0},{8,4},{12,8},{16,12},{20,16},{24,20},{28,24},{5,1},{9,5},{13... | collective-permute-start | bytes 1572872 | tf_op jit(solution)/shard_map/ppermute | solution.py:222
  556.3 14.7 %copy-start.16 = (bf16[1,512,1536]{2,1,0:T(8,128)(2,1)S(1)}, bf16[1,512,1536]{2,1,0:T(8,128)(2,1)}, u32[]{:S(2)}) copy-start(bf16[1,512,1536]{2,1,0:T(8,128)(2,1)} %param.9) | copy-start | bytes 4718596
  556.3 14.7 %copy-start.32 = (f32[512]{0:T(512)S(1)}, f32[512]{0:T(512)}, u32[]{:S(2)}) copy-start(f32[512]{0:T(512)} %fusion.55) | copy-start | bytes 6148
  556.3 14.7 %copy-start.36 = (f32[1536]{0:T(1024)S(1)}, f32[1536]{0:T(1024)}, u32[]{:S(2)}) copy-start(f32[1536]{0:T(1024)} %param.16) | copy-start | bytes 18436
  556.3 14.5 %collective-permute-start.3 = (f32[512,256]{0,1:T(8,128)S(1)}, f32[512,256]{0,1:T(8,128)S(1)}, u32[]{:S(2)}, u32[]{:S(2)}) collective-permute-start(f32[512,256]{0,1:T(8,128)S(1)} %get-tuple-element.96), channel_id=1, source_target_pairs={{8,0},{12,4},{16,8},{20,12},{24,16},{28,20},{9,1},{13,5},{17,9},{2... | collective-permute-start | bytes 1572872 | tf_op jit(solution)/shard_map/ppermute | solution.py:222
  589.7 194.9 %copy-start.31 = (f32[512]{0:T(512)S(1)}, f32[512]{0:T(512)}, u32[]{:S(2)}) copy-start(f32[512]{0:T(512)} %copy-done.30) | copy-start | bytes 6148
  (25 other events, 150.2 us)
Sparse Core Ops, SparseCore 0:
  9.6 43.4 all-gather.4
  54.7 37.4 all-gather.6
  138.0 47.1 all-gather.8
  223.5 57.9 reduce-scatter.2
  286.3 46.7 all-gather.10
  387.0 57.9 reduce-scatter.4

commit v3 on v2

--- a/solution.py
+++ b/solution.py
@@ -169,27 +169,30 @@
         copy.wait_send()
 
 
-def reduce_all(gs, p, v, width):
-    seq, slot = gs[0].shape[:2]
+def reduce_all(gd, gi, p, v, width):
+    seq, slot, units = gd.shape
     depth = seq // 2
     rows, model_width = p.shape[1:]
     cols = model_width // 4
-    widths = tuple(g.shape[2] for g in gs)
-    chunks = sum(widths) // width
+    chunks = 3 * units // width
     dma = pltpu.SemaphoreType.DMA
-    n = len(gs)
-
-    def kernel(*refs):
-        reduce_kernel(depth, widths, refs[:n], refs[n], refs[n + 1], refs[n + 2 : 2 * n + 2], *refs[2 * n + 2 :])
+
+    def kernel(gd_ref, gi_ref, p_ref, v_ref, gd_out, gi_out, *refs):
+        g_refs = (gd_ref, gi_ref.at[0], gi_ref.at[1])
+        reduce_kernel(depth, (units,) * 3, g_refs, p_ref, v_ref, (gd_out, gi_out.at[0], gi_out.at[1]), *refs)
 
     vm = pl.BlockSpec(memory_space=pltpu.VMEM)
-    out = pl.pallas_call(
+    return pl.pallas_call(
         kernel,
         name="reduce_all",
-        out_shape=[jax.ShapeDtypeStruct((slot, total), F32) for total in widths]
-        + [jax.ShapeDtypeStruct((rows, cols), F32), jax.ShapeDtypeStruct(v.shape, F32)],
-        in_specs=[vm] * (n + 2),
-        out_specs=[vm] * (n + 2),
+        out_shape=[
+            jax.ShapeDtypeStruct((slot, units), F32),
+            jax.ShapeDtypeStruct((2, slot, units), F32),
+            jax.ShapeDtypeStruct((rows, cols), F32),
+            jax.ShapeDtypeStruct(v.shape, F32),
+        ],
+        in_specs=[vm] * 4,
+        out_specs=[vm] * 4,
         scratch_shapes=[
             pltpu.VMEM((chunks, depth, slot, width), BF16),
             pltpu.VMEM((chunks, depth, slot, width), BF16),
@@ -205,15 +208,257 @@
             dma((depth - 1,)), dma((depth - 1,)), dma((2 + depth,)), dma((2 + depth,)),
         ],
         compiler_params=pltpu.CompilerParams(collective_id=1, has_side_effects=True, vmem_limit_bytes=60 << 20),
-    )(*[g.reshape(depth, 2, slot, -1) for g in gs], p.reshape(depth, 2, rows, model_width), v)
-    return out[:n], out[n], out[n + 1]
-
-
-def reduce_plain(gs, p, v, width):
-    gs = [lax.psum_scatter(g, "seq", scatter_dimension=0, tiled=False).astype(F32) for g in gs]
+    )(gd.reshape(depth, 2, slot, units), gi.reshape(2, depth, 2, slot, units), p.reshape(depth, 2, rows, model_width), v)
+
+
+def reduce_plain(gd, gi, p, v, width):
+    gd = lax.psum_scatter(gd, "seq", scatter_dimension=0, tiled=False).astype(F32)
+    gi = lax.psum_scatter(gi, "seq", scatter_dimension=1, tiled=False).astype(F32)
     p = lax.psum_scatter(p, "seq", scatter_dimension=0, tiled=False)
     p = lax.psum_scatter(p, "wt", scatter_dimension=1, tiled=True).astype(F32)
-    return gs, p, lax.psum(v, ("seq", "wt"))
+    return gd, gi, p, lax.psum(v, ("seq", "wt"))
+
+
+def contract(a, b, dim_a, dim_b):
+    return lax.dot_general(a, b, (((dim_a,), (dim_b,)), ((), ())), preferred_element_type=F32)
+
+
+def tiles(total, width, body):
+    def step(i, _):
+        body(pl.ds(pl.multiple_of(i * width, width), width))
+        return 0
+
+    lax.fori_loop(0, total // width, step, 0)
+
+
+def flat(block):
+    return block.reshape(-1, block.shape[-1])
+
+
+def ffn_kernel(h, wi_hbm, wd_hbm, mid_hbm, teacher_hbm, valid, scale, out, cot, dh, gd, gi, squares,
+               wi, wd, mid, teacher, hall, dall, act, hid, acc, far, out_low, sent, got, stage,
+               load, h_send, h_recv, d_send, d_recv, p_send, p_recv, store, g_store):
+    seq, wt = lax.axis_index("seq"), lax.axis_index("wt")
+    y, c = wt // 2, wt % 2
+    sib, peer = (seq, y * 2 + 1 - c), (seq, (1 - y) * 2 + c)
+    half, width = h.shape[1:]
+    units = wd.shape[0]
+
+    def fetch(src, dst, sem):
+        copy = pltpu.make_async_copy(src, dst, sem)
+        copy.start()
+        return copy
+
+    loads = [fetch(*pair, load.at[n]) for n, pair in enumerate(
+        ((h, hall.at[0]), (wi_hbm, wi), (wd_hbm, wd), (mid_hbm, mid), (teacher_hbm, teacher)))]
+    greet([sib, peer])
+    pending = []
+
+    def go(*args):
+        nonlocal pending
+        pending.append(remote(*args))
+        return pending[-1]
+
+    def spread(src, dst, send, recv, j):
+        a = go(src.at[j], dst.at[2, j], send.at[0, j], recv.at[0, j], peer)
+        b = go(src.at[j], dst.at[1, j], send.at[1, j], recv.at[1, j], sib)
+        return a, b
+
+    def relay(dst, send, recv, j):
+        return go(dst.at[2, j], dst.at[3, j], send.at[2, j], recv.at[2, j], sib)
+
+    def group(ref, g):
+        return ref.at[2:4, g - 2] if g >= 2 else ref.at[g]
+
+    h_copies = [spread(h, hall, h_send, h_recv, j) for j in range(2)]
+
+    def gated(g):
+        rows = flat(group(hall, g)[...])
+
+        def body(cols):
+            gate = contract(rows, wi[0, :, cols], 1, 0)
+            up = contract(rows, wi[1, :, cols], 1, 0)
+            square = gate * gate
+            turn = jnp.tanh(gate * (0.7978845608028654 + 0.035677408136300125 * square))
+            upper = 0.5 + 0.5 * turn
+            value = gate * upper
+            slope = upper + 0.5 * gate * (1.0 - turn * turn) * (0.7978845608028654 + 0.10703222440890038 * square)
+            shape = (2, half, up.shape[-1])
+            group(hid, g)[:, :, cols] = (value * up).astype(BF16).reshape(shape)
+            group(act.at[0], g)[:, :, cols] = (slope * up).astype(BF16).reshape(shape)
+            group(act.at[1], g)[:, :, cols] = value.astype(BF16).reshape(shape)
+
+        tiles(units, 384, body)
+
+    def emit(g, cols, part):
+        if g == 0:
+            acc[:, :, cols] = part.reshape(2, half, -1)
+        elif g == 1:
+            sent[0, :, :, cols] = part.astype(BF16).reshape(2, half, -1)
+        else:
+            far[:, cols] = part[:half]
+            sent[1, g - 2, :, cols] = part[half:].astype(BF16)
+
+    def down(g):
+        rows = flat(group(hid, g)[...])
+        tiles(width, 512, lambda cols: emit(g, cols, contract(rows, wd[:, cols], 1, 0)))
+
+    def push(phase, kind, j):
+        return go(sent.at[kind, j], got.at[kind, j], p_send.at[phase, kind, j], p_recv.at[phase, kind, j], peer if kind == 2 else sib)
+
+    def sums(phase, compute, copies, buffer, send, recv, before):
+        kept = {}
+        compute(0)
+        for j in range(2):
+            copies[j][1].wait_recv()
+        compute(1)
+        for j in range(2):
+            kept[0, j] = push(phase, 0, j)
+        for j in range(2):
+            copies[j][0].wait_recv()
+            passed = relay(buffer, send, recv, j)
+            passed.wait_recv()
+            compute(2 + j)
+            kept[1, j] = push(phase, 1, j)
+            kept[1, j].wait_recv()
+            sent[2, j] = (far[...] + got[1, j].astype(F32)).astype(BF16)
+            kept[2, j] = push(phase, 2, j)
+        return kept
+
+    def forward(g):
+        gated(g)
+        down(g)
+
+    for one in loads[:3]:
+        one.wait()
+    kept = sums(0, forward, h_copies, hall, h_send, h_recv, None)
+    first, pending = pending, []
+    loads[3].wait()
+    loads[4].wait()
+    total = jnp.zeros((), F32)
+    d_copies, saves = [], []
+    factor = scale[0, 0]
+    for j in range(2):
+        kept[0, j].wait_recv()
+        kept[2, j].wait_recv()
+        step = half // 4
+
+        def rows_of(i, so_far):
+            r = pl.ds(pl.multiple_of(i * step, step), step)
+            value = mid[j, r, :] + acc[j, r, :] + got[0, j, r, :].astype(F32) + got[2, j, r, :].astype(F32)
+            out_low[j, r, :] = value.astype(BF16)
+            diff = value - teacher[j, r, :].astype(F32)
+            masked = valid[j, r, :] * diff
+            grad = masked * factor
+            mid[j, r, :] = grad
+            dall[0, j, r, :] = grad.astype(BF16)
+            return so_far + jnp.sum(masked * diff)
+
+        total = lax.fori_loop(0, 4, rows_of, total)
+        d_copies.append(spread(dall.at[0], dall, d_send, d_recv, j))
+        saves.append(fetch(out_low.at[j], out.at[j], store.at[0, j]))
+        saves.append(fetch(mid.at[j], cot.at[j], store.at[1, j]))
+    squares[...] = jnp.full(squares.shape, total)
+
+    def backward(g):
+        rows = flat(group(dall, g)[...])
+
+        def body(cols):
+            grad = contract(rows, wd[cols, :], 1, 1).reshape(2, half, -1)
+            for n in range(2):
+                part = group(act.at[n], g)
+                part[:, :, cols] = (grad * part[:, :, cols].astype(F32)).astype(BF16)
+
+        tiles(units, 384, body)
+        gate, up = flat(group(act.at[0], g)[...]), flat(group(act.at[1], g)[...])
+        tiles(width, 512, lambda cols: emit(g, cols, contract(gate, wi[0, cols, :], 1, 1) + contract(up, wi[1, cols, :], 1, 1)))
+
+    for copy in first:
+        copy.wait_send()
+    kept = sums(1, backward, d_copies, dall, d_send, d_recv, None)
+    count = 0
+    blocks = width // 256
+    left, right = {}, {}
+
+    def weight(left, right, target):
+        def body(i, _):
+            for n in range(2):
+                at = pl.ds(pl.multiple_of(i * 512 + n * 256, 256), 256)
+
+                @pl.when(i > 0)
+                def _():
+                    pltpu.make_async_copy(stage.at[n], target.at[at], g_store.at[n]).wait()
+
+                stage[n] = contract(left(at), right(), 0, 0).astype(BF16)
+                pltpu.make_async_copy(stage.at[n], target.at[at], g_store.at[n]).start()
+            return 0
+
+        lax.fori_loop(0, width // 512, body, 0)
+        for n in range(2):
+            pltpu.make_async_copy(stage.at[n], target.at[pl.ds(0, 256)], g_store.at[n]).wait()
+
+    weight(lambda at: flat(dall[:, :, :, at].reshape(4, 2 * half, 256)), lambda: flat(hid[...].reshape(4, 2 * half, units)), gd)
+    for n in range(2):
+        weight(lambda at: flat(hall[:, :, :, at].reshape(4, 2 * half, 256)), lambda n=n: flat(act[n].reshape(4, 2 * half, units)), gi.at[n])
+    for j in range(2):
+        kept[0, j].wait_recv()
+        kept[2, j].wait_recv()
+        saves[2 * j + 1].wait()
+
+        def sum_rows(i, _):
+            r = pl.ds(pl.multiple_of(i * step, step), step)
+            mid[j, r, :] = acc[j, r, :] + got[0, j, r, :].astype(F32) + got[2, j, r, :].astype(F32)
+            return 0
+
+        lax.fori_loop(0, 4, sum_rows, 0)
+        saves.append(fetch(mid.at[j], dh.at[j], store.at[2, j]))
+    for copy in pending:
+        copy.wait_send()
+    for n in (0, 2, 4, 5):
+        saves[n].wait()
+
+
+def ffn(h, wi, wd, mid, teacher, valid, scale):
+    rows, width = h.shape
+    units = wd.shape[0]
+    half = rows // 2
+    split = lambda a: a.reshape(2, half, a.shape[-1])
+    dma = pltpu.SemaphoreType.DMA
+    hbm, vm = pl.BlockSpec(memory_space=pl.ANY), pl.BlockSpec(memory_space=pltpu.VMEM)
+    out, cot, dh, gd, gi, squares = pl.pallas_call(
+        ffn_kernel,
+        name="ffn",
+        out_shape=[
+            jax.ShapeDtypeStruct((2, half, width), BF16),
+            jax.ShapeDtypeStruct((2, half, width), F32),
+            jax.ShapeDtypeStruct((2, half, width), F32),
+            jax.ShapeDtypeStruct((width, units), BF16),
+            jax.ShapeDtypeStruct((2, width, units), BF16),
+            jax.ShapeDtypeStruct((8, 128), F32),
+        ],
+        in_specs=[hbm] * 5 + [vm, pl.BlockSpec(memory_space=pltpu.SMEM)],
+        out_specs=[hbm] * 5 + [vm],
+        scratch_shapes=[
+            pltpu.VMEM((2, width, units), BF16),
+            pltpu.VMEM((units, width), BF16),
+            pltpu.VMEM((2, half, width), F32),
+            pltpu.VMEM((2, half, width), BF16),
+            pltpu.VMEM((4, 2, half, width), BF16),
+            pltpu.VMEM((4, 2, half, width), BF16),
+            pltpu.VMEM((2, 4, 2, half, units), BF16),
+            pltpu.VMEM((4, 2, half, units), BF16),
+            pltpu.VMEM((2, half, width), F32),
+            pltpu.VMEM((half, width), F32),
+            pltpu.VMEM((2, half, width), BF16),
+            pltpu.VMEM((3, 2, half, width), BF16),
+            pltpu.VMEM((3, 2, half, width), BF16),
+            pltpu.VMEM((2, 256, units), BF16),
+            dma((5,)), dma((3, 2)), dma((3, 2)), dma((3, 2)), dma((3, 2)),
+            dma((2, 3, 2)), dma((2, 3, 2)), dma((3, 2)), dma((2,)),
+        ],
+        compiler_params=pltpu.CompilerParams(collective_id=2, has_side_effects=True, vmem_limit_bytes=63 << 20),
+    )(split(h), wi, wd, split(mid), split(teacher), split(valid), scale)
+    return out.reshape(rows, width), cot.reshape(rows, width), dh.reshape(rows, width), gd, gi, squares[0, 0]
 
 
 def passed_along(block, axis, distance):
@@ -256,7 +501,6 @@
     edge_rows = reach_count * tok_rows
     scale = 1.0 / math.sqrt(HD)
     inputs = tokens[0].astype(jnp.float32)
-    target = teacher[0].astype(jnp.float32)
     positions = seq_place * tok_rows - edge_rows + jnp.arange(edge_rows + tok_rows, dtype=jnp.int32)
     seq_ids = stream_ids(positions, seq_lengths[0], stream_len)
     valid = (seq_ids[edge_rows:] >= 0).astype(jnp.float32)
@@ -299,27 +543,10 @@
     middle = inputs + jnp.dot(mixed_b, out_full, preferred_element_type=jnp.float32)
     normed_two_f, norm_two_pull = jax.vjp(rms_scale, middle, gain_ffn)
     normed_two = normed_two_f.astype(jnp.bfloat16)
-    normed_all = lax.all_gather(normed_two, "wt", axis=0, tiled=True)
-    gate_up = jnp.einsum("td,dgf->tgf", normed_all, w_in, preferred_element_type=jnp.float32)
-    hidden_f, act_pull = jax.vjp(gated_act, gate_up)
-    hidden = hidden_f.astype(jnp.bfloat16)
-    ffn_low = jnp.dot(hidden, w_down, preferred_element_type=jnp.float32).astype(jnp.bfloat16)
-    ffn_part = lax.psum_scatter(ffn_low, "wt", scatter_dimension=0, tiled=True)
-    output = middle + ffn_part.astype(jnp.float32)
-    diff = output - target
-    masked_diff = valid[:, None] * diff
-    squares = jnp.sum(masked_diff * diff)
-    cotangent = masked_diff * (all_slots / valid_total)
-    cot_all = lax.all_gather(cotangent.astype(jnp.bfloat16), "wt", axis=0, tiled=True)
-    grad_down = jnp.einsum("td,tf->df", cot_all, hidden, preferred_element_type=jnp.float32)
-    grad_down = grad_down.astype(jnp.bfloat16)
-    grad_hidden = jnp.einsum("td,fd->tf", cot_all, w_down, preferred_element_type=jnp.float32)
-    grad_gu = act_pull(grad_hidden)[0].astype(jnp.bfloat16)
-    norm_two_low = jnp.einsum("tgf,dgf->td", grad_gu, w_in, preferred_element_type=jnp.float32).astype(jnp.bfloat16)
-    grad_norm_two = lax.psum_scatter(norm_two_low, "wt", scatter_dimension=0, tiled=True).astype(jnp.float32)
-    grad_gate, grad_up = (
-        jnp.einsum("td,tf->df", normed_all, grad_gu[:, half], preferred_element_type=jnp.float32).astype(jnp.bfloat16)
-        for half in range(2)
+    scale_up = (all_slots / valid_total).reshape(1, 1)
+    w_pair = jnp.swapaxes(w_in, 0, 1)
+    output, cotangent, grad_norm_two, grad_down, grad_in, squares = ffn(
+        normed_two, w_pair, w_down, middle, teacher[0], valid[:, None], scale_up
     )
     grad_middle_norm, grad_gain_ffn = norm_two_pull(grad_norm_two)
     grad_middle = cotangent + grad_middle_norm
@@ -387,18 +614,18 @@
         axis=1,
     )
     small = jnp.stack([grad_gain_attn, grad_gain_ffn, jnp.full((model_width,), squares)] + [jnp.zeros_like(grad_gain_attn)] * 5)
-    ffn_grads = [part.reshape(seq_devices, slot, -1) for part in (grad_down, grad_gate, grad_up)]
+    grad_down, grad_in = grad_down.reshape(seq_devices, slot, -1), grad_in.reshape(2, seq_devices, slot, -1)
     reduce = reduce_all if slot % 16 == 0 and kv_slot % 16 == 0 else reduce_plain
-    (grad_down, grad_gate, grad_up), packed, small = reduce(ffn_grads, packed, small, 384)
+    grad_down, grad_in, packed, small = reduce(grad_down, grad_in, packed, small, 384)
     grad_queries = packed[:slot].T
     grad_keyvals = packed[slot:-slot].T.reshape(-1, 2, kv_slot)
     grad_out = packed[-slot:].T
     grad_down = grad_down.T
-    grad_in = jnp.stack([grad_gate, grad_up], axis=1)
+    grad_in = jnp.swapaxes(grad_in, 0, 1)
     gain_attn_all, gain_ffn_all, squares_all = small[0], small[1], small[2, 0]
     loss = squares_all / (valid_total * model_width)
     return (
-        output.astype(jnp.bfloat16)[None],
+        output[None],
         loss,
         grad_inputs[None],
         grad_queries,

time: 806 us -> 648 us (0.80)
  waiting for transfers between devices: 218 us -> 37.8 us
  Pallas kernels: 188 us -> 338 us
  matrix products: 239 us -> 123 us
  other arithmetic: 87.2 us -> 66.2 us
    pallas_call x0 -> x1, Pallas kernels: none -> 150 us  [ffn(): pl.pallas_call(ffn_kernel, name='ffn', out_shape=[jax.ShapeDtypeStruct((2...]
    dot_general x7 -> x0, matrix products: 110 us -> none  [the longest x2 24.2 us: per_device(): jnp.einsum('td,tf->df', normed_all, grad_gu[:, half], preferred_element_t...]
    all_gather x2 -> x0, waiting for transfers between devices: 94.2 us -> none  [the longest x1 47.3 us: per_device(): normed_all = lax.all_gather(normed_two, 'wt', axis=0, tiled=True)]
    reduce_scatter x2 -> x0, waiting for transfers between devices: 71.4 us -> none  [the longest x1 51.6 us: per_device(): ffn_part = lax.psum_scatter(ffn_low, 'wt', scatter_dimension=0, tiled=True)]
    convert_element_type x3 -> x0, other arithmetic: 15.3 us -> none  [the longest x1 7.31 us: per_device(): grad_gu = act_pull(grad_hidden)[0].astype(jnp.bfloat16)]
    all_gather x1, waiting for transfers between devices: 40.1 us -> 27.4 us  [per_device(): lax.all_gather(w_attn, 'wt', axis=0, tiled=True)]
    unnamed x80 -> x72, local copies, waits for them, and re-layouts: 19.2 us -> 25.4 us
  transfers between devices with their start and end apart: 10 -> 6, of which waited for: 8 -> 4; matrix products, arithmetic and copies ran while one was open for 14% -> 11% of each run, Pallas kernels for 0% -> 0%
where the time goes in v3:
time: 648 us; the launch traced here: 642 us
  Pallas kernels  338 us (52%)
  matrix products  123 us (19%)
  other arithmetic  66.2 us (10%)
  local copies, waits for them, and re-layouts  39.8 us (6%)
  waiting for transfers between devices  37.8 us (6%)
  between operations  18.7 us (3%)
  starting transfers between devices  12.6 us (2%)
    pallas_call x1, Pallas kernels, reduce_all(): pl.pallas_call(kernel, name='reduce_all', out_shape=[jax.ShapeDtypeStruct...  188 us
    pallas_call x1, Pallas kernels, ffn(): pl.pallas_call(ffn_kernel, name='ffn', out_shape=[jax.ShapeDtypeStruct((2...  150 us
    convert_element_type x1, other arithmetic, backward_block(): grad_scores_low = grad_scores.astype(jnp.bfloat16)  31.5 us
    dot_general x1, matrix products, backward_block(): jnp.einsum('qhe,ke->hqk', grad_mixed, window[:, HD:], preferred_element_t...  30.5 us
    all_gather x1, waiting for transfers between devices, per_device(): lax.all_gather(w_attn, 'wt', axis=0, tiled=True)  27.4 us
    unnamed x72, local copies, waits for them, and re-layouts  25.4 us
    dot_general x1, matrix products, forward_block(): jnp.einsum('hqk,ke->qhe', weights, window[:, HD:], preferred_element_type...  17.5 us
    dot_general x1, matrix products, backward_block(): jnp.einsum('hqk,qhe->ke', weights, grad_mixed, preferred_element_type=jnp...  17.1 us
  transfers between devices with their start and end apart: 6, of which 4 were waited for; matrix products, arithmetic and copies ran while one was open for 11% of the time, Pallas kernels for 0%

profile of v3, /device:TPU:11, one launch (start us, length us, event | category | flops | bytes accessed | tf_op | source)
XLA Modules:
  0.0 642.3 jit_solution(11763214686460920856)
XLA Ops:
  10.7 6.2 psum.7
  16.8 7.5 %copy.55 = bf16[1536,2,1152]{2,0,1:T(8,128)(2,1)} copy(bf16[1536,2,1152]{2,1,0:T(2,128)(2,1)} %param.14) | data formatting | bytes 14155776 | tf_op args[5]
  25.7 27.4 %all-gather.3.cloned.1.call-done = bf16[1536,1792]{1,0:T(8,128)(2,1)} async-done(((bf16[384,1792]{1,0:T(8,128)(2,1)}), bf16[1536,1792]{1,0:T(8,128)(2,1)}) %all-gather.3.cloned.1.call-update) | async-done | bytes 5505040 | tf_op jit(solution)/shard_map/all_gather | solution.py:509
  53.1 5.6 convolution_convert_fusion.3
  74.1 15.4 %fusion.4 = (f32[12,512]{1,0:T(8,128)S(1)}, f32[1536,512,12]{1,0,2:T(8,128)}) fusion(pred[512,1536]{0,1:T(8,128)(4,1)S(1)} %fusion.18, bf16[512,12,128]{0,2,1:T(8,128)(2,1)S(1)} %bitcast.122, bf16[1536,256]{1,0:T(8,128)(2,1)S(1)} %pad_maximum_fusion.4), kind=kOutput, calls=%fused_computation.9 | convolution fusion | flops 2444224512 | bytes 40525824 | tf_op jit(solution)/shard_map/while/body/eval_jaxpr/qhe,ke->hqk/dot_general | solution.py:524
  89.5 16.1 %exponential_reduce_fusion = f32[12,512]{1,0:T(8,128)S(1)} fusion(f32[1536,512,12]{1,0,2:T(8,128)} %get-tuple-element.105, f32[12,512]{1,0:T(8,128)S(1)} %get-tuple-element.104, pred[512,1536]{0,1:T(8,128)(4,1)S(1)} %fusion.18), kind=kLoop, calls=%fused_computation.7 | loop fusion | flops 37742592 | bytes 38584320 | tf_op jit(solution)/shard_map/while/body/eval_jaxpr/reduce_sum | solution.py:534
  105.6 17.5 %convolution_convert_fusion.4 = bf16[128,12,512]{2,0,1:T(8,128)(2,1)} fusion(bf16[1536,256]{1,0:T(8,128)(2,1)S(1)} %pad_maximum_fusion.4, f32[1536,512,12]{1,0,2:T(8,128)} %get-tuple-element.105, f32[12,512]{1,0:T(8,128)S(1)} %log_add_fusion, pred[512,1536]{0,1:T(8,128)(4,1)S(1)} %fusion.18), kind=kOutput, calls=%fused_computation.52 | convolution fusion | flops 2454454272 | bytes 40534016 | tf_op jit(solution)/shard_map/while/body/eval_jaxpr/hqk,ke->qhe/dot_general | solution.py:536
  123.1 5.3 multiply_reduce_fusion.1
  131.5 150.2 %ffn.1 = (bf16[2,256,1536]{2,1,0:T(8,128)(2,1)}, f32[2,256,1536]{2,1,0:T(8,128)}, f32[2,256,1536]{2,1,0:T(8,128)}, bf16[1536,1152]{1,0:T(8,128)(2,1)}, bf16[2,1536,1152]{2,1,0:T(8,128)(2,1)}, /*index=5*/f32[8,128]{1,0:T(8,128)}) custom-call(bf16[2,256,1536]{2,1,0:T(8,128)(2,1)} %bitcast.125, bf16[2,1536,1152]{2,1,0:T(8,128)(2,1)} %bitcast.118, ...), custom_call_target="tpu_custom_call" | custom-call | tf_op jit(solution)/shard_map/ffn/pallas_call | solution.py:428
  281.8 3.8 fusion.14
  291.0 3.8 convolution_convert_fusion.2
  296.6 30.5 %fusion = (f32[12,512]{1,0:T(8,128)S(1)}, f32[1536,512,12]{1,0,2:T(8,128)}) fusion(f32[1536,512,12]{1,0,2:T(8,128)} %get-tuple-element.105, f32[12,512]{1,0:T(8,128)S(1)} %log_add_fusion, pred[512,1536]{0,1:T(8,128)(4,1)S(1)} %fusion.18, bf16[512,12,128]{0,2,1:T(8,128)(2,1)S(1)} %bitcast.120, bf16[1536,256]{1,0:T(8,128)(2,1)S(1)} %copy-done.14), kind=kOutput, calls=%fused_computation.2 | convolution fusion | flops 2463098880 | bytes 78307328 | tf_op jit(solution)/shard_map/while/body/eval_jaxpr/qhe,ke->hqk/dot_general | solution.py:563
  327.1 17.1 %convolution_bitcast_fusion = f32[1536,128]{0,1:T(8,128)} fusion(bf16[512,12,128]{0,2,1:T(8,128)(2,1)S(1)} %bitcast.121, f32[1536,512,12]{1,0,2:T(8,128)} %get-tuple-element.105, f32[12,512]{1,0:T(8,128)S(1)} %log_add_fusion, pred[512,1536]{0,1:T(8,128)(4,1)S(1)} %fusion.18), kind=kOutput, calls=%fused_computation.44 | convolution fusion | flops 2453667840 | bytes 40919040 | tf_op jit(solution)/shard_map/while/body/eval_jaxpr/hqk,qhe->ke/dot_general | solution.py:578
  344.2 31.5 %fusion.2 = bf16[12,512,1536]{1,2,0:T(8,128)(2,1)} fusion(f32[1536,512,12]{1,0,2:T(8,128)} %get-tuple-element.109, f32[1536,512,12]{1,0,2:T(8,128)} %get-tuple-element.105, f32[12,512]{1,0:T(8,128)S(1)} %get-tuple-element.108, f32[12,512]{1,0:T(8,128)S(1)} %log_add_fusion, pred[512,1536]{0,1:T(8,128)(4,1)S(1)} %fusion.18), kind=kLoop, calls=%fused_computation.4 | loop fusion | flops 56623104 | bytes 95207424 | tf_op jit(solution)/shard_map/while/body/eval_jaxpr/convert_element_type | solution.py:567
  375.8 9.3 %multiply_convert_fusion = bf16[128,12,512]{2,0,1:T(8,128)(2,1)S(1)} fusion(bf16[12,512,1536]{1,2,0:T(8,128)(2,1)} %fusion.2, bf16[1536,256]{1,0:T(8,128)(2,1)S(1)} %copy-done.14), kind=kOutput, calls=%fused_computation.33 | convolution fusion | flops 2417491968 | bytes 20840448 | tf_op jit(solution)/shard_map/while/body/eval_jaxpr/hqk,ke->qhe/dot_general | solution.py:569
  387.9 6.0 fusion.19
  394.0 4.1 collective-permute-start.2
  401.3 3.4 convolution_convert_fusion
  404.8 4.6 collective-permute-done.2
  411.5 4.2 convolution_convert_fusion.1
  418.2 5.2 fusion.13
  423.4 4.9 pad_maximum_fusion.p_ref
  429.6 187.5 %reduce_all.1 = (f32[192,1152]{1,0:T(8,128)}, f32[2,192,1152]{2,1,0:T(8,128)}, f32[416,384]{1,0:T(8,128)}, f32[8,1536]{1,0:T(8,128)}) custom-call(bf16[4,2,192,1152]{3,2,1,0:T(8,128)(2,1)} %bitcast.127, bf16[2,4,2,192,1152]{4,3,2,1,0:T(8,128)(2,1)} %bitcast.124, bf16[4,2,416,1536]{3,2,1,0:T(8,128)(2,1)} %pad_maximum_fusion.p_ref, f32[8,1536]{1,0:T(8,128)} %stack.9.v_ref), custom_call_target="tpu_custom_call" | custom-call | tf_op jit(solution)/shard_map/reduce_all/pallas_call | solution.py:185
  623.3 4.1 copy.43
  (121 shorter events, 52.4 us)
Async XLA Ops:
  7.2 45.9 %all-gather.3.cloned.1.call-start = ((), (), s32[]{:S(2)}) async-start(), calls=%async_computation | async-start | bytes 6881280 | tf_op jit(solution)/shard_map/all_gather | solution.py:509
  7.9 115.2 %all-gather.5.cloned.1.call-start = ((), (), s32[]{:S(2)}) async-start(), calls=%async_computation.1 | async-start | bytes 5898240 | tf_op jit(solution)/shard_map/all_gather | solution.py:510
  9.1 15.3 %copy-start.23 = (f32[512]{0:T(512)}, f32[512]{0:T(512)S(1)}, u32[]{:S(2)}) copy-start(f32[512]{0:T(512)S(1)} %fusion.12) | copy-start | bytes 6148
  9.1 44.0 %copy-start.25 = (f32[512]{0:T(512)}, f32[512]{0:T(512)S(1)}, u32[]{:S(2)}) copy-start(f32[512]{0:T(512)S(1)} %fusion.39) | copy-start | bytes 6148
  9.8 14.6 %copy-start.21 = (s32[1536]{0:T(1024)}, s32[1536]{0:T(1024)S(1)}, u32[]{:S(2)}) copy-start(s32[1536]{0:T(1024)S(1)} %negate_select_fusion) | copy-start | bytes 18436
  16.8 36.3 %copy-start.27 = (f32[1536]{0:T(1024)S(1)}, f32[1536]{0:T(1024)}, u32[]{:S(2)}) copy-start(f32[1536]{0:T(1024)} %param.16) | copy-start | bytes 18436
  25.7 39.6 %copy-start.22 = (s32[1536]{0:T(1024)S(1)}, s32[1536]{0:T(1024)}, u32[]{:S(2)}) copy-start(s32[1536]{0:T(1024)} %copy-done.21) | copy-start | bytes 18436
  25.7 39.6 %slice-start.1 = ((s32[1536]{0:T(1024)}), s32[512]{0:T(512)S(1)}, s32[]{:S(2)}) async-start(s32[1536]{0:T(1024)} %copy-done.21), calls=%async_computation.3 | async-start | bytes 4096 | tf_op jit(solution)/shard_map/while/body/eval_jaxpr/dynamic_slice | solution.py:523
  58.8 10.9 %copy-start.17 = (bf16[512,256]{1,0:T(8,128)(2,1)}, bf16[512,256]{1,0:T(8,128)(2,1)S(1)}, u32[]{:S(2)}) copy-start(bf16[512,256]{1,0:T(8,128)(2,1)S(1)} %slice.83) | copy-start | bytes 786436
  58.8 10.9 %collective-permute-start = (bf16[512,256]{1,0:T(8,128)(2,1)S(1)}, bf16[512,256]{1,0:T(8,128)(2,1)S(1)}, u32[]{:S(2)}, u32[]{:S(2)}) collective-permute-start(bf16[512,256]{1,0:T(8,128)(2,1)S(1)} %slice.83), channel_id=1, source_target_pairs={{0,8},{4,12},{8,16},{12,20},{16,24},{20,28},{1,9},{5,13},{9,17},{1... | collective-permute-start | bytes 786440 | tf_op jit(solution)/shard_map/ppermute | solution.py:467
  61.9 11.0 %collective-permute-start.1 = (bf16[512,256]{1,0:T(8,128)(2,1)S(1)}, bf16[512,256]{1,0:T(8,128)(2,1)}, u32[]{:S(2)}, u32[]{:S(2)}) collective-permute-start(bf16[512,256]{1,0:T(8,128)(2,1)S(1)} %slice.83), channel_id=1, source_target_pairs={{0,4},{4,8},{8,12},{12,16},{16,20},{20,24},{24,28},{1,5},{5,9},{9,... | collective-permute-start | bytes 786440 | tf_op jit(solution)/shard_map/ppermute | solution.py:467
  69.6 19.8 %copy-start.7 = (bf16[512,1536]{0,1:T(8,128)(2,1)}, bf16[512,1536]{0,1:T(8,128)(2,1)S(1)}, u32[]{:S(2)}) copy-start(bf16[512,1536]{0,1:T(8,128)(2,1)S(1)} %copy.31) | copy-start | bytes 4718596
  74.1 31.5 %copy-start.13 = (bf16[1536,256]{1,0:T(8,128)(2,1)}, bf16[1536,256]{1,0:T(8,128)(2,1)S(1)}, u32[]{:S(2)}) copy-start(bf16[1536,256]{1,0:T(8,128)(2,1)S(1)} %pad_maximum_fusion.4) | copy-start | bytes 2359300
  105.6 17.5 %copy-start.10 = (bf16[1,512,1536]{2,1,0:T(8,128)(2,1)S(1)}, bf16[1,512,1536]{2,1,0:T(8,128)(2,1)}, u32[]{:S(2)}) copy-start(bf16[1,512,1536]{2,1,0:T(8,128)(2,1)} %param.9) | copy-start | bytes 4718596
  375.7 11.7 %copy-start = (bf16[12,512,1536]{1,2,0:T(8,128)(2,1)S(1)}, bf16[12,512,1536]{1,2,0:T(8,128)(2,1)}, u32[]{:S(2)}) copy-start(bf16[12,512,1536]{1,2,0:T(8,128)(2,1)} %fusion.2) | copy-start | bytes 56623108
  375.8 12.1 %copy-start.8 = (bf16[512,1536]{0,1:T(8,128)(2,1)S(1)}, bf16[512,1536]{0,1:T(8,128)(2,1)}, u32[]{:S(2)}) copy-start(bf16[512,1536]{0,1:T(8,128)(2,1)} %copy-done.7) | copy-start | bytes 4718596
  387.9 13.4 %copy-start.5 = (f32[512,1536]{1,0:T(8,128)S(1)}, f32[512,1536]{1,0:T(8,128)}, u32[]{:S(2)}) copy-start(f32[512,1536]{1,0:T(8,128)} %copy-done.4) | copy-start | bytes 9437188
  387.9 13.4 %copy-start.29 = (bf16[128,12,512]{2,0,1:T(8,128)(2,1)S(1)}, bf16[128,12,512]{2,0,1:T(8,128)(2,1)}, u32[]{:S(2)}) copy-start(bf16[128,12,512]{2,0,1:T(8,128)(2,1)} %convolution_convert_fusion.4) | copy-start | bytes 4718596
  394.0 15.3 %collective-permute-start.2 = (f32[512,256]{0,1:T(8,128)S(1)}, f32[512,256]{0,1:T(8,128)S(1)}, u32[]{:S(2)}, u32[]{:S(2)}) collective-permute-start(f32[512,256]{0,1:T(8,128)S(1)} %get-tuple-element.100), channel_id=1, source_target_pairs={{4,0},{8,4},{12,8},{16,12},{20,16},{24,20},{28,24},{5,1},{9,5},{13... | collective-permute-start | bytes 1572872 | tf_op jit(solution)/shard_map/ppermute | solution.py:467
  398.2 13.1 %collective-permute-start.3 = (f32[512,256]{0,1:T(8,128)S(1)}, f32[512,256]{0,1:T(8,128)S(1)}, u32[]{:S(2)}, u32[]{:S(2)}) collective-permute-start(f32[512,256]{0,1:T(8,128)S(1)} %get-tuple-element.101), channel_id=1, source_target_pairs={{8,0},{12,4},{16,8},{20,12},{24,16},{28,20},{9,1},{13,5},{17,9},{2... | collective-permute-start | bytes 1572872 | tf_op jit(solution)/shard_map/ppermute | solution.py:467
  401.3 16.8 %slice-start.2 = ((s8[5505024]{0:T(1024)(128)(4,1)}), s8[4194304]{0:T(1024)(128)(4,1)S(1)}, s32[]{:S(2)}) async-start(s8[5505024]{0:T(1024)(128)(4,1)} %bitcast.137), calls=%async_computation.4 | async-start | bytes 8388608
  429.6 193.7 %copy-start.24 = (f32[512]{0:T(512)S(1)}, f32[512]{0:T(512)}, u32[]{:S(2)}) copy-start(f32[512]{0:T(512)} %copy-done.23) | copy-start | bytes 6148
  617.1 10.3 %copy-start.12 = (bf16[1,512,1536]{2,1,0:T(8,128)(2,1)S(1)}, bf16[1,512,1536]{2,1,0:T(8,128)(2,1)}, u32[]{:S(2)}) copy-start(bf16[1,512,1536]{2,1,0:T(8,128)(2,1)} %param.9) | copy-start | bytes 4718596
  617.1 10.3 %copy-start.15 = (f32[512,1536]{1,0:T(8,128)S(1)}, f32[512,1536]{1,0:T(8,128)}, u32[]{:S(2)}) copy-start(f32[512,1536]{1,0:T(8,128)} %get-tuple-element.110) | copy-start | bytes 9437188
  (18 other events, 90.7 us)
Sparse Core Ops, SparseCore 0:
  9.6 43.4 all-gather.2
  54.6 37.4 all-gather.4

commit v4 on v3

--- a/solution.py
+++ b/solution.py
@@ -10,7 +10,7 @@
 HEADS = 12
 HD = 128
 WINDOW = 1024
-QBLK = 512
+QROWS = 256
 
 
 EPSILON = 1e-06
@@ -460,6 +460,96 @@
     )(split(h), wi, wd, split(mid), split(teacher), split(valid), scale)
     return out.reshape(rows, width), cot.reshape(rows, width), dh.reshape(rows, width), gd, gi, squares[0, 0]
 
+def pair_rows(block):
+    return jnp.concatenate([block[:, :HD], block[:, HD:]], axis=0)
+
+
+def pair_columns(block):
+    rows = block.shape[0] // 2
+    return jnp.concatenate([block[:rows], block[rows:]], axis=1)
+
+
+def attend_kernel(q, kv, q_ids, k_ids, out, probs, bias):
+    i, pair = pl.program_id(0), pl.program_id(1)
+    reach = WINDOW + QROWS
+    keys = pl.ds(pl.multiple_of(i * QROWS, QROWS), reach)
+
+    @pl.when(pair == 0)
+    def _():
+        row = lax.broadcasted_iota(jnp.int32, (QROWS, reach), 0)
+        offset = lax.broadcasted_iota(jnp.int32, (QROWS, reach), 1) - WINDOW - row
+        allowed = (offset <= 0) & (offset > -WINDOW) & (q_ids[...] == k_ids[:, keys])
+        bias[...] = jnp.where(allowed, 0.0, NEGATIVE)
+
+    scores = contract(pair_rows(q[...]), kv[keys, :HD], 1, 1) * (math.log2(math.e) / math.sqrt(HD))
+    shifted = scores.reshape(2, QROWS, reach) + bias[...][None]
+    powers = jnp.exp2(shifted - jnp.max(shifted, axis=-1, keepdims=True))
+    weights = (powers * (1.0 / jnp.sum(powers, axis=-1, keepdims=True))).astype(BF16)
+    probs[0] = weights
+    mixed = contract(weights.reshape(2 * QROWS, reach), kv[keys, HD:], 1, 0)
+    out[...] = pair_columns(mixed).astype(BF16)
+
+
+def attend(queries, width, extended, q_ids, k_ids):
+    rows = queries.shape[0]
+    blocks, pairs, reach = rows // QROWS, width // (2 * HD), WINDOW + QROWS
+    return pl.pallas_call(
+        attend_kernel,
+        name="attend",
+        grid=(blocks, pairs),
+        out_shape=[
+            jax.ShapeDtypeStruct((rows, width), BF16),
+            jax.ShapeDtypeStruct((blocks, 2 * pairs, QROWS, reach), BF16),
+        ],
+        in_specs=[
+            pl.BlockSpec((QROWS, 2 * HD), lambda i, p: (i, p)),
+            pl.BlockSpec(extended.shape, lambda i, p: (0, 0)),
+            pl.BlockSpec((QROWS, 1), lambda i, p: (i, 0)),
+            pl.BlockSpec(k_ids.shape, lambda i, p: (0, 0)),
+        ],
+        out_specs=[
+            pl.BlockSpec((QROWS, 2 * HD), lambda i, p: (i, p)),
+            pl.BlockSpec((1, 2, QROWS, reach), lambda i, p: (i, p, 0, 0)),
+        ],
+        scratch_shapes=[pltpu.VMEM((QROWS, reach), F32)],
+        compiler_params=pltpu.CompilerParams(vmem_limit_bytes=48 << 20),
+    )(queries, extended, q_ids, k_ids)
+
+
+def attend_back_kernel(q, kv, grad, mixed, probs, grad_q, grad_kv):
+    i, pair = pl.program_id(0), pl.program_id(1)
+    reach = WINDOW + QROWS
+    keys = pl.ds(pl.multiple_of(i * QROWS, QROWS), reach)
+
+    @pl.when((i == 0) & (pair == 0))
+    def _():
+        grad_kv[...] = jnp.zeros_like(grad_kv)
+
+    queries, grads = pair_rows(q[...]), pair_rows(grad[...])
+    weights = probs[0].reshape(2 * QROWS, reach)
+    dots = jnp.sum(grads.astype(F32) * pair_rows(mixed[...]).astype(F32), axis=-1, keepdims=True)
+    steep = contract(grads, kv[keys, HD:], 1, 1) - dots
+    steep = (weights.astype(F32) * steep).astype(BF16)
+    grad_q[...] = (pair_columns(contract(steep, kv[keys, :HD], 1, 0)) * (1.0 / math.sqrt(HD))).astype(BF16)
+    grad_kv[keys, :HD] += contract(steep, queries, 0, 0)
+    grad_kv[keys, HD:] += contract(weights, grads, 0, 0)
+
+
+def attend_back(queries, extended, grad_mixed, mixed, probs):
+    rows, width = mixed.shape
+    blocks, pairs, reach = rows // QROWS, width // (2 * HD), WINDOW + QROWS
+    block = pl.BlockSpec((QROWS, 2 * HD), lambda i, p: (i, p))
+    whole = pl.BlockSpec(extended.shape, lambda i, p: (0, 0))
+    return pl.pallas_call(
+        attend_back_kernel,
+        name="attend_back",
+        grid=(blocks, pairs),
+        out_shape=[jax.ShapeDtypeStruct((rows, width), BF16), jax.ShapeDtypeStruct(extended.shape, F32)],
+        in_specs=[block, whole, block, block, pl.BlockSpec((1, 2, QROWS, reach), lambda i, p: (i, p, 0, 0))],
+        out_specs=[block, whole],
+        compiler_params=pltpu.CompilerParams(vmem_limit_bytes=48 << 20),
+    )(queries, extended, grad_mixed, mixed, probs)
+
 
 def passed_along(block, axis, distance):
     devices = range(lax.axis_size(axis))
@@ -477,17 +567,6 @@
     inside = (positions >= 0) & (positions < seq_ends[-1])
     number = jnp.sum((positions[:, None] >= seq_starts[None, :]).astype(jnp.int32), axis=1) - 1
     return jnp.where(inside, number, -(positions + 2 * stream_len))
-
-
-def window_mask(query_ids, key_ids):
-    query_pos = lax.broadcasted_iota(jnp.int32, (QBLK, WINDOW + QBLK), 0)
-    key_pos = lax.broadcasted_iota(jnp.int32, (QBLK, WINDOW + QBLK), 1)
-    offset = key_pos - WINDOW - query_pos
-    return (offset <= 0) & (offset > -WINDOW) & (query_ids[:, None] == key_ids[None, :])
-
-
-def gated_act(gate_up):
-    return jax.nn.gelu(gate_up[:, 0, :]) * gate_up[:, 1, :]
 
 
 def per_device(tokens, teacher, seq_lengths, w_attn, w_out, w_in, w_down, gain_attn, gain_ffn):
@@ -499,7 +578,6 @@
     all_slots = stream_len * lax.axis_size("wt")
     reach_count = (WINDOW + tok_rows - 1) // tok_rows
     edge_rows = reach_count * tok_rows
-    scale = 1.0 / math.sqrt(HD)
     inputs = tokens[0].astype(jnp.float32)
     positions = seq_place * tok_rows - edge_rows + jnp.arange(edge_rows + tok_rows, dtype=jnp.int32)
     seq_ids = stream_ids(positions, seq_lengths[0], stream_len)
@@ -512,34 +590,10 @@
     normed_f, norm_one_pull = jax.vjp(rms_scale, inputs, gain_attn)
     normed = normed_f.astype(jnp.bfloat16)
     qkv = jnp.dot(normed, attn_full, preferred_element_type=jnp.float32).astype(jnp.bfloat16)
-    queries = qkv[:, :model_width].reshape(tok_rows, HEADS, HD)
     key_value = qkv[:, model_width:]
     earlier = [passed_along(key_value, "seq", back_step) for back_step in range(reach_count, 0, -1)]
     extended = jnp.concatenate(earlier + [key_value], axis=0)
-    block_count = tok_rows // QBLK
-
-    def block_scores(block):
-        start = block * QBLK
-        query_ids = lax.dynamic_slice_in_dim(seq_ids, start + edge_rows, QBLK)
-        raw = jnp.einsum(
-            "qhe,ke->hqk", queries, extended[:, :HD], preferred_element_type=jnp.float32
-        )
-        allowed = window_mask(query_ids, seq_ids)
-        masked = jnp.where(allowed[None], raw * scale, NEGATIVE)
-        return (queries, extended, masked)
-
-    def forward_block(block):
-        q_blk, window, masked = block_scores(block)
-        top = jnp.max(masked, axis=-1, keepdims=True)
-        log_total = top + jnp.log(jnp.sum(jnp.exp(masked - top), axis=-1, keepdims=True))
-        weights = jnp.exp(masked - log_total).astype(jnp.bfloat16)
-        mixed = jnp.einsum(
-            "hqk,ke->qhe", weights, window[:, HD:], preferred_element_type=jnp.float32
-        )
-        return (mixed, log_total)
-
-    mixed_blocks, log_totals = lax.map(forward_block, jnp.arange(block_count, dtype=jnp.int32))
-    mixed_b = mixed_blocks.reshape(tok_rows, model_width).astype(jnp.bfloat16)
+    mixed_b, probs = attend(qkv, model_width, extended, seq_ids[edge_rows:, None], seq_ids[None, :])
     middle = inputs + jnp.dot(mixed_b, out_full, preferred_element_type=jnp.float32)
     normed_two_f, norm_two_pull = jax.vjp(rms_scale, middle, gain_ffn)
     normed_two = normed_two_f.astype(jnp.bfloat16)
@@ -553,48 +607,15 @@
     grad_mid_low = grad_middle.astype(jnp.bfloat16)
     grad_out = jnp.einsum("te,td->ed", grad_mid_low, mixed_b, preferred_element_type=jnp.float32)
     grad_mixed = jnp.einsum("te,de->td", grad_mid_low, out_full, preferred_element_type=jnp.float32)
-    grad_mixed = grad_mixed.astype(jnp.bfloat16).reshape(tok_rows, HEADS, HD)
-
-    def backward_block(grad_ext, block):
-        q_blk, window, masked = block_scores(block)
-        log_total = lax.dynamic_index_in_dim(log_totals, block, 0, keepdims=False)
-        probs = jnp.exp(masked - log_total)
-        weights = probs.astype(jnp.bfloat16)
-        grad_weights = jnp.einsum(
-            "qhe,ke->hqk", grad_mixed, window[:, HD:], preferred_element_type=jnp.float32
-        )
-        grad_scores = probs * (grad_weights - jnp.sum(probs * grad_weights, axis=-1, keepdims=True))
-        grad_scores_low = grad_scores.astype(jnp.bfloat16)
-        grad_query = (
-            jnp.einsum(
-                "hqk,ke->qhe", grad_scores_low, window[:, :HD], preferred_element_type=jnp.float32
-            )
-            * scale
-        )
-        grad_key = (
-            jnp.einsum("hqk,qhe->ke", grad_scores_low, q_blk, preferred_element_type=jnp.float32)
-            * scale
-        )
-        grad_value = jnp.einsum(
-            "hqk,qhe->ke", weights, grad_mixed, preferred_element_type=jnp.float32
-        )
-        updated = grad_ext + jnp.concatenate([grad_key, grad_value], axis=1)
-        return (updated, grad_query)
-
-    grad_ext, grad_query_blocks = lax.scan(
-        backward_block,
-        jnp.zeros((edge_rows + tok_rows, 2 * HD), jnp.float32),
-        jnp.arange(block_count, dtype=jnp.int32),
-    )
+    grad_query, grad_ext = attend_back(qkv, extended, grad_mixed.astype(jnp.bfloat16), mixed_b, probs)
     grad_kv = grad_ext[edge_rows:]
     for back_step in range(1, reach_count + 1):
         slab_rows = grad_ext[
             edge_rows - back_step * tok_rows : edge_rows - (back_step - 1) * tok_rows
         ]
         grad_kv = grad_kv + passed_along(slab_rows, "seq", -back_step)
-    grad_qkv = jnp.concatenate(
-        [grad_query_blocks.reshape(tok_rows, model_width), grad_kv], axis=1
-    ).astype(jnp.bfloat16)
+    grad_key = (grad_kv[:, :HD] * (1.0 / math.sqrt(HD))).astype(jnp.bfloat16)
+    grad_qkv = jnp.concatenate([grad_query, grad_key, grad_kv[:, HD:].astype(jnp.bfloat16)], axis=1)
     grad_attn = jnp.einsum("te,td->ed", grad_qkv, normed, preferred_element_type=jnp.float32)
     grad_normed = jnp.einsum("te,de->td", grad_qkv, attn_full, preferred_element_type=jnp.float32)
     grad_input_norm, grad_gain_attn = norm_one_pull(grad_normed)

time: 648 us -> 553 us (0.85)
  matrix products: 123 us -> 25.9 us
  Pallas kernels: 338 us -> 385 us
  other arithmetic: 66.2 us -> 19.2 us
  waiting for transfers between devices: 37.8 us -> 50.5 us
  local copies, waits for them, and re-layouts: 39.8 us -> 29.7 us
    dot_general x6 -> x0, matrix products: 95.9 us -> none  [the longest x1 30.5 us: backward_block(): jnp.einsum('qhe,ke->hqk', grad_mixed, window[:, HD:], preferred_element_t...]
    pallas_call x0 -> x2, Pallas kernels: none -> 47.9 us  [the longest x1 27.1 us: attend(): pl.pallas_call(attend_kernel, name='attend', grid=(blocks, pairs), out_sh...]
    convert_element_type x1, other arithmetic: 31.5 us -> 0.02 us  [per_device(): grad_key = (grad_kv[:, :HD] * (1.0 / math.sqrt(HD))).astype(jnp.bfloat16)]
    reduce_sum x1 -> x0, other arithmetic: 16.1 us -> none  [forward_block(): jnp.sum(jnp.exp(masked - top), axis=-1, keepdims=True)]
    all_gather x1, waiting for transfers between devices: 27.4 us -> 43.3 us  [per_device(): lax.all_gather(w_attn, 'wt', axis=0, tiled=True)]
    unnamed x72 -> x44, local copies, waits for them, and re-layouts: 25.4 us -> 19.8 us
  transfers between devices with their start and end apart: 6 -> 6, of which waited for: 4 -> 3; matrix products, arithmetic and copies ran while one was open for 11% -> 4% of each run, Pallas kernels for 0% -> 5%
where the time goes in v4:
time: 553 us; the launch traced here: 547 us
  Pallas kernels  385 us (70%)
  waiting for transfers between devices  50.5 us (9%)
  local copies, waits for them, and re-layouts  29.7 us (5%)
  matrix products  25.9 us (5%)
  other arithmetic  19.2 us (3%)
  between operations  18.6 us (3%)
  starting transfers between devices  11.3 us (2%)
  blocking collectives  6.6 us (1%)
    pallas_call x1, Pallas kernels, reduce_all(): pl.pallas_call(kernel, name='reduce_all', out_shape=[jax.ShapeDtypeStruct...  187 us
    pallas_call x1, Pallas kernels, ffn(): pl.pallas_call(ffn_kernel, name='ffn', out_shape=[jax.ShapeDtypeStruct((2...  150 us
    all_gather x1, waiting for transfers between devices, per_device(): lax.all_gather(w_attn, 'wt', axis=0, tiled=True)  43.3 us
    pallas_call x1, Pallas kernels, attend(): pl.pallas_call(attend_kernel, name='attend', grid=(blocks, pairs), out_sh...  27.1 us
    pallas_call x1, Pallas kernels, attend_back(): pl.pallas_call(attend_back_kernel, name='attend_back', grid=(blocks, pair...  20.8 us
    unnamed x44, local copies, waits for them, and re-layouts  19.8 us
    ppermute x4, starting transfers between devices, passed_along(): return lax.ppermute(block, axis, route)  11.2 us
  transfers between devices with their start and end apart: 6, of which 3 were waited for; matrix products, arithmetic and copies ran while one was open for 4% of the time, Pallas kernels for 5%

profile of v4, /device:TPU:11, one launch (start us, length us, event | category | flops | bytes accessed | tf_op | source)
XLA Modules:
  0.0 546.7 jit_solution(3974660781474585053)
XLA Ops:
  9.8 43.3 %all-gather.3.cloned.1.call-done = bf16[1536,1792]{1,0:T(8,128)(2,1)} async-done(((bf16[384,1792]{1,0:T(8,128)(2,1)}), bf16[1536,1792]{1,0:T(8,128)(2,1)}) %all-gather.3.cloned.1.call-update) | async-done | bytes 5505040 | tf_op jit(solution)/shard_map/all_gather | solution.py:587
  53.1 5.6 %convolution_convert_fusion.3.q = bf16[512,1792]{1,0:T(8,128)(2,1)S(1)} fusion(bf16[1536,1792]{1,0:T(8,128)(2,1)} %all-gather.3.cloned.1.call-done, bf16[1,512,1536]{2,1,0:T(8,128)(2,1)S(1)} %copy-done.9, f32[1536]{0:T(1024)S(1)} %copy-done.15, f32[512]{0:T(512)S(1)} %fusion.25), kind=kOutput, calls=%fused_computation.27 | convolution fusion | flops 2822635520 | bytes 8921088 | tf_op jit(solution)/shard_map/dot_general | solution.py:592
  58.8 3.1 collective-permute-start
  61.9 3.1 collective-permute-start.1
  65.0 6.6 %psum.7 = f32[]{:T(128)} all-reduce(f32[]{:T(128)S(6)} %convert_element_type.69), channel_id=1, replica_groups=mesh['seq'=8,'wt'=4] {'wt'}, use_global_device_ids=true, to_apply=%region_2.3 | all-reduce | flops 1 | bytes 8 | tf_op jit(solution)/shard_map/psum | solution.py:585
  72.6 6.8 %copy.26 = bf16[1536,2,1152]{2,0,1:T(8,128)(2,1)} copy(bf16[1536,2,1152]{2,1,0:T(2,128)(2,1)} %param.14) | data formatting | bytes 14155776 | tf_op args[5]
  82.6 27.1 %attend.1 = (bf16[512,1536]{1,0:T(8,128)(2,1)S(1)}, bf16[2,12,256,1280]{3,2,1,0:T(8,128)(2,1)}) custom-call(bf16[512,1792]{1,0:T(8,128)(2,1)S(1)} %convolution_convert_fusion.3.q, bf16[1536,256]{1,0:T(8,128)(2,1)S(1)} %pad_maximum_fusion.2.kv, s32[512,1]{1,0:T(8,128)S(1)} %copy.21.q_ids, s32[1,1536]{1,0:T(1,128)S(1)} %and_select_fusion.k_ids), custom_call_target="tpu_custom_call" | custom-call | tf_op jit(solution)/shard_map/attend/pallas_call | solution.py:496
  110.9 6.0 %multiply_reduce_fusion.1 = (f32[512]{0:T(512)S(1)}, f32[512,1536]{1,0:T(8,128)S(1)}) fusion(bf16[512,1536]{1,0:T(8,128)(2,1)} %copy-done.1, bf16[1536,1536]{1,0:T(8,128)(2,1)} %all-gather.5.cloned.1.call-done, bf16[1,512,1536]{2,1,0:T(8,128)(2,1)} %param.9), kind=kOutput, calls=%fused_computation.25 | convolution fusion | flops 2419064320 | bytes 11012096 | tf_op jit(solution)/shard_map/dot_general | solution.py:597
  120.0 150.4 %ffn.1 = (bf16[2,256,1536]{2,1,0:T(8,128)(2,1)}, f32[2,256,1536]{2,1,0:T(8,128)}, f32[2,256,1536]{2,1,0:T(8,128)}, bf16[1536,1152]{1,0:T(8,128)(2,1)}, bf16[2,1536,1152]{2,1,0:T(8,128)(2,1)}, /*index=5*/f32[8,128]{1,0:T(8,128)}) custom-call(bf16[2,256,1536]{2,1,0:T(8,128)(2,1)} %bitcast.66, bf16[2,1536,1152]{2,1,0:T(8,128)(2,1)} %bitcast.63, ...), custom_call_target="tpu_custom_call" | custom-call | tf_op jit(solution)/shard_map/ffn/pallas_call | solution.py:428
  270.5 3.8 fusion.9
  275.1 2.8 fusion.4
  278.0 2.7 convolution_convert_fusion.2.grad
  280.7 20.8 %attend_back.1 = (bf16[512,1536]{1,0:T(8,128)(2,1)S(1)}, f32[1536,256]{1,0:T(8,128)S(1)}) custom-call(bf16[512,1792]{1,0:T(8,128)(2,1)} %copy-done, bf16[1536,256]{1,0:T(8,128)(2,1)S(1)} %pad_maximum_fusion.2.kv, bf16[512,1536]{1,0:T(8,128)(2,1)S(1)} %convolution_convert_fusion.2.grad, bf16[512,1536]{1,0:T(8,128)(2,1)} %copy-done.1, ...), custom_call_target="tpu_custom_call" | custom-call | tf_op jit(solution)/shard_map/attend_back/pallas_call | solution.py:543
  301.6 2.2 collective-permute-start.2
  303.8 2.8 collective-permute-start.3
  307.8 3.0 convolution_convert_fusion
  310.9 4.8 collective-permute-done.2
  316.9 3.7 convolution_convert_fusion.1
  320.6 2.4 copy-done.5
  323.1 4.9 fusion.8
  328.0 5.0 pad_maximum_fusion.p_ref
  334.4 186.6 %reduce_all.1 = (f32[192,1152]{1,0:T(8,128)}, f32[2,192,1152]{2,1,0:T(8,128)}, f32[416,384]{1,0:T(8,128)}, f32[8,1536]{1,0:T(8,128)}) custom-call(bf16[4,2,192,1152]{3,2,1,0:T(8,128)(2,1)} %bitcast.68, bf16[2,4,2,192,1152]{4,3,2,1,0:T(8,128)(2,1)} %bitcast.65, bf16[4,2,416,1536]{3,2,1,0:T(8,128)(2,1)} %pad_maximum_fusion.p_ref, f32[8,1536]{1,0:T(8,128)} %stack.9.v_ref), custom_call_target="tpu_custom_call" | custom-call | tf_op jit(solution)/shard_map/reduce_all/pallas_call | solution.py:185
  527.2 4.1 copy.24
  531.2 4.5 fusion.6
  (83 shorter events, 22.0 us)
Async XLA Ops:
  7.2 2.2 copy-start.9
  7.2 45.9 %copy-start.15 = (f32[1536]{0:T(1024)S(1)}, f32[1536]{0:T(1024)}, u32[]{:S(2)}) copy-start(f32[1536]{0:T(1024)} %param.16) | copy-start | bytes 18436
  7.2 45.9 %all-gather.3.cloned.1.call-start = ((), (), s32[]{:S(2)}) async-start(), calls=%async_computation | async-start | bytes 6881280 | tf_op jit(solution)/shard_map/all_gather | solution.py:587
  7.9 102.9 %all-gather.5.cloned.1.call-start = ((), (), s32[]{:S(2)}) async-start(), calls=%async_computation.1 | async-start | bytes 5898240 | tf_op jit(solution)/shard_map/all_gather | solution.py:588
  58.7 23.9 %copy-start = (bf16[512,1792]{1,0:T(8,128)(2,1)}, bf16[512,1792]{1,0:T(8,128)(2,1)S(1)}, u32[]{:S(2)}) copy-start(bf16[512,1792]{1,0:T(8,128)(2,1)S(1)} %convolution_convert_fusion.3.q) | copy-start | bytes 5505028
  58.8 22.1 %collective-permute-start = (bf16[512,256]{1,0:T(8,128)(2,1)S(1)}, bf16[512,256]{1,0:T(8,128)(2,1)S(1)}, u32[]{:S(2)}, u32[]{:S(2)}) collective-permute-start(bf16[512,256]{1,0:T(8,128)(2,1)S(1)} %slice.76), channel_id=1, source_target_pairs={{0,8},{4,12},{8,16},{12,20},{16,24},{20,28},{1,9},{5,13},{9,17},{1... | collective-permute-start | bytes 786440 | tf_op jit(solution)/shard_map/ppermute | solution.py:557
  61.9 19.6 %collective-permute-start.1 = (bf16[512,256]{1,0:T(8,128)(2,1)S(1)}, bf16[512,256]{1,0:T(8,128)(2,1)}, u32[]{:S(2)}, u32[]{:S(2)}) collective-permute-start(bf16[512,256]{1,0:T(8,128)(2,1)S(1)} %slice.76), channel_id=1, source_target_pairs={{0,4},{4,8},{8,12},{12,16},{16,20},{20,24},{24,28},{1,5},{5,9},{9,... | collective-permute-start | bytes 786440 | tf_op jit(solution)/shard_map/ppermute | solution.py:557
  110.9 7.7 %copy-start.14 = (f32[1536]{0:T(1024)S(1)}, f32[1536]{0:T(1024)}, u32[]{:S(2)}) copy-start(f32[1536]{0:T(1024)} %param.17) | copy-start | bytes 18436
  270.4 3.8 copy-start.4
  270.4 4.7 copy-start.8
  270.4 7.5 %slice-start.3 = ((s8[4718592]{0:T(1024)(128)(4,1)}), s8[4194304]{0:T(1024)(128)(4,1)S(1)}, s32[]{:S(2)}) async-start(s8[4718592]{0:T(1024)(128)(4,1)} %bitcast.79), calls=%async_computation.5 | async-start | bytes 8388608
  275.1 2.8 slice-start.4
  278.0 29.9 %copy-start.6 = (f32[512,1536]{1,0:T(8,128)}, f32[512,1536]{1,0:T(8,128)S(1)}, u32[]{:S(2)}) copy-start(f32[512,1536]{1,0:T(8,128)S(1)} %fusion.4) | copy-start | bytes 9437188
  280.7 27.2 %copy-start.2 = (bf16[512,1536]{1,0:T(8,128)(2,1)S(1)}, bf16[512,1536]{1,0:T(8,128)(2,1)}, u32[]{:S(2)}) copy-start(bf16[512,1536]{1,0:T(8,128)(2,1)} %copy-done.1) | copy-start | bytes 4718596
  301.6 14.1 %collective-permute-start.2 = (f32[512,256]{1,0:T(8,128)S(1)}, f32[512,256]{1,0:T(8,128)S(1)}, u32[]{:S(2)}, u32[]{:S(2)}) collective-permute-start(f32[512,256]{1,0:T(8,128)S(1)} %get-tuple-element.66), channel_id=1, source_target_pairs={{4,0},{8,4},{12,8},{16,12},{20,16},{24,20},{28,24},{5,1},{9,5},{13... | collective-permute-start | bytes 1572872 | tf_op jit(solution)/shard_map/ppermute | solution.py:557
  303.8 12.9 %collective-permute-start.3 = (f32[512,256]{1,0:T(8,128)S(1)}, f32[512,256]{1,0:T(8,128)S(1)}, u32[]{:S(2)}, u32[]{:S(2)}) collective-permute-start(f32[512,256]{1,0:T(8,128)S(1)} %get-tuple-element.67), channel_id=1, source_target_pairs={{8,0},{12,4},{16,8},{20,12},{24,16},{28,20},{9,1},{13,5},{17,9},{2... | collective-permute-start | bytes 1572872 | tf_op jit(solution)/shard_map/ppermute | solution.py:557
  307.8 9.0 %copy-start.10 = (bf16[1,512,1536]{2,1,0:T(8,128)(2,1)S(1)}, bf16[1,512,1536]{2,1,0:T(8,128)(2,1)}, u32[]{:S(2)}) copy-start(bf16[1,512,1536]{2,1,0:T(8,128)(2,1)} %param.9) | copy-start | bytes 4718596
  316.7 6.4 %slice-start.1 = ((s8[5505024]{0:T(1024)(128)(4,1)}), s8[1310720]{0:T(1024)(128)(4,1)S(1)}, s32[]{:S(2)}) async-start(s8[5505024]{0:T(1024)(128)(4,1)} %bitcast.77), calls=%async_computation.3 | async-start | bytes 2621440
  316.9 6.2 %slice-start.2 = ((s8[5505024]{0:T(1024)(128)(4,1)}), s8[4194304]{0:T(1024)(128)(4,1)S(1)}, s32[]{:S(2)}) async-start(s8[5505024]{0:T(1024)(128)(4,1)} %bitcast.77), calls=%async_computation.4 | async-start | bytes 8388608
  320.6 2.4 copy-start.5
  323.1 4.9 slice-start
  521.0 10.2 %copy-start.7 = (f32[512,1536]{1,0:T(8,128)S(1)}, f32[512,1536]{1,0:T(8,128)}, u32[]{:S(2)}) copy-start(f32[512,1536]{1,0:T(8,128)} %copy-done.6) | copy-start | bytes 9437188
  531.2 5.2 copy-start.11
  535.7 1.9 copy-start.12
  (3 other events, 3.5 us)
Sparse Core Ops, SparseCore 0:
  9.6 43.4 all-gather.2
  54.7 37.5 all-gather.4

commit v5 on v4

--- a/solution.py
+++ b/solution.py
@@ -45,173 +45,7 @@
     pl.semaphore_wait(barrier, len(devices))
 
 
-def reduce_kernel(depth, widths, g_refs, p_ref, v_ref, g_outs, p_out, v_out, gx, gt, gz, pc, py, px, pt, pz, vb,
-                  gxs, gxr, gzs, gzr, pcs, pcr, pys, pyr, pxs, pxr, pzs, pzr, vs, vr):
-    z, x, y, c = places()
-    width = gx.shape[-1]
-    cols = pc.shape[-1]
-    sib, ypeer, xpeer = device(z, x, y, 1 - c), device(z, x, 1 - y, c), device(z, 1 - x, y, c)
-    zs = [lax.rem(z + d, depth) for d in range(depth)]
-    zpeers = [device(zs[d], x, y, c) for d in range(depth)]
-    greet([sib, ypeer, xpeer] + zpeers[1:])
-    places_of = [(i, k * width) for i, total in enumerate(widths) for k in range(total // width)]
-    chunks = len(places_of)
-    started = []
-
-    def go(*args):
-        started.append(remote(*args))
-        return started[-1]
-
-    order = list(range(1, depth)) + [0]
-    core = {}
-    for d in order:
-        for h in range(2):
-            at = pl.multiple_of((2 * h + 1 - c) * cols, cols)
-            core[d, h] = go(p_ref.at[zs[d], :, :, pl.ds(at, cols)], pc.at[d, h], pcs.at[d, h], pcr.at[d, h], sib)
-    gxc, gzc, pyc, pxc, pzc, vc = {}, {}, {}, {}, {}, {}
-
-    def g_send(k):
-        if k < chunks:
-            i, at = places_of[k]
-            gxc[k] = go(g_refs[i].at[:, 1 - x, :, pl.ds(at, width)], gx.at[k], gxs.at[k], gxr.at[k], xpeer)
-
-    for k in range(2):
-        g_send(k)
-    vc[0] = go(v_ref, vb.at[0], vs.at[0], vr.at[0], sib)
-
-    def p_y(d):
-        for h in range(2):
-            core[d, h].wait_recv()
-        mine = pl.multiple_of((2 * (1 - y) + c) * cols, cols)
-        pt[d] = (p_ref[zs[d], :, :, pl.ds(mine, cols)].astype(F32) + pc[d, 1 - y].astype(F32)).astype(BF16)
-        pyc[d] = go(pt.at[d], py.at[d], pys.at[d], pyr.at[d], ypeer)
-
-    def g_step(k):
-        gxc[k].wait_recv()
-        g_send(k + 2)
-        i, at = places_of[k]
-        for d in range(depth):
-            own = g_refs[i][zs[d], x, :, at : at + width].astype(F32)
-            gt[k, d] = (own + gx[k, zs[d]].astype(F32)).astype(BF16)
-            if d:
-                gzc[k, d] = go(gt.at[k, d], gz.at[k, d - 1], gzs.at[k, d - 1], gzr.at[k, d - 1], zpeers[d])
-
-    def g_end(k):
-        total = gt[k, 0].astype(F32)
-        for d in range(1, depth):
-            gzc[k, d].wait_recv()
-            total += gz[k, d - 1].astype(F32)
-        i, at = places_of[k]
-        g_outs[i][:, at : at + width] = total
-
-    def p_half(d, side):
-        mine = pl.multiple_of((2 * y + c) * cols, cols)
-        own = p_ref[zs[d], side, :, pl.ds(mine, cols)].astype(F32)
-        return own + pc[d, y, side].astype(F32) + py[d, side].astype(F32)
-
-    def p_x(d):
-        pyc[d].wait_recv()
-        pt[depth + d, 0] = p_half(d, 1 - x).astype(BF16)
-        pxc[d] = go(pt.at[depth + d, 0], px.at[d], pxs.at[d], pxr.at[d], xpeer)
-
-    def p_z(d):
-        pxc[d].wait_recv()
-        pt[depth + d, 1] = (p_half(d, x) + px[d].astype(F32)).astype(BF16)
-        if d:
-            pzc[d] = go(pt.at[depth + d, 1], pz.at[d - 1], pzs.at[d - 1], pzr.at[d - 1], zpeers[d])
-
-    def v_y():
-        vc[0].wait_recv()
-        vb[4] = v_ref[...] + vb[0]
-        vc[1] = go(vb.at[4], vb.at[1], vs.at[1], vr.at[1], ypeer)
-
-    def v_x():
-        vc[1].wait_recv()
-        vb[5] = vb[4] + vb[1]
-        vc[2] = go(vb.at[5], vb.at[2], vs.at[2], vr.at[2], xpeer)
-
-    def v_z():
-        vc[2].wait_recv()
-        vb[6] = vb[5] + vb[2]
-        for d in range(1, depth):
-            vc[2 + d] = go(vb.at[6], vb.at[6 + d], vs.at[2 + d], vr.at[2 + d], zpeers[d])
-
-    def v_end():
-        for d in range(1, depth):
-            vc[2 + d].wait_recv()
-        total = vb[6 + lax.rem(z, depth)]
-        for n in range(1, depth):
-            total += vb[6 + lax.rem(z - n + depth, depth)]
-        v_out[...] = total
-
-    todo = [lambda d=d: p_y(d) for d in order] + [v_y]
-    late = [lambda: p_x(order[0]), v_x, lambda: p_x(order[1]), lambda: p_z(order[0]), v_z]
-    late += [lambda: p_x(order[2]), lambda: p_z(order[1]), lambda: p_x(order[3]), lambda: p_z(order[2]), lambda: p_z(order[3]), v_end]
-    for k in range(chunks):
-        g_step(k)
-        if k >= 2:
-            g_end(k - 2)
-        for _ in range(2):
-            if todo:
-                todo.pop(0)()
-            elif k >= 4 and late:
-                late.pop(0)()
-    for step in todo + late:
-        step()
-    g_end(chunks - 2)
-    g_end(chunks - 1)
-    total = pt[depth, 1].astype(F32)
-    for d in range(1, depth):
-        pzc[d].wait_recv()
-        total += pz[d - 1].astype(F32)
-    p_out[...] = total
-    for copy in started:
-        copy.wait_send()
-
-
-def reduce_all(gd, gi, p, v, width):
-    seq, slot, units = gd.shape
-    depth = seq // 2
-    rows, model_width = p.shape[1:]
-    cols = model_width // 4
-    chunks = 3 * units // width
-    dma = pltpu.SemaphoreType.DMA
-
-    def kernel(gd_ref, gi_ref, p_ref, v_ref, gd_out, gi_out, *refs):
-        g_refs = (gd_ref, gi_ref.at[0], gi_ref.at[1])
-        reduce_kernel(depth, (units,) * 3, g_refs, p_ref, v_ref, (gd_out, gi_out.at[0], gi_out.at[1]), *refs)
-
-    vm = pl.BlockSpec(memory_space=pltpu.VMEM)
-    return pl.pallas_call(
-        kernel,
-        name="reduce_all",
-        out_shape=[
-            jax.ShapeDtypeStruct((slot, units), F32),
-            jax.ShapeDtypeStruct((2, slot, units), F32),
-            jax.ShapeDtypeStruct((rows, cols), F32),
-            jax.ShapeDtypeStruct(v.shape, F32),
-        ],
-        in_specs=[vm] * 4,
-        out_specs=[vm] * 4,
-        scratch_shapes=[
-            pltpu.VMEM((chunks, depth, slot, width), BF16),
-            pltpu.VMEM((chunks, depth, slot, width), BF16),
-            pltpu.VMEM((chunks, depth - 1, slot, width), BF16),
-            pltpu.VMEM((depth, 2, 2, rows, cols), BF16),
-            pltpu.VMEM((depth, 2, rows, cols), BF16),
-            pltpu.VMEM((depth, rows, cols), BF16),
-            pltpu.VMEM((2 * depth, 2, rows, cols), BF16),
-            pltpu.VMEM((depth - 1, rows, cols), BF16),
-            pltpu.VMEM((6 + depth,) + v.shape, F32),
-            dma((chunks,)), dma((chunks,)), dma((chunks, depth - 1)), dma((chunks, depth - 1)),
-            dma((depth, 2)), dma((depth, 2)), dma((depth,)), dma((depth,)), dma((depth,)), dma((depth,)),
-            dma((depth - 1,)), dma((depth - 1,)), dma((2 + depth,)), dma((2 + depth,)),
-        ],
-        compiler_params=pltpu.CompilerParams(collective_id=1, has_side_effects=True, vmem_limit_bytes=60 << 20),
-    )(gd.reshape(depth, 2, slot, units), gi.reshape(2, depth, 2, slot, units), p.reshape(depth, 2, rows, model_width), v)
-
-
-def reduce_plain(gd, gi, p, v, width):
+def reduce_plain(gd, gi, p, v):
     gd = lax.psum_scatter(gd, "seq", scatter_dimension=0, tiled=False).astype(F32)
     gi = lax.psum_scatter(gi, "seq", scatter_dimension=1, tiled=False).astype(F32)
     p = lax.psum_scatter(p, "seq", scatter_dimension=0, tiled=False)
@@ -458,7 +292,7 @@
         ],
         compiler_params=pltpu.CompilerParams(collective_id=2, has_side_effects=True, vmem_limit_bytes=63 << 20),
     )(split(h), wi, wd, split(mid), split(teacher), split(valid), scale)
-    return out.reshape(rows, width), cot.reshape(rows, width), dh.reshape(rows, width), gd, gi, squares[0, 0]
+    return out.reshape(rows, width), cot.reshape(rows, width), dh.reshape(rows, width), gd, gi, squares
 
 def pair_rows(block):
     return jnp.concatenate([block[:, :HD], block[:, HD:]], axis=0)
@@ -549,6 +383,428 @@
         out_specs=[block, whole],
         compiler_params=pltpu.CompilerParams(vmem_limit_bytes=48 << 20),
     )(queries, extended, grad_mixed, mixed, probs)
+
+
+GRAD_COLS = 384
+AHEAD = 3
+
+
+class RowSum:
+    def __init__(self, source, buffers, sems, where, go):
+        self.source, self.go = source, go
+        self.core, self.side, self.cross, self.along = buffers
+        self.cs, self.cr, self.ys, self.yr, self.xs, self.xr, self.zs_, self.zr = sems
+        self.x, self.y, self.c, self.zs, self.sib, self.ypeer, self.xpeer, self.zpeers = where
+        self.depth, self.cols = len(self.zs), self.core.shape[-1]
+        self.order = list(range(1, self.depth)) + [0]
+        self.moved = {}
+
+    def columns(self, y, c):
+        return pl.ds(pl.multiple_of((2 * y + c) * self.cols, self.cols), self.cols)
+
+    def first(self, d):
+        for h in range(2):
+            part = self.source.at[self.zs[d], :, :, self.columns(h, 1 - self.c)]
+            self.moved["c", d, h] = self.go(part, self.core.at[d, h], self.cs.at[d, h], self.cr.at[d, h], self.sib)
+
+    def second(self, d):
+        for h in range(2):
+            self.moved["c", d, h].wait_recv()
+        far = 1 - self.y
+        own = self.source[self.zs[d], :, :, self.columns(far, self.c)].astype(F32)
+        self.core[d, far] = (own + self.core[d, far].astype(F32)).astype(BF16)
+        self.moved["y", d] = self.go(self.core.at[d, far], self.side.at[d], self.ys.at[d], self.yr.at[d], self.ypeer)
+
+    def kept(self, d, x):
+        own = self.source[self.zs[d], x, :, self.columns(self.y, self.c)].astype(F32)
+        return own + self.core[d, self.y, x].astype(F32) + self.side[d, x].astype(F32)
+
+    def third(self, d):
+        self.moved["y", d].wait_recv()
+        self.side[d, 1 - self.x] = self.kept(d, 1 - self.x).astype(BF16)
+        self.moved["x", d] = self.go(self.side.at[d, 1 - self.x], self.cross.at[d], self.xs.at[d], self.xr.at[d], self.xpeer)
+
+    def fourth(self, d):
+        self.moved["x", d].wait_recv()
+        self.cross[d] = (self.kept(d, self.x) + self.cross[d].astype(F32)).astype(BF16)
+        if d:
+            self.moved["z", d] = self.go(
+                self.cross.at[d], self.along.at[d - 1], self.zs_.at[d - 1], self.zr.at[d - 1], self.zpeers[d]
+            )
+
+    def total(self):
+        value = self.cross[0].astype(F32)
+        for d in range(1, self.depth):
+            self.moved["z", d].wait_recv()
+            value += self.along[d - 1].astype(F32)
+        return value
+
+
+def norm_back(values, grad, gain):
+    r = lax.rsqrt(jnp.mean(values * values, axis=-1, keepdims=True) + EPSILON)
+    scaled = grad * gain
+    slope = r * r * r * jnp.mean(values * scaled, axis=-1, keepdims=True)
+    return r * scaled - values * slope, jnp.sum(grad * values * r, axis=0, keepdims=True)
+
+
+def finish_kernel(dh_hbm, cot_hbm, middle_hbm, w_out_hbm, w_attn_hbm, mixed_hbm, probs_hbm, qkv_hbm, ext_hbm, normed_hbm,
+                  tokens_hbm, gd_hbm, gi_hbm, gain_attn, gain_ffn, squares,
+                  grad_x, grad_d, grad_i, grad_qkv_out, grad_o, small_out,
+                  dh, cot, middle, weight, mixed, probs, qkv, ext, normed, low, dmix, dkv, slabs, slabs_in,
+                  gx, gz, own, staged, po, pa, ocore, oside, ocross, oalong, acore, aside, across, aalong, vb,
+                  load, p_load, own_load, out_sem, slab_s, slab_r, gxs, gxr, gzs, gzr, o_sems, a_sems, vs, vr):
+    z, x, y, c = places()
+    depth, width = own.shape[1], own.shape[-1]
+    rows, model_width = dh.shape
+    units = gd_hbm.shape[-1]
+    seq = 2 * depth
+    me = 2 * z + x
+    sib, ypeer, xpeer = device(z, x, y, 1 - c), device(z, x, 1 - y, c), device(z, 1 - x, y, c)
+    zs = [lax.rem(z + d, depth) for d in range(depth)]
+    zpeers = [device(zs[d], x, y, c) for d in range(depth)]
+    wt = 2 * y + c
+    diagonal = (lax.rem(me + seq - 1 + 2 * x, seq), wt)
+    back = [(lax.rem(me + seq - step, seq), wt) for step in (1, 2)]
+
+    def fetch(src, dst, sem):
+        copy = pltpu.make_async_copy(src, dst, sem)
+        copy.start()
+        return copy
+
+    loads = {}
+    for n, (name, src, dst) in enumerate((
+        ("dh", dh_hbm, dh), ("cot", cot_hbm, cot), ("w_out", w_out_hbm, weight.at[:, :model_width]), ("mixed", mixed_hbm, mixed),
+        ("qkv", qkv_hbm, qkv), ("ext", ext_hbm, ext), ("normed", normed_hbm, normed))):
+        loads[name] = fetch(src, dst, load.at[n])
+    greet([sib, ypeer, xpeer, diagonal] + zpeers[1:])
+    started = []
+
+    def go(*args):
+        started.append(remote(*args))
+        return started[-1]
+
+    spots = [(n, at) for n in range(3) for at in range(0, units, width)]
+    chunks = len(spots)
+    gxc, gzc, owned = {}, {}, {}
+
+    def g_ref(k, side):
+        n, at = spots[k]
+        ref = gd_hbm if n == 0 else gi_hbm.at[n - 1]
+        return ref.at[:, side, :, pl.ds(at, width)]
+
+    def g_send(k):
+        if k < chunks:
+            gxc[k] = go(g_ref(k, 1 - x), gx.at[k], gxs.at[k], gxr.at[k], xpeer)
+
+    def g_load(k):
+        if k < chunks:
+            owned[k] = fetch(g_ref(k, x), own.at[k % 2], own_load.at[k % 2])
+
+    def g_step(k):
+        gxc[k].wait_recv()
+        g_send(k + AHEAD)
+        owned[k].wait()
+        for d in range(depth):
+            gx[k, zs[d]] = (own[k % 2, zs[d]].astype(F32) + gx[k, zs[d]].astype(F32)).astype(BF16)
+            if d:
+                gzc[k, d] = go(gx.at[k, zs[d]], gz.at[k, d - 1], gzs.at[k, d - 1], gzr.at[k, d - 1], zpeers[d])
+        g_load(k + 2)
+
+    stores = {}
+
+    def g_end(k):
+        total = gx[k, z].astype(F32)
+        for d in range(1, depth):
+            gzc[k, d].wait_recv()
+            total += gz[k, d - 1].astype(F32)
+        if k >= 2:
+            stores[k - 2].wait()
+        staged[k % 2] = total
+        n, at = spots[k]
+        target = grad_d if n == 0 else grad_i.at[n - 1]
+        stores[k] = fetch(staged.at[k % 2], target.at[:, pl.ds(at, width)], out_sem.at[k % 2])
+
+    for k in range(AHEAD):
+        g_send(k)
+    g_load(0)
+    g_load(1)
+    where = (x, y, c, zs, sib, ypeer, xpeer, zpeers)
+    sum_o = RowSum(po, (ocore, oside, ocross, oalong), o_sems, where, go)
+    sum_a = RowSum(pa, (acore, aside, across, aalong), a_sems, where, go)
+
+    step = middle.shape[1]
+    steps = rows // step
+    mids = [None] * steps
+
+    def mid_load(n):
+        if n < steps:
+            mids[n] = fetch(middle_hbm.at[pl.ds(n * step, step)], middle.at[n % 2], load.at[8 + n % 2])
+
+    mid_load(0)
+    mid_load(1)
+    loads["dh"].wait()
+    loads["cot"].wait()
+    gain_grad = jnp.zeros((1, model_width), F32)
+    for n in range(steps):
+        mids[n].wait()
+        r = pl.ds(n * step, step)
+        grad, part = norm_back(middle[n % 2], dh[r, :], gain_ffn[...])
+        grad = cot[r, :] + grad
+        cot[r, :] = grad
+        low[r, :model_width] = grad.astype(BF16)
+        gain_grad += part
+        mid_load(n + 2)
+    vb[0] = jnp.zeros(vb.shape[1:], F32)
+    vb[0, 1:2] = gain_grad
+    vb[0, 2:3] = jnp.broadcast_to(squares[0:1, 0:1], (1, model_width))
+    loads["w_out"].wait()
+    loads["mixed"].wait()
+    rows_low = lambda: low[:, :model_width]
+
+    def out_back(cols):
+        dmix[:, cols] = contract(rows_low(), weight[cols, :model_width], 1, 1).astype(BF16)
+
+    tiles(model_width, 512, out_back)
+    loads["w_attn"] = fetch(w_attn_hbm, weight, load.at[7])
+
+    def out_grad(d, _):
+        cols = pl.ds(pl.multiple_of(d * 2 * po.shape[2], 128), 2 * po.shape[2])
+        po[d] = contract(low[:, cols], mixed[...], 0, 0).astype(BF16).reshape(po.shape[1:])
+        return 0
+
+    lax.fori_loop(0, depth, out_grad, 0)
+    for d in sum_o.order:
+        sum_o.first(d)
+    g_step(0)
+    blocks, pairs, reach = probs_hbm.shape[0], probs_hbm.shape[1], probs.shape[-1]
+    count = blocks * pairs
+
+    def p_fetch(t):
+        return pltpu.make_async_copy(probs_hbm.at[t // pairs, t % pairs], probs.at[t % 2], p_load.at[t % 2])
+
+    p_fetch(0).start()
+    p_fetch(1).start()
+    dkv[...] = jnp.zeros_like(dkv)
+    loads["qkv"].wait()
+    loads["ext"].wait()
+    for i in range(blocks):
+        q_rows, keys = pl.ds(i * QROWS, QROWS), pl.ds(i * QROWS, reach)
+
+        def one(pair, _):
+            t = i * pairs + pair
+            cols = pl.ds(pl.multiple_of(pair * 2 * HD, 2 * HD), 2 * HD)
+            queries, grads = pair_rows(qkv[q_rows, cols]), pair_rows(dmix[q_rows, cols])
+            outs = pair_rows(mixed[q_rows, cols])
+            dots = jnp.sum(grads.astype(F32) * outs.astype(F32), axis=-1, keepdims=True)
+            slot = lax.rem(t, 2)
+            p_fetch(t).wait()
+            weights = flat(probs[slot])
+            steep = contract(grads, ext[keys, HD:], 1, 1) - dots
+            steep = (weights.astype(F32) * steep).astype(BF16)
+            low[q_rows, cols] = (pair_columns(contract(steep, ext[keys, :HD], 1, 0)) * (1.0 / math.sqrt(HD))).astype(BF16)
+            dkv[keys, :HD] += contract(steep, queries, 0, 0)
+            dkv[keys, HD:] += contract(weights, grads, 0, 0)
+
+            @pl.when(t + 2 < count)
+            def _():
+                p_fetch(t + 2).start()
+
+            return 0
+
+        lax.fori_loop(0, pairs, one, 0)
+        if i == 0:
+            for d in sum_o.order:
+                sum_o.second(d)
+            g_step(1)
+    for n in range(2):
+        slabs[n] = dkv[(1 - n) * rows : (2 - n) * rows, :].astype(BF16)
+    returned = [go(slabs.at[n], slabs_in.at[n], slab_s.at[n], slab_r.at[n], back[n]) for n in range(2)]
+    loads["normed"].wait()
+    slot_rows = model_width // seq
+
+    def query_grad(d, _):
+        cols = pl.ds(pl.multiple_of(d * 2 * slot_rows, 128), 2 * slot_rows)
+        pa[d, :, :slot_rows] = contract(low[:, cols], normed[...], 0, 0).astype(BF16).reshape(2, slot_rows, model_width)
+        return 0
+
+    lax.fori_loop(0, depth, query_grad, 0)
+    g_step(2)
+    for one in returned:
+        one.wait_recv()
+    summed = dkv[2 * rows :, :] + slabs_in[0].astype(F32) + slabs_in[1].astype(F32)
+    low[:, model_width : model_width + HD] = (summed[:, :HD] * (1.0 / math.sqrt(HD))).astype(BF16)
+    low[:, model_width + HD :] = summed[:, HD:].astype(BF16)
+    kv_grad = contract(low[:, model_width:], normed[...], 0, 0).astype(BF16)
+    kv_rows = HD // seq
+    for n in range(2):
+        part = kv_grad[n * HD : (n + 1) * HD].reshape(depth, 2, kv_rows, model_width)
+        pa[:, :, slot_rows + n * kv_rows : slot_rows + (n + 1) * kv_rows] = part
+    for d in sum_a.order:
+        sum_a.first(d)
+    loads["tokens"] = fetch(tokens_hbm, mixed, load.at[3])
+    loads["w_attn"].wait()
+
+    def attn_back(cols):
+        dh[:, cols] = contract(low[...], weight[cols, :], 1, 1)
+
+    tiles(model_width, 512, attn_back)
+    for d in sum_a.order:
+        sum_a.second(d)
+    g_step(3)
+    loads["tokens"].wait()
+
+    def last_norm(n, so_far):
+        r = pl.ds(pl.multiple_of(n * step, step), step)
+        grad, part = norm_back(mixed[r, :].astype(F32), dh[r, :], gain_attn[...])
+        cot[r, :] += grad
+        return so_far + part
+
+    vb[0, 0:1] = lax.fori_loop(0, steps, last_norm, jnp.zeros((1, model_width), F32))
+    saved = fetch(cot, grad_x, load.at[0])
+
+    vc = {}
+
+    def v_first():
+        vc[0] = go(vb.at[0], vb.at[1], vs.at[0], vr.at[0], sib)
+
+    def v_swap(n, to):
+        vc[n - 1].wait_recv()
+        vb[2 * n] = vb[2 * n - 2] + vb[2 * n - 1]
+        vc[n] = go(vb.at[2 * n], vb.at[2 * n + 1], vs.at[n], vr.at[n], to)
+
+    def v_along():
+        vc[2].wait_recv()
+        vb[6] = vb[4] + vb[5]
+        for d in range(1, depth):
+            vc[2 + d] = go(vb.at[6], vb.at[6 + d], vs.at[2 + d], vr.at[2 + d], zpeers[d])
+
+    def v_end():
+        for d in range(1, depth):
+            vc[2 + d].wait_recv()
+        total = vb[6 + z]
+        for n in range(1, depth):
+            total += vb[6 + lax.rem(z - n + depth, depth)]
+        small_out[...] = total
+
+    v_first()
+    o, a = sum_o.order, sum_a.order
+    g_end(0)
+    for d in o:
+        sum_o.third(d)
+    v_swap(1, ypeer)
+    g_step(4)
+    g_end(1)
+    for d in o:
+        sum_o.fourth(d)
+    v_swap(2, xpeer)
+    g_step(5)
+    g_end(2)
+    sum_a.third(a[0])
+    sum_a.third(a[1])
+    v_along()
+    g_step(6)
+    g_end(3)
+    sum_a.third(a[2])
+    sum_a.third(a[3])
+    sum_a.fourth(a[0])
+    grad_o[...] = sum_o.total()
+    g_step(7)
+    g_end(4)
+    for d in a[1:]:
+        sum_a.fourth(d)
+    v_end()
+    for k in range(8, chunks):
+        g_step(k)
+        g_end(k - 3)
+    g_end(chunks - 3)
+    grad_qkv_out[...] = sum_a.total()
+    g_end(chunks - 2)
+    g_end(chunks - 1)
+    for copy in started:
+        copy.wait_send()
+    saved.wait()
+    stores[chunks - 2].wait()
+    stores[chunks - 1].wait()
+
+
+def finish(dh, cot, middle, w_out, w_attn, mixed, probs, qkv, ext, normed, tokens, gd, gi, gain_attn, gain_ffn, squares, seq):
+    rows, model_width = dh.shape
+    depth, slot, units = seq // 2, model_width // seq, gd.shape[-1]
+    kv_rows, cols = 2 * HD // seq, model_width // 4
+    blocks, heads, _, reach = probs.shape
+    chunks = 3 * units // GRAD_COLS
+    qkv_slot = slot + kv_rows
+    step = 128
+    dma = pltpu.SemaphoreType.DMA
+    hbm, vm = pl.BlockSpec(memory_space=pl.ANY), pl.BlockSpec(memory_space=pltpu.VMEM)
+
+    def sum_buffers(n):
+        return [
+            pltpu.VMEM((depth, 2, 2, n, cols), BF16),
+            pltpu.VMEM((depth, 2, n, cols), BF16),
+            pltpu.VMEM((depth, n, cols), BF16),
+            pltpu.VMEM((depth - 1, n, cols), BF16),
+        ]
+
+    sum_sems = [dma((depth, 2)), dma((depth, 2)), dma((depth,)), dma((depth,)), dma((depth,)), dma((depth,)), dma((depth - 1,)), dma((depth - 1,))]
+
+    def kernel(*refs):
+        refs = list(refs)
+        at = len(refs) - 18
+        o_sems, a_sems = refs[at : at + 8], refs[at + 8 : at + 16]
+        finish_kernel(*refs[:at], o_sems, a_sems, *refs[at + 16 :])
+
+    return pl.pallas_call(
+        kernel,
+        name="finish",
+        out_shape=[
+            jax.ShapeDtypeStruct((rows, model_width), F32),
+            jax.ShapeDtypeStruct((slot, units), F32),
+            jax.ShapeDtypeStruct((2, slot, units), F32),
+            jax.ShapeDtypeStruct((qkv_slot, cols), F32),
+            jax.ShapeDtypeStruct((slot, cols), F32),
+            jax.ShapeDtypeStruct((8, model_width), F32),
+        ],
+        in_specs=[hbm] * 13 + [vm] * 3,
+        out_specs=[hbm] * 3 + [vm] * 3,
+        scratch_shapes=[
+            pltpu.VMEM((rows, model_width), F32),
+            pltpu.VMEM((rows, model_width), F32),
+            pltpu.VMEM((2, step, model_width), F32),
+            pltpu.VMEM(w_attn.shape, BF16),
+            pltpu.VMEM((rows, model_width), BF16),
+            pltpu.VMEM((2, 2, QROWS, reach), BF16),
+            pltpu.VMEM(qkv.shape, BF16),
+            pltpu.VMEM(ext.shape, BF16),
+            pltpu.VMEM((rows, model_width), BF16),
+            pltpu.VMEM(qkv.shape, BF16),
+            pltpu.VMEM((rows, model_width), BF16),
+            pltpu.VMEM(ext.shape, F32),
+            pltpu.VMEM((2, rows, 2 * HD), BF16),
+            pltpu.VMEM((2, rows, 2 * HD), BF16),
+            pltpu.VMEM((chunks, depth, slot, GRAD_COLS), BF16),
+            pltpu.VMEM((chunks, depth - 1, slot, GRAD_COLS), BF16),
+            pltpu.VMEM((2, depth, slot, GRAD_COLS), BF16),
+            pltpu.VMEM((2, slot, GRAD_COLS), F32),
+            pltpu.VMEM((depth, 2, slot, model_width), BF16),
+            pltpu.VMEM((depth, 2, qkv_slot, model_width), BF16),
+        ]
+        + sum_buffers(slot)
+        + sum_buffers(qkv_slot)
+        + [pltpu.VMEM((6 + depth, 8, model_width), F32)]
+        + [
+            dma((10,)), dma((2,)), dma((2,)), dma((2,)), dma((2,)), dma((2,)),
+            dma((chunks,)), dma((chunks,)), dma((chunks, depth - 1)), dma((chunks, depth - 1)),
+        ]
+        + sum_sems
+        + sum_sems
+        + [dma((2 + depth,)), dma((2 + depth,))],
+        compiler_params=pltpu.CompilerParams(collective_id=1, has_side_effects=True, vmem_limit_bytes=63 << 20),
+    )(
+        dh, cot, middle, w_out, w_attn, mixed, probs.reshape(blocks, heads // 2, 2, QROWS, reach), qkv, ext, normed, tokens,
+        gd.reshape(depth, 2, slot, units), gi.reshape(2, depth, 2, slot, units),
+        gain_attn.reshape(1, -1), gain_ffn.reshape(1, -1), squares,
+    )
 
 
 def passed_along(block, axis, distance):
@@ -602,45 +858,51 @@
     output, cotangent, grad_norm_two, grad_down, grad_in, squares = ffn(
         normed_two, w_pair, w_down, middle, teacher[0], valid[:, None], scale_up
     )
-    grad_middle_norm, grad_gain_ffn = norm_two_pull(grad_norm_two)
-    grad_middle = cotangent + grad_middle_norm
-    grad_mid_low = grad_middle.astype(jnp.bfloat16)
-    grad_out = jnp.einsum("te,td->ed", grad_mid_low, mixed_b, preferred_element_type=jnp.float32)
-    grad_mixed = jnp.einsum("te,de->td", grad_mid_low, out_full, preferred_element_type=jnp.float32)
-    grad_query, grad_ext = attend_back(qkv, extended, grad_mixed.astype(jnp.bfloat16), mixed_b, probs)
-    grad_kv = grad_ext[edge_rows:]
-    for back_step in range(1, reach_count + 1):
-        slab_rows = grad_ext[
-            edge_rows - back_step * tok_rows : edge_rows - (back_step - 1) * tok_rows
-        ]
-        grad_kv = grad_kv + passed_along(slab_rows, "seq", -back_step)
-    grad_key = (grad_kv[:, :HD] * (1.0 / math.sqrt(HD))).astype(jnp.bfloat16)
-    grad_qkv = jnp.concatenate([grad_query, grad_key, grad_kv[:, HD:].astype(jnp.bfloat16)], axis=1)
-    grad_attn = jnp.einsum("te,td->ed", grad_qkv, normed, preferred_element_type=jnp.float32)
-    grad_normed = jnp.einsum("te,de->td", grad_qkv, attn_full, preferred_element_type=jnp.float32)
-    grad_input_norm, grad_gain_attn = norm_one_pull(grad_normed)
-    grad_inputs = grad_middle + grad_input_norm
     slot, kv_slot = model_width // seq_devices, HD // seq_devices
-    grad_attn = grad_attn.astype(jnp.bfloat16)
-    grad_key, grad_value = (
-        grad_attn[model_width + at : model_width + at + HD].reshape(seq_devices, kv_slot, model_width) for at in (0, HD)
-    )
-    packed = jnp.concatenate(
-        [
-            grad_attn[:model_width].reshape(seq_devices, slot, model_width),
-            grad_key,
-            grad_value,
-            grad_out.astype(jnp.bfloat16).reshape(seq_devices, slot, model_width),
-        ],
-        axis=1,
-    )
-    small = jnp.stack([grad_gain_attn, grad_gain_ffn, jnp.full((model_width,), squares)] + [jnp.zeros_like(grad_gain_attn)] * 5)
-    grad_down, grad_in = grad_down.reshape(seq_devices, slot, -1), grad_in.reshape(2, seq_devices, slot, -1)
-    reduce = reduce_all if slot % 16 == 0 and kv_slot % 16 == 0 else reduce_plain
-    grad_down, grad_in, packed, small = reduce(grad_down, grad_in, packed, small, 384)
-    grad_queries = packed[:slot].T
-    grad_keyvals = packed[slot:-slot].T.reshape(-1, 2, kv_slot)
-    grad_out = packed[-slot:].T
+    if slot % 16 == 0 and kv_slot % 16 == 0:
+        grad_inputs, grad_down, grad_in, grad_attn, grad_out, small = finish(
+            grad_norm_two, cotangent, middle, out_full, attn_full, mixed_b, probs, qkv, extended, normed, tokens[0],
+            grad_down, grad_in, gain_attn, gain_ffn, squares, seq_devices,
+        )
+    else:
+        grad_middle_norm, grad_gain_ffn = norm_two_pull(grad_norm_two)
+        grad_middle = cotangent + grad_middle_norm
+        grad_mid_low = grad_middle.astype(jnp.bfloat16)
+        grad_out = jnp.einsum("te,td->ed", grad_mid_low, mixed_b, preferred_element_type=jnp.float32)
+        grad_mixed = jnp.einsum("te,de->td", grad_mid_low, out_full, preferred_element_type=jnp.float32)
+        grad_query, grad_ext = attend_back(qkv, extended, grad_mixed.astype(jnp.bfloat16), mixed_b, probs)
+        grad_kv = grad_ext[edge_rows:]
+        for back_step in range(1, reach_count + 1):
+            slab_rows = grad_ext[
+                edge_rows - back_step * tok_rows : edge_rows - (back_step - 1) * tok_rows
+            ]
+            grad_kv = grad_kv + passed_along(slab_rows, "seq", -back_step)
+        grad_key = (grad_kv[:, :HD] * (1.0 / math.sqrt(HD))).astype(jnp.bfloat16)
+        grad_qkv = jnp.concatenate([grad_query, grad_key, grad_kv[:, HD:].astype(jnp.bfloat16)], axis=1)
+        grad_attn = jnp.einsum("te,td->ed", grad_qkv, normed, preferred_element_type=jnp.float32)
+        grad_normed = jnp.einsum("te,de->td", grad_qkv, attn_full, preferred_element_type=jnp.float32)
+        grad_input_norm, grad_gain_attn = norm_one_pull(grad_normed)
+        grad_inputs = grad_middle + grad_input_norm
+        grad_attn = grad_attn.astype(jnp.bfloat16)
+        grad_key, grad_value = (
+            grad_attn[model_width + at : model_width + at + HD].reshape(seq_devices, kv_slot, model_width) for at in (0, HD)
+        )
+        packed = jnp.concatenate(
+            [
+                grad_attn[:model_width].reshape(seq_devices, slot, model_width),
+                grad_key,
+                grad_value,
+                grad_out.astype(jnp.bfloat16).reshape(seq_devices, slot, model_width),
+            ],
+            axis=1,
+        )
+        small = jnp.stack([grad_gain_attn, grad_gain_ffn, jnp.full((model_width,), squares[0, 0])] + [jnp.zeros_like(grad_gain_attn)] * 5)
+        grad_down, grad_in = grad_down.reshape(seq_devices, slot, -1), grad_in.reshape(2, seq_devices, slot, -1)
+        grad_down, grad_in, packed, small = reduce_plain(grad_down, grad_in, packed, small)
+        grad_attn, grad_out = packed[:-slot], packed[-slot:]
+    grad_queries = grad_attn[:slot].T
+    grad_keyvals = grad_attn[slot:].T.reshape(-1, 2, kv_slot)
+    grad_out = grad_out.T
     grad_down = grad_down.T
     grad_in = jnp.swapaxes(grad_in, 0, 1)
     gain_attn_all, gain_ffn_all, squares_all = small[0], small[1], small[2, 0]

time: 553 us -> 493 us (0.89)
  Pallas kernels: 385 us -> 365 us
  other arithmetic: 19.2 us -> 3.35 us
  matrix products: 25.9 us -> 11.5 us
  waiting for transfers between devices: 50.5 us -> 44.3 us
    pallas_call x2 -> x1, Pallas kernels: 207 us -> 187 us  [finish(): pl.pallas_call(kernel, name='finish', out_shape=[jax.ShapeDtypeStruct((ro...]
    dot_general x4 -> x0, matrix products: 14.3 us -> none  [the longest x1 4.91 us: per_device(): jnp.einsum('te,de->td', grad_qkv, attn_full, preferred_element_type=jnp.f...]
    ppermute x4 -> x2, waiting for transfers between devices: 5.81 us -> 0.01 us  [passed_along(): return lax.ppermute(block, axis, route)]
    ppermute x4 -> x2, starting transfers between devices: 11.2 us -> 6.21 us  [passed_along(): return lax.ppermute(block, axis, route)]
    unnamed x44 -> x28, local copies, waits for them, and re-layouts: 19.8 us -> 19.8 us
  transfers between devices with their start and end apart: 6 -> 4, of which waited for: 3 -> 1; matrix products, arithmetic and copies ran while one was open for 4% -> 4% of each run, Pallas kernels for 5% -> 6%
where the time goes in v5:
time: 493 us; the launch traced here: 484 us
  Pallas kernels  365 us (74%)
  waiting for transfers between devices  44.3 us (9%)
  local copies, waits for them, and re-layouts  28.6 us (6%)
  between operations  18.3 us (4%)
  matrix products  11.5 us (2%)
  blocking collectives  6.61 us (1%)
  starting transfers between devices  6.28 us (1%)
    pallas_call x1, Pallas kernels, finish(): pl.pallas_call(kernel, name='finish', out_shape=[jax.ShapeDtypeStruct((ro...  187 us
    pallas_call x1, Pallas kernels, ffn(): pl.pallas_call(ffn_kernel, name='ffn', out_shape=[jax.ShapeDtypeStruct((2...  150 us
    all_gather x1, waiting for transfers between devices, per_device(): lax.all_gather(w_attn, 'wt', axis=0, tiled=True)  42.9 us
    pallas_call x1, Pallas kernels, attend(): pl.pallas_call(attend_kernel, name='attend', grid=(blocks, pairs), out_sh...  27.1 us
    unnamed x28, local copies, waits for them, and re-layouts  19.8 us
  transfers between devices with their start and end apart: 4, of which 1 were waited for; matrix products, arithmetic and copies ran while one was open for 4% of the time, Pallas kernels for 6%

profile of v5, /device:TPU:11, one launch (start us, length us, event | category | flops | bytes accessed | tf_op | source)
XLA Modules:
  0.0 483.5 jit_solution(12114449363255578305)
XLA Ops:
  10.2 42.9 %all-gather.3.cloned.1.call-done.refs_4_ = bf16[1536,1792]{1,0:T(8,128)(2,1)} async-done(((bf16[384,1792]{1,0:T(8,128)(2,1)}), bf16[1536,1792]{1,0:T(8,128)(2,1)}) %all-gather.3.cloned.1.call-update) | async-done | bytes 5505040 | tf_op jit(solution)/shard_map/all_gather | solution.py:843
  53.1 5.6 %convolution_convert_fusion.q.refs_7_ = bf16[512,1792]{1,0:T(8,128)(2,1)S(1)} fusion(bf16[512,1536]{1,0:T(8,128)(2,1)S(1)} %fusion.2.refs_9_, bf16[1536,1792]{1,0:T(8,128)(2,1)} %all-gather.3.cloned.1.call-done.refs_4_), kind=kOutput, calls=%fused_computation.9 | convolution fusion | flops 2819489792 | bytes 8912896 | tf_op jit(solution)/shard_map/dot_general | solution.py:848
  58.7 0.8 slice.35
  59.5 3.1 collective-permute-start
  62.6 3.1 collective-permute-start.1
  65.7 6.6 %psum.7 = f32[]{:T(128)} all-reduce(f32[]{:T(128)S(6)} %convert_element_type.49), channel_id=1, replica_groups=mesh['seq'=8,'wt'=4] {'wt'}, use_global_device_ids=true, to_apply=%region_2.3 | all-reduce | flops 1 | bytes 8 | tf_op jit(solution)/shard_map/psum | solution.py:841
  73.1 0.9 copy.23.valid
  73.9 6.8 %copy.26 = bf16[1536,2,1152]{2,0,1:T(8,128)(2,1)} copy(bf16[1536,2,1152]{2,1,0:T(2,128)(2,1)} %param.14) | data formatting | bytes 14155776 | tf_op args[5]
  82.8 1.0 pad_maximum_fusion.kv.refs_8_
  83.8 27.1 %attend.1 = (bf16[512,1536]{1,0:T(8,128)(2,1)S(1)}, bf16[2,12,256,1280]{3,2,1,0:T(8,128)(2,1)}) custom-call(bf16[512,1792]{1,0:T(8,128)(2,1)S(1)} %convolution_convert_fusion.q.refs_7_, bf16[1536,256]{1,0:T(8,128)(2,1)S(1)} %pad_maximum_fusion.kv.refs_8_, s32[512,1]{1,0:T(8,128)S(1)} %copy.21.q_ids, s32[1,1536]{1,0:T(1,128)S(1)} %and_select_fusion.k_ids), custom_call_target="tpu_custom_call" | custom-call | tf_op jit(solution)/shard_map/attend/pallas_call | solution.py:330
  110.9 1.1 copy-done.2
  112.0 6.0 %multiply_reduce_fusion = (f32[512]{0:T(512)S(1)}, f32[512,1536]{1,0:T(8,128)S(1)}) fusion(bf16[512,1536]{1,0:T(8,128)(2,1)} %copy-done.2, bf16[1536,1536]{1,0:T(8,128)(2,1)} %all-gather.5.cloned.1.call-done.refs_3_, bf16[1,512,1536]{2,1,0:T(8,128)(2,1)} %param.9), kind=kOutput, calls=%fused_computation.8 | convolution fusion | flops 2419064320 | bytes 11012096 | tf_op jit(solution)/shard_map/dot_general | solution.py:853
  118.0 1.6 copy-done.3
  119.7 1.5 multiply_convert_fusion
  121.1 150.0 %ffn.1 = (bf16[2,256,1536]{2,1,0:T(8,128)(2,1)}, f32[2,256,1536]{2,1,0:T(8,128)}, f32[2,256,1536]{2,1,0:T(8,128)}, bf16[1536,1152]{1,0:T(8,128)(2,1)}, bf16[2,1536,1152]{2,1,0:T(8,128)(2,1)}, /*index=5*/f32[8,128]{1,0:T(8,128)}) custom-call(bf16[2,256,1536]{2,1,0:T(8,128)(2,1)} %bitcast.44, bf16[2,1536,1152]{2,1,0:T(8,128)(2,1)} %bitcast.39, ...), custom_call_target="tpu_custom_call" | custom-call | tf_op jit(solution)/shard_map/ffn/pallas_call | solution.py:262
  271.2 187.5 %finish.1 = (f32[512,1536]{1,0:T(8,128)}, f32[192,1152]{1,0:T(8,128)}, f32[2,192,1152]{2,1,0:T(8,128)}, f32[224,384]{1,0:T(8,128)}, f32[192,384]{1,0:T(8,128)}, /*index=5*/f32[8,1536]{1,0:T(8,128)}) custom-call(f32[512,1536]{1,0:T(8,128)} %bitcast.47, f32[512,1536]{1,0:T(8,128)} %bitcast.46, f32[512,1536]{1,0:T(8,128)} %copy-done.3, ...), custom_call_target="tpu_custom_call" | custom-call | tf_op jit(solution)/shard_map/finish/pallas_call | solution.py:757
  458.7 1.7 slice_bitcast_fusion
  460.4 1.4 slice.32
  461.8 1.5 slice_reduce_fusion
  463.3 1.2 slice.30
  464.5 4.2 copy.24
  469.4 2.7 copy.32
  472.0 1.7 copy.33
  474.4 0.9 copy.35
  (39 shorter events, 4.4 us)
Async XLA Ops:
  7.2 2.2 copy-start.4
  7.2 2.6 copy-start.9
  7.2 45.9 %all-gather.3.cloned.1.call-start = ((), (), s32[]{:S(2)}) async-start(), calls=%async_computation | async-start | bytes 6881280 | tf_op jit(solution)/shard_map/all_gather | solution.py:843
  7.9 104.1 %all-gather.5.cloned.1.call-start = ((), (), s32[]{:S(2)}) async-start(), calls=%async_computation.1 | async-start | bytes 5898240 | tf_op jit(solution)/shard_map/all_gather | solution.py:844
  10.2 48.5 %copy-start.5 = (bf16[512,1536]{1,0:T(8,128)(2,1)}, bf16[512,1536]{1,0:T(8,128)(2,1)S(1)}, u32[]{:S(2)}) copy-start(bf16[512,1536]{1,0:T(8,128)(2,1)S(1)} %fusion.2.refs_9_) | copy-start | bytes 4718596
  58.7 25.1 %copy-start = (bf16[512,1792]{1,0:T(8,128)(2,1)}, bf16[512,1792]{1,0:T(8,128)(2,1)S(1)}, u32[]{:S(2)}) copy-start(bf16[512,1792]{1,0:T(8,128)(2,1)S(1)} %convolution_convert_fusion.q.refs_7_) | copy-start | bytes 5505028
  59.5 23.3 %collective-permute-start = (bf16[512,256]{1,0:T(8,128)(2,1)}, bf16[512,256]{1,0:T(8,128)(2,1)S(1)}, u32[]{:S(2)}, u32[]{:S(2)}) collective-permute-start(bf16[512,256]{1,0:T(8,128)(2,1)} %slice.35), channel_id=1, source_target_pairs={{0,8},{4,12},{8,16},{12,20},{16,24},{20,28},{1,9},{5,13},{9,17},{1... | collective-permute-start | bytes 786440 | tf_op jit(solution)/shard_map/ppermute | solution.py:813
  62.6 20.2 %collective-permute-start.1 = (bf16[512,256]{1,0:T(8,128)(2,1)}, bf16[512,256]{1,0:T(8,128)(2,1)S(1)}, u32[]{:S(2)}, u32[]{:S(2)}) collective-permute-start(bf16[512,256]{1,0:T(8,128)(2,1)} %slice.35), channel_id=1, source_target_pairs={{0,4},{4,8},{8,12},{12,16},{16,20},{20,24},{24,28},{1,5},{5,9},{9,... | collective-permute-start | bytes 786440 | tf_op jit(solution)/shard_map/ppermute | solution.py:813
  73.9 6.8 %copy-start.10 = (f32[1536]{0:T(1024)S(1)}, f32[1536]{0:T(1024)}, u32[]{:S(2)}) copy-start(f32[1536]{0:T(1024)} %param.17) | copy-start | bytes 18436
  83.8 34.2 %copy-start.1 = (bf16[1536,256]{1,0:T(8,128)(2,1)}, bf16[1536,256]{1,0:T(8,128)(2,1)S(1)}, u32[]{:S(2)}) copy-start(bf16[1536,256]{1,0:T(8,128)(2,1)S(1)} %pad_maximum_fusion.kv.refs_8_) | copy-start | bytes 2359300
  110.9 1.1 copy-start.2
  118.0 1.7 copy-start.3
  464.5 7.5 %copy-start.6 = (f32[512,1536]{1,0:T(8,128)S(1)}, f32[512,1536]{1,0:T(8,128)}, u32[]{:S(2)}) copy-start(f32[512,1536]{1,0:T(8,128)} %get-tuple-element.33) | copy-start | bytes 9437188
  472.0 1.7 copy-start.8
  472.0 2.4 copy-start.7
Sparse Core Ops, SparseCore 0:
  9.6 43.4 all-gather.2
  54.7 37.5 all-gather.4
